TPU v7x, 128 devices: a whole 4x4x4 slice. The times are simulated.
128 devices in a mesh: cache: 8 (over x, core), space: 8 (over z, y_hi), head: 2 (over y_lo).
Axes of the slice: x: 4, y: 4 (y_hi: 2, y_lo: 2; y = y_hi * 2 + y_lo), z: 4, core: 2. Of those that a mesh axis runs over, the one named last changes fastest.
Arguments:
- queries: bfloat16 [32, 640, 2560], P('cache', 'space', 'head'), may hold values from -8 to 8, as said below
- keys: bfloat16 [32, 640, 2560], P('cache', 'space', 'head'), may hold values from -8 to 8, as said below
- values: bfloat16 [32, 640, 2560], P('cache', 'space', 'head'), may hold values from -6 to 6
- cache_keys: bfloat16 [16, 640, 2560], P('cache', 'space', 'head'), may hold values from -8 to 8
- cache_values: bfloat16 [16, 640, 2560], P('cache', 'space', 'head'), may hold values from -6 to 6
- window: int32 [32, 2], replicated, may hold values from 0 to 15, as said below
- span_slot: int32 [16], replicated, may hold values from 0 to 15, as said below
- counts: int32 [16], replicated, may hold values from 320 to 640
- out_weight: bfloat16 [2560, 5120], P('head'), may hold values from -0.125 to 0.125
Outputs:
- mixed: bfloat16 [32, 640, 5120], P('cache', 'space', 'head')
Inputs may be any that keep to these rules, and one draw needn't show every extreme that they name: `queries`: values of order one. `keys`: values of order one. `window`: for every block of 4 current spans (rows b * 4 .. (b + 1) * 4 - 1) and every cache group g, the block's entries name exactly one cached span id whose slot lies in g * 2 .. (g + 1) * 2 - 1; entries may repeat. `span_slot`: each slot once.
All inputs are finite; a program needn't handle non-finite values.
Results may differ from a plain program's by a relative error of at most 0.0052.
Values may be sent and summed in bfloat16 or wider, within the bound.
No kernel may reach another device: no remote copies, remote signals or barrier semaphores. Data moves between devices by JAX's collectives and lax.ppermute only.
A program may use at most 192 MiB of HBM per device.

v0:
```python
import math

import jax
import jax.numpy as jnp
from jax import lax
from jax.sharding import PartitionSpec as P

HD = 128
WIN = 2


def on_device(
    queries, keys, values, cache_keys, cache_values, window, span_slot, counts, out_weight
):
    groups = queries.shape[0]
    tok_rows = queries.shape[1]
    feat_width = queries.shape[2]
    heads_here = feat_width // HD
    group_index = lax.axis_index("cache")
    space_count = lax.axis_size("space")
    cache_count = lax.axis_size("cache")
    held_count = cache_keys.shape[0]
    span_len = tok_rows * space_count
    scale = 1.0 / math.sqrt(HD)
    all_slots = span_slot[window]
    mine_slots = lax.dynamic_slice_in_dim(all_slots, group_index * groups, groups, 0)
    mine_ids = lax.dynamic_slice_in_dim(window, group_index * groups, groups, 0)
    lengths = counts[mine_ids]
    per_group = all_slots.reshape(cache_count, groups * WIN)
    owned_here = per_group // held_count == group_index
    picked = jnp.max(jnp.where(owned_here, per_group % held_count, 0), axis=1)
    send_keys = cache_keys[picked]
    send_values = cache_values[picked]
    got_keys, got_values = (
        lax.all_to_all(send_keys, "cache", split_axis=0, concat_axis=0, tiled=True),
        lax.all_to_all(send_values, "cache", split_axis=0, concat_axis=0, tiled=True),
    )
    owners = mine_slots // held_count
    near_keys = got_keys[owners]
    near_values = got_values[owners]
    local_keys = jnp.concatenate([keys[:, None], near_keys], 1)
    local_values = jnp.concatenate([values[:, None], near_values], 1)
    whole_keys, whole_values = (
        lax.all_gather(local_keys, "space", axis=2, tiled=True),
        lax.all_gather(local_values, "space", axis=2, tiled=True),
    )
    spots = jnp.arange(span_len)
    cached_valid = spots[None, None, :] < lengths[:, :, None]
    valid = jnp.concatenate([jnp.ones((groups, 1, span_len), dtype=bool), cached_valid], 1).reshape(
        groups, -1
    )
    key_set = whole_keys.reshape(groups, -1, heads_here, HD)
    value_set = whole_values.reshape(groups, -1, heads_here, HD)
    query_set = queries.reshape(groups, tok_rows, heads_here, HD)
    scores = (
        jnp.einsum("cqhd,ckhd->chqk", query_set, key_set, preferred_element_type=jnp.float32)
        * scale
    )
    scores = jnp.where(valid[:, None, None, :], scores, -jnp.inf)
    top = jnp.max(scores, axis=3, keepdims=True)
    weights = jnp.exp(scores - top)
    totals = jnp.sum(weights, axis=3)
    numer = jnp.einsum(
        "chqk,ckhd->cqhd",
        weights.astype(jnp.bfloat16),
        value_set,
        preferred_element_type=jnp.float32,
    )
    attended = (
        (numer / jnp.transpose(totals, (0, 2, 1))[:, :, :, None])
        .astype(jnp.bfloat16)
        .reshape(groups, tok_rows, feat_width)
    )
    partial_value = jnp.einsum(
        "cqf,fd->cqd", attended, out_weight, preferred_element_type=jnp.float32
    )
    mixed = lax.psum_scatter(partial_value, "head", scatter_dimension=2, tiled=True)
    return mixed.astype(jnp.bfloat16)


def solution(mesh):
    in_specs = (
        P("cache", "space", "head"),
        P("cache", "space", "head"),
        P("cache", "space", "head"),
        P("cache", "space", "head"),
        P("cache", "space", "head"),
        P(),
        P(),
        P(),
        P("head", None),
    )
    out_specs = P("cache", "space", "head")
    return jax.shard_map(
        on_device, mesh=mesh, in_specs=in_specs, out_specs=out_specs, check_vma=False
    )
```

profile of v0, /device:TPU:0, one launch (start us, length us, event | category | flops | bytes accessed | tf_op | source)
XLA Modules:
  0.0 700.3 jit_solution(3270885303758558681)
XLA Ops:
  6.5 0.8 compare_select_fusion.2
  7.3 0.1 copy.49
  7.4 0.1 reshape.37
  7.5 0.0 copy-start.3
  7.5 0.8 gather_fusion
  8.3 0.1 reshape.36
  8.4 0.1 copy.50
  8.5 0.1 reduce_max.28
  8.6 0.1 reduce_max.29
  8.8 0.0 copy-done.3
  8.8 1.8 gather_fusion.1
  10.6 4.4 all-to-all-start
  15.0 0.0 all-gather.3.cloned.1.call-start
  15.1 0.1 reshape.53
  15.2 22.1 %all-to-all-done = bf16[8,80,1280]{2,1,0:T(8,128)(2,1)S(1)} async-done(((bf16[8,80,1280]{2,1,0:T(8,128)(2,1)}), bf16[8,80,1280]{2,1,0:T(8,128)(2,1)S(1)}, u32[]{:S(2)}, u32[]{:S(2)}) %all-to-all-start) | async-done | bytes 1638432 | tf_op jit(solution)/shard_map/all_to_all | solution.py:36
  37.3 1.8 gather_fusion.2
  39.1 1.7 pad_maximum_fusion
  40.8 2.7 copy.54
  43.5 0.0 all-gather.3.cloned.1.call-update
  43.5 0.0 all-gather.5.cloned.1.call-start
  43.6 0.0 copy-done.4
  43.6 1.8 gather_fusion.4
  45.4 26.0 %all_to_all.10 = bf16[8,80,1280]{2,1,0:T(8,128)(2,1)S(1)} all-to-all(bf16[8,80,1280]{2,1,0:T(8,128)(2,1)} %gather_fusion.4), channel_id=1, replica_groups=mesh['cache'=8,'space'=8,'head'=2] {'cache'}, dimensions={0} | all-to-all | bytes 3276800 | tf_op jit(solution)/shard_map/all_to_all | solution.py:35
  71.4 1.8 gather_fusion.5
  73.2 1.7 pad_maximum_fusion.1
  74.9 2.7 copy.58
  77.6 0.0 all-gather.5.cloned.1.call-update
  77.6 0.2 reduce-scatter.2.cloned.1.call-start
  77.8 0.1 constant_dynamic-slice_fusion
  77.9 0.1 copy.66
  78.0 0.1 reshape.61
  78.1 0.6 gather_fusion.3
  78.8 0.1 reshape.60
  78.9 0.1 copy.57
  78.9 0.1 iota_compare_fusion
  79.1 174.1 %all-gather.3.cloned.1.call-done = bf16[4,3,640,1280]{3,0,1,2:T(4,128)(2,1)} async-done(((bf16[4,3,80,1280]{3,0,1,2:T(4,128)(2,1)}), bf16[4,3,640,1280]{3,0,1,2:T(4,128)(2,1)}) %all-gather.3.cloned.1.call-update) | async-done | bytes 19660816 | tf_op jit(solution)/shard_map/all_gather | solution.py:45
  253.2 43.2 %copy.55 = bf16[4,3,640,1280]{2,1,3,0:T(4,128)(2,1)} copy(bf16[4,3,640,1280]{3,0,1,2:T(4,128)(2,1)} %all-gather.3.cloned.1.call-done) | data formatting | bytes 39321600 | tf_op jit(solution)/shard_map/all_gather | solution.py:45
  296.4 46.9 %reshape.31 = bf16[4,1920,10,128]{1,3,2,0:T(8,128)(2,1)} reshape(bf16[4,3,640,1280]{2,1,3,0:T(4,128)(2,1)} %copy.55) | data formatting | bytes 39321600 | tf_op jit(solution)/shard_map/reshape | solution.py:53
  343.3 118.8 %all-gather.5.cloned.1.call-done = bf16[4,3,640,1280]{3,0,1,2:T(4,128)(2,1)} async-done(((bf16[4,3,80,1280]{3,0,1,2:T(4,128)(2,1)}), bf16[4,3,640,1280]{3,0,1,2:T(4,128)(2,1)}) %all-gather.5.cloned.1.call-update) | async-done | bytes 19660816 | tf_op jit(solution)/shard_map/all_gather | solution.py:44
  462.2 42.8 %copy.59 = bf16[4,3,640,1280]{2,1,3,0:T(4,128)(2,1)} copy(bf16[4,3,640,1280]{3,0,1,2:T(4,128)(2,1)} %all-gather.5.cloned.1.call-done) | data formatting | bytes 39321600 | tf_op jit(solution)/shard_map/all_gather | solution.py:44
  505.0 46.6 %reshape.32 = bf16[4,1920,10,128]{1,3,2,0:T(8,128)(2,1)} reshape(bf16[4,3,640,1280]{2,1,3,0:T(4,128)(2,1)} %copy.59) | data formatting | bytes 39321600 | tf_op jit(solution)/shard_map/reshape | solution.py:52
  551.5 13.8 %bitcast_reduce_fusion = (f32[4,10,80]{2,1,0:T(8,128)S(1)}, f32[4,10,1920,80]{2,3,1,0:T(8,128)}) fusion(pred[4,1920]{1,0:T(4,128)(4,1)S(1)} %bitcast.57, bf16[4,1920,10,128]{1,3,2,0:T(8,128)(2,1)} %reshape.32, bf16[4,80,1280]{2,1,0:T(8,128)(2,1)S(1)} %copy-done), kind=kOutput, calls=%fused_computation.7 | convolution fusion | flops 1591292800 | bytes 45076480 | tf_op jit(solution)/shard_map/cqhd,ckhd->chqk/dot_general | solution.py:56
  565.4 11.5 %fusion.1 = f32[4,10,80]{2,1,0:T(8,128)S(1)} fusion(f32[4,10,1920,80]{2,3,1,0:T(8,128)} %get-tuple-element.6, f32[4,10,80]{2,1,0:T(8,128)S(1)} %get-tuple-element.5, pred[4,1920]{1,0:T(4,128)(4,1)S(1)} %bitcast.58), kind=kLoop, calls=%fused_computation.10 | loop fusion | flops 24572800 | bytes 24609280 | tf_op jit(solution)/shard_map/reduce_sum | solution.py:62
  576.8 22.1 %fusion.14 = bf16[4,10,10,8,128]{4,3,2,1,0:T(8,128)(2,1)S(1)} fusion(bf16[4,1920,10,128]{1,3,2,0:T(8,128)(2,1)} %reshape.31, f32[4,10,1920,80]{2,3,1,0:T(8,128)} %get-tuple-element.6, f32[4,10,80]{2,1,0:T(8,128)S(1)} %get-tuple-element.5, pred[4,1920]{1,0:T(4,128)(4,1)S(1)} %bitcast.59, f32[4,80,10]{1,2,0:T(8,128)S(1)} %bitcast.60), kind=kOutput, calls=%fused_computation.23 | convolution fusion | flops 1598259200 | bytes 45089280 | tf_op jit(solution)/shard_map/chqk,ckhd->cqhd/dot_general | solution.py:63
  598.9 11.3 %fusion.3 = f32[4,80,5120]{2,1,0:T(8,128)} fusion(bf16[1280,5120]{1,0:T(8,128)(2,1)} %param.17, bf16[4,10,10,8,128]{4,3,2,1,0:T(8,128)(2,1)S(1)} %fusion.14), kind=kOutput, calls=%fused_computation.12 | convolution fusion | flops 4194304000 | bytes 20480000 | tf_op jit(solution)/shard_map/cqf,fd->cqd/dot_general | solution.py:74
  610.2 0.0 reduce-scatter.2.cloned.1.call-update
  610.2 80.3 %reduce-scatter.2.cloned.1.call-done = f32[4,80,2560]{2,1,0:T(8,128)} async-done(((f32[4,80,5120]{2,1,0:T(8,128)}), f32[4,80,2560]{2,1,0:T(8,128)}) %reduce-scatter.2.cloned.1.call-update) | async-done | bytes 3276816 | tf_op jit(solution)/shard_map/reduce_scatter | solution.py:77
  690.5 3.3 convert_element_type.11
  (22 shorter events, 0.1 us)
Async XLA Ops:
  6.5 545.0 %copy-start = (bf16[4,80,1280]{2,1,0:T(8,128)(2,1)S(1)}, bf16[4,80,1280]{2,1,0:T(8,128)(2,1)}, u32[]{:S(2)}) copy-start(bf16[4,80,1280]{2,1,0:T(8,128)(2,1)} %param.9) | copy-start | bytes 2457604
  6.5 1.0 copy-start.1
  7.5 1.2 copy-start.3
  8.3 30.8 %copy-start.5 = (bf16[4,80,1280]{2,1,0:T(8,128)(2,1)S(1)}, bf16[4,80,1280]{2,1,0:T(8,128)(2,1)}, u32[]{:S(2)}) copy-start(bf16[4,80,1280]{2,1,0:T(8,128)(2,1)} %param.11) | copy-start | bytes 2457604
  10.6 26.7 %all-to-all-start = ((bf16[8,80,1280]{2,1,0:T(8,128)(2,1)}), bf16[8,80,1280]{2,1,0:T(8,128)(2,1)S(1)}, u32[]{:S(2)}, u32[]{:S(2)}) async-start(bf16[8,80,1280]{2,1,0:T(8,128)(2,1)} %gather_fusion.1), calls=%async_computation | async-start | bytes 3276800 | tf_op jit(solution)/shard_map/all_to_all | solution.py:36
  15.0 238.2 %all-gather.3.cloned.1.call-start = ((), (), s32[]{:S(2)}) async-start(), calls=%async_computation.3 | async-start | bytes 22118400 | tf_op jit(solution)/shard_map/all_gather | solution.py:45
  39.1 4.5 copy-start.4
  43.5 29.7 %copy-start.6 = (bf16[4,80,1280]{2,1,0:T(8,128)(2,1)S(1)}, bf16[4,80,1280]{2,1,0:T(8,128)(2,1)}, u32[]{:S(2)}) copy-start(bf16[4,80,1280]{2,1,0:T(8,128)(2,1)} %param.10) | copy-start | bytes 2457604
  43.5 418.7 %all-gather.5.cloned.1.call-start = ((), (), s32[]{:S(2)}) async-start(), calls=%async_computation.4 | async-start | bytes 22118400 | tf_op jit(solution)/shard_map/all_gather | solution.py:44
  73.2 4.6 copy-start.7
  73.2 4.9 copy-start.2
  77.6 612.9 %reduce-scatter.2.cloned.1.call-start = ((), (), s32[]{:S(2)}) async-start(), calls=%async_computation.5 | async-start | bytes 9830400 | tf_op jit(solution)/shard_map/reduce_scatter | solution.py:77
Sparse Core Ops, SparseCore 0:
  43.6 209.4 all-gather.2
  255.5 206.6 all-gather.4
  610.4 80.1 reduce-scatter.1
where the time goes:
time: 706 us; the launch traced here: 700 us
  waiting for transfers between devices  395 us (56%)
  local copies, waits for them, and re-layouts  195 us (28%)
  matrix products  47.2 us (7%)
  blocking collectives  26 us (4%)
  other arithmetic  19.2 us (3%)
  between operations  13.3 us (2%)
    all_gather x1, waiting for transfers between devices, on_device(): lax.all_gather(local_values, 'space', axis=2, tiled=True)  174 us
    all_gather x1, waiting for transfers between devices, on_device(): lax.all_gather(local_keys, 'space', axis=2, tiled=True)  119 us
    reduce_scatter x1, waiting for transfers between devices, on_device(): lax.psum_scatter(partial_value, 'head', scatter_dimension=2, tiled=True)  80.3 us
    reshape x1, local copies, waits for them, and re-layouts, on_device(): value_set = whole_values.reshape(groups, -1, heads_here, HD)  46.9 us
    reshape x1, local copies, waits for them, and re-layouts, on_device(): key_set = whole_keys.reshape(groups, -1, heads_here, HD)  46.6 us
    all_gather x1, local copies, waits for them, and re-layouts, on_device(): lax.all_gather(local_values, 'space', axis=2, tiled=True)  43.2 us
    all_gather x1, local copies, waits for them, and re-layouts, on_device(): lax.all_gather(local_keys, 'space', axis=2, tiled=True)  42.8 us
    all_to_all x1, blocking collectives, on_device(): lax.all_to_all(send_keys, 'cache', split_axis=0, concat_axis=0, tiled=True)  26 us
  transfers between devices with their start and end apart: 4, of which 4 were waited for; matrix products, arithmetic and copies ran while one was open for 14% of the time, Pallas kernels for 0%

commit v1 on v0

v1 whole, which is shorter than its diff:
```python
import math

import jax
import jax.numpy as jnp
from jax import lax
from jax.experimental import pallas as pl
from jax.experimental.pallas import tpu as pltpu
from jax.sharding import PartitionSpec as P

HD = 128
WIN = 2
SPANS = 4
GROUPS = 8
SPACE = 8
ROWS = 80
SPAN = SPACE * ROWS
HEADS = 10
WIDE = SPACE * HD
PAIRS = 5
UNITS = 3 * PAIRS + 2 * WIN
VMEM = pl.BlockSpec(memory_space=pltpu.VMEM)
SMEM = pl.BlockSpec(memory_space=pltpu.SMEM)
MIB = 1 << 20


def params(mib):
    return pltpu.CompilerParams(vmem_limit_bytes=mib * MIB)


def picked(window, span_slot, block, group):
    place = jnp.int32(0)
    for span in range(SPANS):
        for w in range(WIN):
            slot = span_slot[window[block * SPANS + span, w]]
            place = jnp.where((slot >> 1) == group, slot & 1, place)
    return place


def pack_slots(window, span_slot, cache_keys, cache_values, by_head, *rest):
    me = lax.axis_index("cache")
    for head in range(SPACE):
        for kv, source in enumerate((cache_keys, cache_values)):
            for slot in range(2):
                row = (kv * 2 + slot) * ROWS
                by_head[head, row : row + ROWS] = source[slot, :, head * HD : (head + 1) * HD]
    for step in range(GROUPS):
        slot = picked(window, span_slot, (me + step) & 7, me)
        for kv, source in enumerate((cache_keys, cache_values)):
            rest[step][kv] = source[slot, :, WIDE:]


def pack_wide(window, span_slot, by_head, sent):
    me = lax.axis_index("cache")
    for block in range(GROUPS):
        slot = picked(window, span_slot, block, me)
        for kv in range(2):
            for space in range(SPACE):
                row = (kv * SPACE + space) * ROWS
                start = pl.multiple_of((kv * 2 + slot) * ROWS, 16)
                sent[block, row : row + ROWS] = by_head[space, pl.ds(start, ROWS)]


def pack_pairs(window, span_slot, queries, keys, values, *refs):
    rest, sent, held = refs[:GROUPS], refs[GROUPS : GROUPS + SPACE], refs[-1]
    group = lax.axis_index("cache")
    me = lax.axis_index("space")
    for step in range(GROUPS):
        held[(group - step) & 7] = rest[step][...]
    for step in range(SPACE):
        to = (me + step) & 7
        span = to >> 1
        wide = pl.ds(pl.multiple_of(to * HD, HD), HD)
        last = pl.multiple_of((to & 1) * HD, HD)
        for kind, source in enumerate((queries, keys, values)):
            for pair in range(SPANS):
                sent[step][kind * PAIRS + pair] = source[pair, :, wide]
            sent[step][kind * PAIRS + SPANS] = source[
                span, :, pl.ds(pl.multiple_of(WIDE + last, HD), HD)
            ]
        for w in range(WIN):
            owner = span_slot[window[group * SPANS + span, w]] >> 1
            for kv in range(2):
                sent[step][3 * PAIRS + 2 * w + kv] = held[owner, kv, :, pl.ds(last, HD)]


def attend(window, span_slot, counts, *refs):
    came, wide, out, q_all, k_all, v_all, done = (refs[:SPACE],) + refs[SPACE:]
    group = lax.axis_index("cache")
    me = lax.axis_index("space")
    factor = math.log2(math.e) / math.sqrt(HD)
    spots = lax.broadcasted_iota(jnp.int32, (SPAN, HD), 0)
    v_all[0:SPAN, HD:] = jnp.ones((SPAN, HD), jnp.bfloat16)

    @pl.loop(0, PAIRS)
    def _(pair):
        for step in range(SPACE):
            rows = pl.ds(step * ROWS, ROWS)
            q_all[rows] = came[step][pair]
            k_all[rows] = came[step][PAIRS + pair]
            v_all[rows, 0:HD] = came[step][2 * PAIRS + pair]
        span = jnp.where(pair < SPANS, pair, me >> 1)
        for w in range(WIN):
            chosen = window[group * SPANS + span, w]
            limit = counts[chosen]
            owner = span_slot[chosen] >> 1
            base = (1 + w) * SPAN
            part = pl.ds(base, SPAN)

            @pl.when(pair < SPANS)
            def _():
                k_all[part] = wide[owner, 0:SPAN]
                v_all[part, 0:HD] = wide[owner, SPAN:]

            @pl.when(pair == SPANS)
            def _():
                for step in range(SPACE):
                    start = pl.multiple_of(base + ((me - step) & 7) * ROWS, 16)
                    k_all[pl.ds(start, ROWS)] = came[step][3 * PAIRS + 2 * w]
                    v_all[pl.ds(start, ROWS), 0:HD] = came[step][3 * PAIRS + 2 * w + 1]

            valid = spots < limit
            first = jnp.broadcast_to(k_all[base : base + 1].astype(jnp.float32), (SPAN, HD))
            k_all[part] = jnp.where(valid, k_all[part].astype(jnp.float32), first).astype(
                jnp.bfloat16
            )
            v_all[part, 0:HD] = jnp.where(
                valid, v_all[part, 0:HD].astype(jnp.float32), 0.0
            ).astype(jnp.bfloat16)
            v_all[part, HD:] = jnp.where(valid, 1.0, 0.0).astype(jnp.bfloat16)
        block = SPAN // 2
        for start in range(0, SPAN, block):
            scores = lax.dot_general(
                q_all[start : start + block],
                k_all[...],
                (((1,), (1,)), ((), ())),
                preferred_element_type=jnp.float32,
            )
            top = jnp.max(scores, axis=1, keepdims=True)
            weights = jnp.exp2((scores - top) * factor).astype(jnp.bfloat16)
            both = jnp.dot(weights, v_all[...], preferred_element_type=jnp.float32)
            done[start : start + block] = (both[:, 0:HD] / both[:, HD:]).astype(jnp.bfloat16)
        for step in range(SPACE):
            to = (me - step) & 7
            for half in range(2):
                out[2 * to + half, pair] = done[step * ROWS : (step + 1) * ROWS]


def project(half, came, own_weight, other_weight, out, features):
    @pl.when(pl.program_id(0) == 0)
    def _():
        for part in range(2):
            source = half[0] if part == 0 else 1 - half[0]
            for space in range(SPACE):
                for pair in range(SPANS):
                    features[part, pair * ROWS : (pair + 1) * ROWS, space * HD : (space + 1) * HD] = (
                        came[2 * space + source, pair * ROWS : (pair + 1) * ROWS]
                    )
                span, column = space // 2, WIDE + space % 2 * HD
                features[part, span * ROWS : (span + 1) * ROWS, column : column + HD] = came[
                    2 * space + source, SPANS * ROWS :
                ]

    total = jnp.dot(features[0], own_weight[...], preferred_element_type=jnp.float32)
    total += jnp.dot(features[1], other_weight[...], preferred_element_type=jnp.float32)
    out[...] = total.astype(jnp.bfloat16)


def shift(x, axis, step):
    return lax.ppermute(x, axis, [(i, (i + step) % 8) for i in range(8)])


def on_device(
    queries, keys, values, cache_keys, cache_values, window, span_slot, counts, out_weight
):
    bf16 = jnp.bfloat16
    shape = jax.ShapeDtypeStruct
    group = lax.axis_index("cache")
    half = lax.axis_index("head")
    depth, width = out_weight.shape
    columns = width // 2

    rows = depth // GROUPS
    lent = lax.dynamic_slice(out_weight, (group * rows, (1 - half) * columns), (rows, columns))
    lent = lax.ppermute(lent, "head", [(0, 1), (1, 0)])
    other_weight = lax.all_gather(lent, "cache", axis=0, tiled=True)

    by_head, *rest = pl.pallas_call(
        pack_slots,
        out_shape=[shape((SPACE, 4 * ROWS, HD), bf16)]
        + [shape((2, ROWS, 2 * HD), bf16)] * GROUPS,
        in_specs=[SMEM] * 2 + [VMEM] * 2,
        out_specs=[VMEM] * (1 + GROUPS),
        compiler_params=params(16),
        name="pack_slots",
    )(window, span_slot, cache_keys, cache_values)
    by_head = lax.all_to_all(by_head, "space", split_axis=0, concat_axis=0, tiled=True)
    rest = [rest[0]] + [shift(rest[step], "cache", step) for step in range(1, GROUPS)]

    wide = pl.pallas_call(
        pack_wide,
        out_shape=shape((GROUPS, 2 * SPAN, HD), bf16),
        in_specs=[SMEM] * 2 + [VMEM],
        out_specs=VMEM,
        compiler_params=params(16),
        name="pack_wide",
    )(window, span_slot, by_head)
    wide = lax.all_to_all(wide, "cache", split_axis=0, concat_axis=0, tiled=True)

    pairs = pl.pallas_call(
        pack_pairs,
        out_shape=[shape((UNITS, ROWS, HD), bf16)] * SPACE,
        in_specs=[SMEM] * 2 + [VMEM] * (3 + GROUPS),
        out_specs=[VMEM] * SPACE,
        scratch_shapes=[pltpu.VMEM((GROUPS, 2, ROWS, 2 * HD), bf16)],
        compiler_params=params(16),
        name="pack_pairs",
    )(window, span_slot, queries, keys, values, *rest)
    came = [pairs[0]] + [shift(pairs[step], "space", step) for step in range(1, SPACE)]

    attended = pl.pallas_call(
        attend,
        out_shape=shape((2 * SPACE, PAIRS, ROWS, HD), bf16),
        in_specs=[SMEM] * 3 + [VMEM] * (SPACE + 1),
        out_specs=VMEM,
        scratch_shapes=[
            pltpu.VMEM((SPAN, HD), bf16),
            pltpu.VMEM((3 * SPAN, HD), bf16),
            pltpu.VMEM((3 * SPAN, 2 * HD), bf16),
            pltpu.VMEM((SPAN, HD), bf16),
        ],
        compiler_params=params(40),
        name="attend",
    )(window, span_slot, counts, *came, wide)
    attended = attended.reshape(2 * SPACE, PAIRS * ROWS, HD)
    attended = lax.all_to_all(
        attended, ("space", "head"), split_axis=0, concat_axis=0, tiled=True
    )

    tile = 512
    steps = columns // tile
    mixed = pl.pallas_call(
        project,
        grid_spec=pltpu.PrefetchScalarGridSpec(
            num_scalar_prefetch=1,
            grid=(steps,),
            in_specs=[
                pl.BlockSpec((2 * SPACE, PAIRS * ROWS, HD), lambda n, h: (0, 0, 0)),
                pl.BlockSpec((depth, tile), lambda n, h: (0, h[0] * steps + n)),
                pl.BlockSpec((depth, tile), lambda n, h: (0, n)),
            ],
            out_specs=pl.BlockSpec((SPANS * ROWS, tile), lambda n, h: (0, n)),
            scratch_shapes=[pltpu.VMEM((2, SPANS * ROWS, depth), bf16)],
        ),
        out_shape=shape((SPANS * ROWS, columns), bf16),
        compiler_params=params(32),
        name="project",
    )(half.astype(jnp.int32).reshape(1), attended, out_weight, other_weight)
    return mixed.reshape(SPANS, ROWS, columns)


def solution(mesh):
    in_specs = (
        P("cache", "space", "head"),
        P("cache", "space", "head"),
        P("cache", "space", "head"),
        P("cache", "space", "head"),
        P("cache", "space", "head"),
        P(),
        P(),
        P(),
        P("head", None),
    )
    out_specs = P("cache", "space", "head")
    return jax.shard_map(
        on_device, mesh=mesh, in_specs=in_specs, out_specs=out_specs, check_vma=False
    )
```

time: 706 us -> 230 us (0.33)
  waiting for transfers between devices: 395 us -> 66 us
  local copies, waits for them, and re-layouts: 195 us -> 29.9 us
  matrix products: 47.2 us -> 0 us
  starting transfers between devices: 4.68 us -> 49.3 us
  blocking collectives: 26 us -> 49.3 us
  Pallas kernels: 0 us -> 21.6 us
  other arithmetic: 19.2 us -> 0 us
    all_gather x2 -> x1, waiting for transfers between devices: 293 us -> 0.01 us  [on_device(): other_weight = lax.all_gather(lent, 'cache', axis=0, tiled=True)]
    reshape x2 -> x0, local copies, waits for them, and re-layouts: 93.5 us -> none  [the longest x1 46.9 us: on_device(): value_set = whole_values.reshape(groups, -1, heads_here, HD)]
    all_gather x2 -> x0, local copies, waits for them, and re-layouts: 86 us -> none  [the longest x1 43.2 us: on_device(): lax.all_gather(local_values, 'space', axis=2, tiled=True)]
    reduce_scatter x1 -> x0, waiting for transfers between devices: 80.3 us -> none  [on_device(): lax.psum_scatter(partial_value, 'head', scatter_dimension=2, tiled=True)]
    ppermute x0 -> x15, waiting for transfers between devices: none -> 66 us  [the longest x14 47.8 us: shift(): return lax.ppermute(x, axis, [(i, (i + step) % 8) for i in range(8)])]
    dot_general x3 -> x0, matrix products: 47.2 us -> none  [the longest x1 22.1 us: on_device(): jnp.einsum('chqk,ckhd->cqhd', weights.astype(jnp.bfloat16), value_set, pr...]
    ppermute x0 -> x15, starting transfers between devices: none -> 44.9 us  [the longest x14 43.1 us: shift(): return lax.ppermute(x, axis, [(i, (i + step) % 8) for i in range(8)])]
    unnamed x17 -> x63, local copies, waits for them, and re-layouts: 0.13 us -> 28.6 us
  transfers between devices with their start and end apart: 4 -> 17, of which waited for: 4 -> 7; matrix products, arithmetic and copies ran while one was open for 14% -> 0% of each run, Pallas kernels for 0% -> 6%
where the time goes in v1:
time: 230 us
  waiting for transfers between devices  66 us (29%)
  starting transfers between devices  49.3 us (21%)
  blocking collectives  49.3 us (21%)
  local copies, waits for them, and re-layouts  29.9 us (13%)
  Pallas kernels  21.6 us (9%)
  between operations  13.5 us (6%)
    ppermute x14, waiting for transfers between devices, shift(): return lax.ppermute(x, axis, [(i, (i + step) % 8) for i in range(8)])  47.8 us
    ppermute x14, starting transfers between devices, shift(): return lax.ppermute(x, axis, [(i, (i + step) % 8) for i in range(8)])  43.1 us
    all_to_all x1, blocking collectives, on_device(): lax.all_to_all(attended, ('space', 'head'), split_axis=0, concat_axis=0,...  29.1 us
    unnamed x63, local copies, waits for them, and re-layouts  28.6 us
    all_to_all x1, blocking collectives, on_device(): lax.all_to_all(by_head, 'space', split_axis=0, concat_axis=0, tiled=True)  20.1 us
    ppermute x1, waiting for transfers between devices, on_device(): lent = lax.ppermute(lent, 'head', [(0, 1), (1, 0)])  18.2 us
    pallas_call x1, Pallas kernels, on_device(): pl.pallas_call(attend, out_shape=shape((2 * SPACE, PAIRS, ROWS, HD), bf16...  11.1 us
    pallas_call x1, Pallas kernels, on_device(): pl.pallas_call(project, grid_spec=pltpu.PrefetchScalarGridSpec(num_scalar...  7.04 us
  transfers between devices with their start and end apart: 17, of which 7 were waited for; matrix products, arithmetic and copies ran while one was open for 0% of the time, Pallas kernels for 6%

profile of v1, /device:TPU:0, one launch (start us, length us, event | category | flops | bytes accessed | tf_op | source)
XLA Modules:
  0.0 229.6 jit_solution(10256964721534074220)
XLA Ops:
  6.5 1.3 dynamic_slice.3
  7.8 1.7 collective-permute-start.14
  9.6 18.2 %collective-permute-done.14 = bf16[160,2560]{1,0:T(8,128)(2,1)S(1)} collective-permute-done((bf16[160,2560]{1,0:T(8,128)(2,1)S(1)}, bf16[160,2560]{1,0:T(8,128)(2,1)S(1)}, u32[]{:S(2)}, u32[]{:S(2)}) %collective-permute-start.14) | collective-permute-done | bytes 819232 | tf_op jit(solution)/shard_map/ppermute | solution.py:184
  27.8 0.9 copy-done.30
  28.7 0.8 copy.13.window
  29.5 0.6 copy-done.20
  30.1 1.1 pack_slots.1
  33.1 0.6 copy-done.26
  35.6 20.1 %all_to_all.15.by_head = bf16[8,320,128]{2,1,0:T(8,128)(2,1)S(1)} all-to-all(bf16[8,320,128]{2,1,0:T(8,128)(2,1)S(1)} %get-tuple-element.38), channel_id=1, replica_groups=mesh['cache'=8,'space'=8,'head'=2] {'space'}, dimensions={0} | all-to-all | bytes 1310720 | tf_op jit(solution)/shard_map/all_to_all | solution.py:196
  55.8 1.0 pack_wide.1
  56.8 1.6 copy-done.1
  58.3 4.4 %all-to-all-start.1 = ((bf16[8,1280,128]{2,1,0:T(8,128)(2,1)}), bf16[8,1280,128]{2,1,0:T(8,128)(2,1)S(1)}, u32[]{:S(2)}, u32[]{:S(2)}) async-start(bf16[8,1280,128]{2,1,0:T(8,128)(2,1)} %copy-done.1), calls=%async_computation.1 | async-start | bytes 5242880 | tf_op jit(solution)/shard_map/all_to_all | solution.py:207
  63.3 1.7 collective-permute-start.1
  64.9 1.9 collective-permute-start.2
  66.9 2.1 collective-permute-start.3
  68.9 1.7 collective-permute-start.4
  70.6 30.7 %collective-permute-done.refs_1_ = bf16[2,80,256]{2,1,0:T(8,128)(2,1)S(1)} collective-permute-done((bf16[2,80,256]{2,1,0:T(8,128)(2,1)}, bf16[2,80,256]{2,1,0:T(8,128)(2,1)S(1)}, u32[]{:S(2)}, u32[]{:S(2)}) %collective-permute-start) | collective-permute-done | bytes 81952 | tf_op jit(solution)/shard_map/ppermute | solution.py:169
  101.3 0.9 collective-permute-start.5
  102.2 1.2 collective-permute-start.6
  103.4 1.8 collective-permute-done.2.refs_3_
  106.0 1.1 copy-done.4
  107.1 1.1 copy-done.5
  108.3 1.4 pack_pairs.1
  109.7 0.7 copy-done.8
  110.4 3.1 %collective-permute-start.10 = (bf16[19,80,128]{2,1,0:T(8,128)(2,1)S(1)}, bf16[19,80,128]{2,1,0:T(8,128)(2,1)S(1)}, u32[]{:S(2)}, u32[]{:S(2)}) collective-permute-start(bf16[19,80,128]{2,1,0:T(8,128)(2,1)S(1)} %get-tuple-element.34), channel_id=1, source_target_pairs={{0,8},{2,10},{4,12},{6,14},{8,0},{10,2},{12,4},{14,6},{1,9},{3,11}... | collective-permute-start | bytes 1167368 | tf_op jit(solution)/shard_map/ppermute | solution.py:169
  113.6 2.8 %collective-permute-start.11 = (bf16[19,80,128]{2,1,0:T(8,128)(2,1)S(1)}, bf16[19,80,128]{2,1,0:T(8,128)(2,1)S(1)}, u32[]{:S(2)}, u32[]{:S(2)}) collective-permute-start(bf16[19,80,128]{2,1,0:T(8,128)(2,1)S(1)} %get-tuple-element.35), channel_id=1, source_target_pairs={{0,10},{2,12},{4,14},{6,0},{8,2},{10,4},{12,6},{14,8},{1,11},{3,13... | collective-permute-start | bytes 1167368 | tf_op jit(solution)/shard_map/ppermute | solution.py:169
  116.4 2.9 %collective-permute-start.12 = (bf16[19,80,128]{2,1,0:T(8,128)(2,1)S(1)}, bf16[19,80,128]{2,1,0:T(8,128)(2,1)S(1)}, u32[]{:S(2)}, u32[]{:S(2)}) collective-permute-start(bf16[19,80,128]{2,1,0:T(8,128)(2,1)S(1)} %get-tuple-element.36), channel_id=1, source_target_pairs={{0,12},{2,14},{4,0},{6,2},{8,4},{10,6},{12,8},{14,10},{1,13},{3,15... | collective-permute-start | bytes 1167368 | tf_op jit(solution)/shard_map/ppermute | solution.py:169
  119.4 3.5 %collective-permute-start.7 = (bf16[19,80,128]{2,1,0:T(8,128)(2,1)S(1)}, bf16[19,80,128]{2,1,0:T(8,128)(2,1)S(1)}, u32[]{:S(2)}, u32[]{:S(2)}) collective-permute-start(bf16[19,80,128]{2,1,0:T(8,128)(2,1)S(1)} %get-tuple-element.31), channel_id=1, source_target_pairs={{0,2},{2,4},{4,6},{6,8},{8,10},{10,12},{12,14},{14,0},{1,3},{3,5},... | collective-permute-start | bytes 1167368 | tf_op jit(solution)/shard_map/ppermute | solution.py:169
  122.9 0.9 collective-permute-done.10.refs_4_
  123.8 10.3 %collective-permute-start.8 = (bf16[19,80,128]{2,1,0:T(8,128)(2,1)S(1)}, bf16[19,80,128]{2,1,0:T(8,128)(2,1)S(1)}, u32[]{:S(2)}, u32[]{:S(2)}) collective-permute-start(bf16[19,80,128]{2,1,0:T(8,128)(2,1)S(1)} %get-tuple-element.32), channel_id=1, source_target_pairs={{0,4},{2,6},{4,8},{6,10},{8,12},{10,14},{12,0},{14,2},{1,5},{3,7},... | collective-permute-start | bytes 1167368 | tf_op jit(solution)/shard_map/ppermute | solution.py:169
  134.2 10.5 %collective-permute-start.9 = (bf16[19,80,128]{2,1,0:T(8,128)(2,1)S(1)}, bf16[19,80,128]{2,1,0:T(8,128)(2,1)S(1)}, u32[]{:S(2)}, u32[]{:S(2)}) collective-permute-start(bf16[19,80,128]{2,1,0:T(8,128)(2,1)S(1)} %get-tuple-element.33), channel_id=1, source_target_pairs={{0,6},{2,8},{4,10},{6,12},{8,14},{10,0},{12,2},{14,4},{1,7},{3,9},... | collective-permute-start | bytes 1167368 | tf_op jit(solution)/shard_map/ppermute | solution.py:169
  144.6 0.7 copy-done.10
  145.4 0.7 copy-done.12
  146.1 0.8 copy-done.14
  146.9 13.5 %collective-permute-done.8.refs_2_ = bf16[19,80,128]{2,1,0:T(8,128)(2,1)S(1)} collective-permute-done((bf16[19,80,128]{2,1,0:T(8,128)(2,1)S(1)}, bf16[19,80,128]{2,1,0:T(8,128)(2,1)S(1)}, u32[]{:S(2)}, u32[]{:S(2)}) %collective-permute-start.8) | collective-permute-done | bytes 389152 | tf_op jit(solution)/shard_map/ppermute | solution.py:169
  160.4 0.7 copy-done.16
  161.2 0.8 copy-done.18
  161.9 1.0 copy-done.9
  162.9 1.0 copy-done.11
  163.9 1.0 copy-done.13
  164.9 1.0 copy-done.15
  165.9 1.0 copy-done.17
  166.9 1.0 copy-done.19
  167.9 11.1 %attend.1 = bf16[16,5,80,128]{3,2,1,0:T(8,128)(2,1)S(1)} custom-call(s32[32,2]{1,0:T(8,128)S(1)} %copy.13.window, s32[16]{0:T(128)S(1)} %copy-done.21, s32[16]{0:T(128)S(1)} %copy-done.22, bf16[19,80,128]{2,1,0:T(8,128)(2,1)S(1)} %copy-done.9, bf16[19,80,128]{2,1,0:T(8,128)(2,1)S(1)} %copy-done.15, bf16[19,80,128]{2,1,0:T(8,128)(2,1)S(1)} %copy-done.17, ...), custom_call_target="tpu_custom_call" | custom-call | tf_op jit(solution)/shard_map/attend/pallas_call | solution.py:220
  179.0 29.1 %all_to_all.16.came = bf16[16,400,128]{2,1,0:T(8,128)(2,1)S(1)} all-to-all(bf16[16,400,128]{2,1,0:T(8,128)(2,1)S(1)} %bitcast.3), channel_id=1, replica_groups=mesh['cache'=8,'space'=8,'head'=2] {'space','head'}, dimensions={0} | all-to-all | bytes 3276800 | tf_op jit(solution)/shard_map/all_to_all | solution.py:235
  208.1 4.7 %copy-done = bf16[1280,5120]{1,0:T(8,128)(2,1)S(1)} copy-done((bf16[1280,5120]{1,0:T(8,128)(2,1)S(1)}, bf16[1280,5120]{1,0:T(8,128)(2,1)}, u32[]{:S(2)}) %copy-start) | copy-done | bytes 13107224
  212.9 2.9 %copy-done.2 = bf16[1280,2560]{1,0:T(8,128)(2,1)S(1)} copy-done((bf16[1280,2560]{1,0:T(8,128)(2,1)S(1)}, bf16[1280,2560]{1,0:T(8,128)(2,1)}, u32[]{:S(2)}) %copy-start.2) | copy-done | bytes 6553624
  215.7 7.0 %project.1 = bf16[320,2560]{1,0:T(8,128)(2,1)} custom-call(s32[1]{0:T(128)} %bitcast.half, bf16[16,400,128]{2,1,0:T(8,128)(2,1)S(1)} %all_to_all.16.came, bf16[1280,5120]{1,0:T(8,128)(2,1)S(1)} %copy-done, bf16[1280,2560]{1,0:T(8,128)(2,1)S(1)} %copy-done.2), custom_call_target="tpu_custom_call" | custom-call | tf_op jit(solution)/shard_map/project/pallas_call | solution.py:241
  (58 shorter events, 5.2 us)
Async XLA Ops:
  6.5 22.9 %copy-start.6 = (bf16[2,80,1280]{2,1,0:T(8,128)(2,1)S(1)}, bf16[2,80,1280]{2,1,0:T(8,128)(2,1)}, u32[]{:S(2)}) copy-start(bf16[2,80,1280]{2,1,0:T(8,128)(2,1)} %cache_keys.1) | copy-start | bytes 1228804
  6.5 22.9 %copy-start.7 = (bf16[2,80,1280]{2,1,0:T(8,128)(2,1)S(1)}, bf16[2,80,1280]{2,1,0:T(8,128)(2,1)}, u32[]{:S(2)}) copy-start(bf16[2,80,1280]{2,1,0:T(8,128)(2,1)} %cache_values.1) | copy-start | bytes 1228804
  6.5 49.2 %copy-start.21 = (s32[16]{0:T(128)S(1)}, s32[16]{0:T(128)}, u32[]{:S(2)}) copy-start(s32[16]{0:T(128)} %span_slot.7) | copy-start | bytes 196
  6.5 201.6 %all-gather.2.cloned.1.call-start = ((), (), s32[]{:S(2)}) async-start(), calls=%async_computation.3 | async-start | bytes 7372800 | tf_op jit(solution)/shard_map/all_gather | solution.py:185
  7.8 20.0 %collective-permute-start.14 = (bf16[160,2560]{1,0:T(8,128)(2,1)S(1)}, bf16[160,2560]{1,0:T(8,128)(2,1)S(1)}, u32[]{:S(2)}, u32[]{:S(2)}) collective-permute-start(bf16[160,2560]{1,0:T(8,128)(2,1)S(1)} %dynamic_slice.3), channel_id=1, source_target_pairs={{0,1},{1,0},{2,3},{3,2},{4,5},{5,4},{6,7},{7,6},{8,9},{9,8},{10,11... | collective-permute-start | bytes 2457608 | tf_op jit(solution)/shard_map/ppermute | solution.py:184
  27.8 0.9 copy-start.30
  29.5 0.7 copy-start.20
  31.2 0.6 copy-start.23
  31.8 0.6 copy-start.24
  32.5 0.6 copy-start.25
  33.1 0.6 copy-start.26
  33.7 0.6 copy-start.27
  34.4 0.6 copy-start.28
  35.0 0.6 copy-start.29
  56.8 1.6 copy-start.1
  58.3 47.7 %copy-start.3 = (bf16[4,80,1280]{2,1,0:T(8,128)(2,1)S(1)}, bf16[4,80,1280]{2,1,0:T(8,128)(2,1)}, u32[]{:S(2)}) copy-start(bf16[4,80,1280]{2,1,0:T(8,128)(2,1)} %queries.1) | copy-start | bytes 2457604
  58.3 103.6 %all-to-all-start.1 = ((bf16[8,1280,128]{2,1,0:T(8,128)(2,1)}), bf16[8,1280,128]{2,1,0:T(8,128)(2,1)S(1)}, u32[]{:S(2)}, u32[]{:S(2)}) async-start(bf16[8,1280,128]{2,1,0:T(8,128)(2,1)} %copy-done.1), calls=%async_computation.1 | async-start | bytes 5242880 | tf_op jit(solution)/shard_map/all_to_all | solution.py:207
  62.8 99.1 %copy-start.22 = (s32[16]{0:T(128)S(1)}, s32[16]{0:T(128)}, u32[]{:S(2)}) copy-start(s32[16]{0:T(128)} %counts.1) | copy-start | bytes 196
  62.8 38.6 %collective-permute-start = (bf16[2,80,256]{2,1,0:T(8,128)(2,1)}, bf16[2,80,256]{2,1,0:T(8,128)(2,1)S(1)}, u32[]{:S(2)}, u32[]{:S(2)}) collective-permute-start(bf16[2,80,256]{2,1,0:T(8,128)(2,1)} %copy-done.29), channel_id=1, source_target_pairs={{0,16},{16,32},{32,48},{48,64},{64,80},{80,96},{96,112},{112,0},{1... | collective-permute-start | bytes 245768 | tf_op jit(solution)/shard_map/ppermute | solution.py:169
  63.3 38.9 %collective-permute-start.1 = (bf16[2,80,256]{2,1,0:T(8,128)(2,1)}, bf16[2,80,256]{2,1,0:T(8,128)(2,1)S(1)}, u32[]{:S(2)}, u32[]{:S(2)}) collective-permute-start(bf16[2,80,256]{2,1,0:T(8,128)(2,1)} %copy-done.28), channel_id=1, source_target_pairs={{0,32},{16,48},{32,64},{48,80},{64,96},{80,112},{96,0},{112,16},{1... | collective-permute-start | bytes 245768 | tf_op jit(solution)/shard_map/ppermute | solution.py:169
  64.9 40.2 %collective-permute-start.2 = (bf16[2,80,256]{2,1,0:T(8,128)(2,1)}, bf16[2,80,256]{2,1,0:T(8,128)(2,1)S(1)}, u32[]{:S(2)}, u32[]{:S(2)}) collective-permute-start(bf16[2,80,256]{2,1,0:T(8,128)(2,1)} %copy-done.27), channel_id=1, source_target_pairs={{0,48},{16,64},{32,80},{48,96},{64,112},{80,0},{96,16},{112,32},{1... | collective-permute-start | bytes 245768 | tf_op jit(solution)/shard_map/ppermute | solution.py:169
  66.9 38.6 %collective-permute-start.3 = (bf16[2,80,256]{2,1,0:T(8,128)(2,1)}, bf16[2,80,256]{2,1,0:T(8,128)(2,1)S(1)}, u32[]{:S(2)}, u32[]{:S(2)}) collective-permute-start(bf16[2,80,256]{2,1,0:T(8,128)(2,1)} %copy-done.26), channel_id=1, source_target_pairs={{0,64},{16,80},{32,96},{48,112},{64,0},{80,16},{96,32},{112,48},{1... | collective-permute-start | bytes 245768 | tf_op jit(solution)/shard_map/ppermute | solution.py:169
  68.9 36.6 %collective-permute-start.4 = (bf16[2,80,256]{2,1,0:T(8,128)(2,1)}, bf16[2,80,256]{2,1,0:T(8,128)(2,1)S(1)}, u32[]{:S(2)}, u32[]{:S(2)}) collective-permute-start(bf16[2,80,256]{2,1,0:T(8,128)(2,1)} %copy-done.25), channel_id=1, source_target_pairs={{0,80},{16,96},{32,112},{48,0},{64,16},{80,32},{96,48},{112,64},{1... | collective-permute-start | bytes 245768 | tf_op jit(solution)/shard_map/ppermute | solution.py:169
  101.3 4.7 %collective-permute-start.5 = (bf16[2,80,256]{2,1,0:T(8,128)(2,1)}, bf16[2,80,256]{2,1,0:T(8,128)(2,1)S(1)}, u32[]{:S(2)}, u32[]{:S(2)}) collective-permute-start(bf16[2,80,256]{2,1,0:T(8,128)(2,1)} %copy-done.24), channel_id=1, source_target_pairs={{0,96},{16,112},{32,0},{48,16},{64,32},{80,48},{96,64},{112,80},{1... | collective-permute-start | bytes 245768 | tf_op jit(solution)/shard_map/ppermute | solution.py:169
  102.2 3.8 %collective-permute-start.6 = (bf16[2,80,256]{2,1,0:T(8,128)(2,1)}, bf16[2,80,256]{2,1,0:T(8,128)(2,1)S(1)}, u32[]{:S(2)}, u32[]{:S(2)}) collective-permute-start(bf16[2,80,256]{2,1,0:T(8,128)(2,1)} %copy-done.23), channel_id=1, source_target_pairs={{0,112},{16,0},{32,16},{48,32},{64,48},{80,64},{96,80},{112,96},{1... | collective-permute-start | bytes 245768 | tf_op jit(solution)/shard_map/ppermute | solution.py:169
  106.0 1.1 copy-start.4
  107.1 1.1 copy-start.5
  109.7 0.7 copy-start.8
  110.4 13.4 %collective-permute-start.10 = (bf16[19,80,128]{2,1,0:T(8,128)(2,1)S(1)}, bf16[19,80,128]{2,1,0:T(8,128)(2,1)S(1)}, u32[]{:S(2)}, u32[]{:S(2)}) collective-permute-start(bf16[19,80,128]{2,1,0:T(8,128)(2,1)S(1)} %get-tuple-element.34), channel_id=1, source_target_pairs={{0,8},{2,10},{4,12},{6,14},{8,0},{10,2},{12,4},{14,6},{1,9},{3,11}... | collective-permute-start | bytes 1167368 | tf_op jit(solution)/shard_map/ppermute | solution.py:169
  113.6 20.6 %collective-permute-start.11 = (bf16[19,80,128]{2,1,0:T(8,128)(2,1)S(1)}, bf16[19,80,128]{2,1,0:T(8,128)(2,1)S(1)}, u32[]{:S(2)}, u32[]{:S(2)}) collective-permute-start(bf16[19,80,128]{2,1,0:T(8,128)(2,1)S(1)} %get-tuple-element.35), channel_id=1, source_target_pairs={{0,10},{2,12},{4,14},{6,0},{8,2},{10,4},{12,6},{14,8},{1,11},{3,13... | collective-permute-start | bytes 1167368 | tf_op jit(solution)/shard_map/ppermute | solution.py:169
  116.4 28.2 %collective-permute-start.12 = (bf16[19,80,128]{2,1,0:T(8,128)(2,1)S(1)}, bf16[19,80,128]{2,1,0:T(8,128)(2,1)S(1)}, u32[]{:S(2)}, u32[]{:S(2)}) collective-permute-start(bf16[19,80,128]{2,1,0:T(8,128)(2,1)S(1)} %get-tuple-element.36), channel_id=1, source_target_pairs={{0,12},{2,14},{4,0},{6,2},{8,4},{10,6},{12,8},{14,10},{1,13},{3,15... | collective-permute-start | bytes 1167368 | tf_op jit(solution)/shard_map/ppermute | solution.py:169
  119.4 26.0 %collective-permute-start.13 = (bf16[19,80,128]{2,1,0:T(8,128)(2,1)S(1)}, bf16[19,80,128]{2,1,0:T(8,128)(2,1)S(1)}, u32[]{:S(2)}, u32[]{:S(2)}) collective-permute-start(bf16[19,80,128]{2,1,0:T(8,128)(2,1)S(1)} %get-tuple-element.37), channel_id=1, source_target_pairs={{0,14},{2,0},{4,2},{6,4},{8,6},{10,8},{12,10},{14,12},{1,15},{3,1}... | collective-permute-start | bytes 1167368 | tf_op jit(solution)/shard_map/ppermute | solution.py:169
  119.4 26.8 %collective-permute-start.7 = (bf16[19,80,128]{2,1,0:T(8,128)(2,1)S(1)}, bf16[19,80,128]{2,1,0:T(8,128)(2,1)S(1)}, u32[]{:S(2)}, u32[]{:S(2)}) collective-permute-start(bf16[19,80,128]{2,1,0:T(8,128)(2,1)S(1)} %get-tuple-element.31), channel_id=1, source_target_pairs={{0,2},{2,4},{4,6},{6,8},{8,10},{10,12},{12,14},{14,0},{1,3},{3,5},... | collective-permute-start | bytes 1167368 | tf_op jit(solution)/shard_map/ppermute | solution.py:169
  123.8 36.6 %collective-permute-start.8 = (bf16[19,80,128]{2,1,0:T(8,128)(2,1)S(1)}, bf16[19,80,128]{2,1,0:T(8,128)(2,1)S(1)}, u32[]{:S(2)}, u32[]{:S(2)}) collective-permute-start(bf16[19,80,128]{2,1,0:T(8,128)(2,1)S(1)} %get-tuple-element.32), channel_id=1, source_target_pairs={{0,4},{2,6},{4,8},{6,10},{8,12},{10,14},{12,0},{14,2},{1,5},{3,7},... | collective-permute-start | bytes 1167368 | tf_op jit(solution)/shard_map/ppermute | solution.py:169
  134.2 27.0 %collective-permute-start.9 = (bf16[19,80,128]{2,1,0:T(8,128)(2,1)S(1)}, bf16[19,80,128]{2,1,0:T(8,128)(2,1)S(1)}, u32[]{:S(2)}, u32[]{:S(2)}) collective-permute-start(bf16[19,80,128]{2,1,0:T(8,128)(2,1)S(1)} %get-tuple-element.33), channel_id=1, source_target_pairs={{0,6},{2,8},{4,10},{6,12},{8,14},{10,0},{12,2},{14,4},{1,7},{3,9},... | collective-permute-start | bytes 1167368 | tf_op jit(solution)/shard_map/ppermute | solution.py:169
  144.6 0.8 copy-start.10
  145.4 0.7 copy-start.12
  146.1 0.8 copy-start.14
  160.4 0.7 copy-start.16
  161.1 0.8 copy-start.18
  161.9 1.0 copy-start.9
  162.9 1.0 copy-start.11
  163.9 1.0 copy-start.13
  164.9 1.0 copy-start.15
  165.9 1.0 copy-start.17
  166.9 1.0 copy-start.19
  208.1 4.7 %copy-start = (bf16[1280,5120]{1,0:T(8,128)(2,1)S(1)}, bf16[1280,5120]{1,0:T(8,128)(2,1)}, u32[]{:S(2)}) copy-start(bf16[1280,5120]{1,0:T(8,128)(2,1)} %own_weight.1) | copy-start | bytes 39321604
  212.9 2.9 %copy-start.2 = (bf16[1280,2560]{1,0:T(8,128)(2,1)S(1)}, bf16[1280,2560]{1,0:T(8,128)(2,1)}, u32[]{:S(2)}) copy-start(bf16[1280,2560]{1,0:T(8,128)(2,1)} %all-gather.2.cloned.1.call-done.other_weight) | copy-start | bytes 19660804
Sparse Core Ops, SparseCore 0:
  28.8 52.5 all-gather.1

commit v2 on v1

v2 whole, which is shorter than its diff:
```python
import math

import jax
import jax.numpy as jnp
from jax import lax
from jax.experimental import pallas as pl
from jax.experimental.pallas import tpu as pltpu
from jax.sharding import PartitionSpec as P

HD = 128
WIN = 2
SPANS = 4
GROUPS = 8
SPACE = 8
ROWS = 80
SPAN = SPACE * ROWS
HEADS = 10
WIDE = SPACE * HD
PAIRS = 5
LENT_STEPS = (0, 2, 6, 4)
UNITS = 3 * PAIRS + 2 * WIN
VMEM = pl.BlockSpec(memory_space=pltpu.VMEM)
HBM = pl.BlockSpec(memory_space=pltpu.HBM)
SMEM = pl.BlockSpec(memory_space=pltpu.SMEM)
MIB = 1 << 20


def params(mib):
    return pltpu.CompilerParams(vmem_limit_bytes=mib * MIB)


def picked(window, span_slot, block, group):
    place = jnp.int32(0)
    for span in range(SPANS):
        for w in range(WIN):
            slot = span_slot[window[block * SPANS + span, w]]
            place = jnp.where((slot >> 1) == group, slot & 1, place)
    return place


def pack_slots(window, span_slot, cache_keys, cache_values, by_head, *rest):
    me = lax.axis_index("cache")
    for head in range(SPACE):
        for kv, source in enumerate((cache_keys, cache_values)):
            for slot in range(2):
                row = (kv * 2 + slot) * ROWS
                by_head[head, row : row + ROWS] = source[slot, :, head * HD : (head + 1) * HD]
    for step in range(GROUPS):
        slot = picked(window, span_slot, (me + step) & 7, me)
        for kv, source in enumerate((cache_keys, cache_values)):
            rest[step][kv] = source[slot, :, WIDE:]


def pack_all(window, span_slot, by_head, queries, keys, values, *refs):
    rest, wide_out, sent = refs[:GROUPS], refs[GROUPS], refs[GROUPS + 1 : GROUPS + 1 + SPACE]
    held, wide, pairs, wide_sems, pair_sems = refs[GROUPS + 1 + SPACE :]
    group = lax.axis_index("cache")
    me = lax.axis_index("space")
    for block in range(GROUPS):
        slot = picked(window, span_slot, block, group)
        for kv in range(2):
            for space in range(SPACE):
                row = (kv * SPACE + space) * ROWS
                start = pl.multiple_of((kv * 2 + slot) * ROWS, 16)
                wide[block, row : row + ROWS] = by_head[space, pl.ds(start, ROWS)]
        pltpu.make_async_copy(wide.at[block], wide_out.at[block], wide_sems.at[block]).start()
    for step in range(GROUPS):
        held[(group - step) & 7] = rest[step][...]
    for step in range(SPACE):
        to = (me + step) & 7
        span = to >> 1
        wide_part = pl.ds(pl.multiple_of(to * HD, HD), HD)
        last = pl.multiple_of((to & 1) * HD, HD)
        for kind, source in enumerate((queries, keys, values)):
            for pair in range(SPANS):
                pairs[step, 3 * pair + kind] = source[pair, :, wide_part]
            pairs[step, 3 * SPANS + kind] = source[
                span, :, pl.ds(pl.multiple_of(WIDE + last, HD), HD)
            ]
        for w in range(WIN):
            owner = span_slot[window[group * SPANS + span, w]] >> 1
            for kv in range(2):
                pairs[step, 3 * PAIRS + 2 * w + kv] = held[owner, kv, :, pl.ds(last, HD)]
        pltpu.make_async_copy(pairs.at[step], sent[step], pair_sems.at[step]).start()
    for block in range(GROUPS):
        pltpu.make_async_copy(wide.at[block], wide_out.at[block], wide_sems.at[block]).wait()
    for step in range(SPACE):
        pltpu.make_async_copy(pairs.at[step], sent[step], pair_sems.at[step]).wait()


def attend(window, span_slot, counts, *refs):
    came, wide, out, own, sent, k_all, v_all, done, ready, left = (refs[:SPACE],) + refs[SPACE:]
    group = lax.axis_index("cache")
    me = lax.axis_index("space")
    factor = math.log2(math.e) / math.sqrt(HD)
    spots = lax.broadcasted_iota(jnp.int32, (SPAN, HD), 0)
    v_all[0:SPAN, HD:] = jnp.ones((SPAN, HD), jnp.bfloat16)

    def fetch(pair, source, target):
        pltpu.make_async_copy(source, target, ready.at[pair]).start()

    for pair in range(PAIRS):
        for step in range(SPACE):
            rows = pl.ds(step * ROWS, ROWS)
            fetch(pair, came[step].at[pl.ds(3 * pair, 3)], own.at[pair, pl.ds(0, 3), rows])
        if pair < SPANS:
            for w in range(WIN):
                owner = span_slot[window[group * SPANS + pair, w]] >> 1
                fetch(pair, wide.at[owner], own.at[pair, pl.ds(3 + 2 * w, 2)])
        else:
            for step in range(SPACE):
                start = pl.multiple_of(((me - step) & 7) * ROWS, 16)
                fetch(
                    pair,
                    came[step].at[pl.ds(3 * PAIRS, 2 * WIN)],
                    own.at[pair, pl.ds(3, 2 * WIN), pl.ds(start, ROWS)],
                )

    @pl.loop(0, PAIRS)
    def _(pair):
        pltpu.make_async_copy(own.at[pair], own.at[pair], ready.at[pair]).wait()
        span = jnp.where(pair < SPANS, pair, me >> 1)
        k_all[0:SPAN] = own[pair, 1]
        v_all[0:SPAN, 0:HD] = own[pair, 2]
        for w in range(WIN):
            limit = counts[window[group * SPANS + span, w]]
            part = slice((1 + w) * SPAN, (2 + w) * SPAN)
            valid = spots < limit
            held = own[pair, 3 + 2 * w].astype(jnp.float32)
            first = jnp.broadcast_to(held[0:1], (SPAN, HD))
            k_all[part] = jnp.where(valid, held, first).astype(jnp.bfloat16)
            held = own[pair, 4 + 2 * w].astype(jnp.float32)
            v_all[part, 0:HD] = jnp.where(valid, held, 0.0).astype(jnp.bfloat16)
            v_all[part, HD:] = jnp.where(valid, 1.0, 0.0).astype(jnp.bfloat16)
        block = SPAN // 2
        for start in range(0, SPAN, block):
            scores = lax.dot_general(
                own[pair, 0, start : start + block],
                k_all[...],
                (((1,), (1,)), ((), ())),
                preferred_element_type=jnp.float32,
            )
            top = jnp.max(scores, axis=1, keepdims=True)
            weights = jnp.exp2((scores - top) * factor).astype(jnp.bfloat16)
            both = jnp.dot(weights, v_all[...], preferred_element_type=jnp.float32)
            done[start : start + block] = (both[:, 0:HD] / both[:, HD:]).astype(jnp.bfloat16)
        for step in range(SPACE):
            to = (me - step) & 7
            for half in range(2):
                sent[2 * to + half, pair] = done[step * ROWS : (step + 1) * ROWS]
        pltpu.make_async_copy(sent.at[:, pair], out.at[:, pair], left.at[pair]).start()

    for pair in range(PAIRS):
        pltpu.make_async_copy(sent.at[:, pair], out.at[:, pair], left.at[pair]).wait()


def project(came, own_weight, *refs):
    lent, out, features, own, other, mixed, came_sems, weight_sems, out_sems = (
        refs[:GROUPS],
        *refs[GROUPS:],
    )
    group = lax.axis_index("cache")
    half = lax.axis_index("head")
    columns = out.shape[1]
    rows = lent[0].shape[0]
    tiles = weight_sems.shape[0]
    tile = columns // tiles
    for part in range(2):
        source = half if part == 0 else 1 - half
        for space in range(SPACE):
            pltpu.make_async_copy(
                came.at[2 * space + source, pl.ds(0, SPANS * ROWS)],
                features.at[part, :, pl.ds(space * HD, HD)],
                came_sems.at[part],
            ).start()
            pltpu.make_async_copy(
                came.at[2 * space + source, pl.ds(SPANS * ROWS, ROWS)],
                features.at[
                    part, pl.ds(space // 2 * ROWS, ROWS), pl.ds(WIDE + space % 2 * HD, HD)
                ],
                came_sems.at[part],
            ).start()
    for step in range(tiles):
        here = pl.ds(step * tile, tile)
        start = pl.multiple_of(half * columns + step * tile, 128)
        pltpu.make_async_copy(
            own_weight.at[:, pl.ds(start, tile)], own.at[step], weight_sems.at[step, 0]
        ).start()
        for place, chunk in enumerate(lent):
            holder = group ^ (place // 4)
            start = pl.multiple_of(((holder - LENT_STEPS[place % 4]) & 7) * rows, 16)
            pltpu.make_async_copy(
                chunk.at[:, here], other.at[step, pl.ds(start, rows)], weight_sems.at[step, 1]
            ).start()
    for part in range(2):
        pltpu.make_async_copy(features.at[part], features.at[part], came_sems.at[part]).wait()
    for step in range(tiles):
        here = pl.ds(step * tile, tile)
        pltpu.make_async_copy(own.at[step], own.at[step], weight_sems.at[step, 0]).wait()
        total = jnp.dot(features[0], own[step], preferred_element_type=jnp.float32)
        pltpu.make_async_copy(other.at[step], other.at[step], weight_sems.at[step, 1]).wait()
        total += jnp.dot(features[1], other[step], preferred_element_type=jnp.float32)
        mixed[step] = total.astype(jnp.bfloat16)
        pltpu.make_async_copy(mixed.at[step], out.at[:, here], out_sems.at[step]).start()
    for step in range(tiles):
        here = pl.ds(step * tile, tile)
        pltpu.make_async_copy(mixed.at[step], out.at[:, here], out_sems.at[step]).wait()


def shift(x, axis, step):
    return lax.ppermute(x, axis, [(i, (i + step) % 8) for i in range(8)])


def on_device(
    queries, keys, values, cache_keys, cache_values, window, span_slot, counts, out_weight
):
    bf16 = jnp.bfloat16
    shape = jax.ShapeDtypeStruct
    group = lax.axis_index("cache")
    half = lax.axis_index("head")
    depth, width = out_weight.shape
    columns = width // 2

    rows = depth // GROUPS
    lent = lax.dynamic_slice(out_weight, (group * rows, (1 - half) * columns), (rows, columns))
    lent = lax.ppermute(lent, "head", [(0, 1), (1, 0)])

    by_head, *rest = pl.pallas_call(
        pack_slots,
        out_shape=[shape((SPACE, 4 * ROWS, HD), bf16)]
        + [shape((2, ROWS, 2 * HD), bf16)] * GROUPS,
        in_specs=[SMEM] * 2 + [VMEM] * 2,
        out_specs=[VMEM] * (1 + GROUPS),
        compiler_params=params(16),
        name="pack_slots",
    )(window, span_slot, cache_keys, cache_values)
    by_head = lax.all_to_all(by_head, "space", split_axis=0, concat_axis=0, tiled=True)
    rest = [rest[0]] + [shift(rest[step], "cache", step) for step in range(1, GROUPS)]

    lent, by_head, *rest = lax.optimization_barrier((lent, by_head, *rest))

    wide, *pairs = pl.pallas_call(
        pack_all,
        out_shape=[shape((GROUPS, 2 * SPAN, HD), bf16)] + [shape((UNITS, ROWS, HD), bf16)] * SPACE,
        in_specs=[SMEM] * 2 + [VMEM] * (4 + GROUPS),
        out_specs=[HBM] * (1 + SPACE),
        scratch_shapes=[
            pltpu.VMEM((GROUPS, 2, ROWS, 2 * HD), bf16),
            pltpu.VMEM((GROUPS, 2 * SPAN, HD), bf16),
            pltpu.VMEM((SPACE, UNITS, ROWS, HD), bf16),
            pltpu.SemaphoreType.DMA((GROUPS,)),
            pltpu.SemaphoreType.DMA((SPACE,)),
        ],
        compiler_params=params(60),
        name="pack_all",
    )(window, span_slot, by_head, queries, keys, values, *rest)
    wide = lax.all_to_all(wide, "cache", split_axis=0, concat_axis=0, tiled=True)
    came = [pairs[0]] + [shift(pairs[step], "space", step) for step in range(1, SPACE)]
    lent, wide, *came = lax.optimization_barrier((lent, wide, *came))

    lent = [lent] + [shift(lent, "cache", step) for step in LENT_STEPS[1:]]
    lent += [lax.ppermute(chunk, "cache", [(i, i ^ 1) for i in range(8)]) for chunk in lent]

    attended = pl.pallas_call(
        attend,
        out_shape=shape((2 * SPACE, PAIRS, ROWS, HD), bf16),
        in_specs=[SMEM] * 3 + [HBM] * (SPACE + 1),
        out_specs=HBM,
        scratch_shapes=[
            pltpu.VMEM((PAIRS, 3 + 2 * WIN, SPAN, HD), bf16),
            pltpu.VMEM((2 * SPACE, PAIRS, ROWS, HD), bf16),
            pltpu.VMEM((3 * SPAN, HD), bf16),
            pltpu.VMEM((3 * SPAN, 2 * HD), bf16),
            pltpu.VMEM((SPAN, HD), bf16),
            pltpu.SemaphoreType.DMA((PAIRS,)),
            pltpu.SemaphoreType.DMA((PAIRS,)),
        ],
        compiler_params=params(60),
        name="attend",
    )(window, span_slot, counts, *came, wide.reshape(GROUPS, 2, SPAN, HD))
    attended = attended.reshape(2 * SPACE, PAIRS * ROWS, HD)
    attended = lax.all_to_all(
        attended, ("space", "head"), split_axis=0, concat_axis=0, tiled=True
    )

    tile = 512
    tiles = columns // tile
    mixed = pl.pallas_call(
        project,
        out_shape=shape((SPANS * ROWS, columns), bf16),
        in_specs=[HBM] * (2 + GROUPS),
        out_specs=HBM,
        scratch_shapes=[
            pltpu.VMEM((2, SPANS * ROWS, depth), bf16),
            pltpu.VMEM((tiles, depth, tile), bf16),
            pltpu.VMEM((tiles, depth, tile), bf16),
            pltpu.VMEM((tiles, SPANS * ROWS, tile), bf16),
            pltpu.SemaphoreType.DMA((2,)),
            pltpu.SemaphoreType.DMA((tiles, 2)),
            pltpu.SemaphoreType.DMA((tiles,)),
        ],
        compiler_params=params(60),
        name="project",
    )(attended, out_weight, *lent)
    return mixed.reshape(SPANS, ROWS, columns)


def solution(mesh):
    in_specs = (
        P("cache", "space", "head"),
        P("cache", "space", "head"),
        P("cache", "space", "head"),
        P("cache", "space", "head"),
        P("cache", "space", "head"),
        P(),
        P(),
        P(),
        P("head", None),
    )
    out_specs = P("cache", "space", "head")
    return jax.shard_map(
        on_device, mesh=mesh, in_specs=in_specs, out_specs=out_specs, check_vma=False
    )
```

time: 230 us -> 150 us (0.65)
  blocking collectives: 49.3 us -> 0 us
  local copies, waits for them, and re-layouts: 29.9 us -> 7.94 us
  between operations: 13.5 us -> 0.4 us
  starting transfers between devices: 49.3 us -> 37.1 us
  Pallas kernels: 21.6 us -> 31.2 us
  waiting for transfers between devices: 66 us -> 72.6 us
    all_to_all x2 -> x0, blocking collectives: 49.3 us -> none  [the longest x1 29.1 us: on_device(): lax.all_to_all(attended, ('space', 'head'), split_axis=0, concat_axis=0,...]
    ppermute x14 -> x17, starting transfers between devices: 43.1 us -> 19.6 us  [shift(): return lax.ppermute(x, axis, [(i, (i + step) % 8) for i in range(8)])]
    unnamed x63 -> x47, local copies, waits for them, and re-layouts: 28.6 us -> 6.75 us
    ppermute x1, waiting for transfers between devices: 18.2 us -> 0.01 us  [on_device(): lent = lax.ppermute(lent, 'head', [(0, 1), (1, 0)])]
    ppermute x14 -> x17, waiting for transfers between devices: 47.8 us -> 63.8 us  [shift(): return lax.ppermute(x, axis, [(i, (i + step) % 8) for i in range(8)])]
    all_to_all x0 -> x2, starting transfers between devices: none -> 11.4 us  [the longest x1 7.65 us: on_device(): lax.all_to_all(by_head, 'space', split_axis=0, concat_axis=0, tiled=True)]
    all_to_all x0 -> x2, waiting for transfers between devices: none -> 8.82 us  [the longest x1 5.22 us: on_device(): lax.all_to_all(by_head, 'space', split_axis=0, concat_axis=0, tiled=True)]
    pallas_call x3 -> x2, Pallas kernels: 9.45 us -> 16.5 us  [the longest x1 11.8 us: on_device(): pl.pallas_call(project, out_shape=shape((SPANS * ROWS, columns), bf16), i...]
  transfers between devices with their start and end apart: 17 -> 25, of which waited for: 7 -> 12; matrix products, arithmetic and copies ran while one was open for 0% -> 1% of each run, Pallas kernels for 6% -> 10%
where the time goes in v2:
time: 150 us; the launch traced here: 149 us
  waiting for transfers between devices  72.6 us (48%)
  starting transfers between devices  37.1 us (25%)
  Pallas kernels  31.2 us (21%)
  local copies, waits for them, and re-layouts  7.94 us (5%)
    ppermute x17, waiting for transfers between devices, shift(): return lax.ppermute(x, axis, [(i, (i + step) % 8) for i in range(8)])  63.8 us
    ppermute x17, starting transfers between devices, shift(): return lax.ppermute(x, axis, [(i, (i + step) % 8) for i in range(8)])  19.6 us
    pallas_call x1, Pallas kernels, on_device(): pl.pallas_call(attend, out_shape=shape((2 * SPACE, PAIRS, ROWS, HD), bf16...  12.8 us
    pallas_call x1, Pallas kernels, on_device(): pl.pallas_call(project, out_shape=shape((SPANS * ROWS, columns), bf16), i...  11.8 us
    all_to_all x1, starting transfers between devices, on_device(): lax.all_to_all(by_head, 'space', split_axis=0, concat_axis=0, tiled=True)  7.65 us
    unnamed x47, local copies, waits for them, and re-layouts  6.75 us
    all_to_all x1, waiting for transfers between devices, on_device(): lax.all_to_all(by_head, 'space', split_axis=0, concat_axis=0, tiled=True)  5.22 us
    pallas_call x1, Pallas kernels, on_device(): pl.pallas_call(pack_all, out_shape=[shape((GROUPS, 2 * SPAN, HD), bf16)]...  4.71 us
  transfers between devices with their start and end apart: 25, of which 12 were waited for; matrix products, arithmetic and copies ran while one was open for 1% of the time, Pallas kernels for 10%

profile of v2, /device:TPU:0, one launch (start us, length us, event | category | flops | bytes accessed | tf_op | source)
XLA Modules:
  0.0 149.3 jit_solution(17889264279775450490)
XLA Ops:
  0.0 1.2 dynamic_slice.3
  1.2 1.7 %collective-permute-start = (bf16[160,2560]{1,0:T(8,128)(2,1)S(1)}, bf16[160,2560]{1,0:T(8,128)(2,1)S(1)}, u32[]{:S(2)}, u32[]{:S(2)}) collective-permute-start(bf16[160,2560]{1,0:T(8,128)(2,1)S(1)} %dynamic_slice.3), channel_id=1, source_target_pairs={{0,1},{1,0},{2,3},{3,2},{4,5},{5,4},{6,7},{7,6},{8,9},{9,8},{10,11... | collective-permute-start | bytes 2457608 | tf_op jit(solution)/shard_map/ppermute | solution.py:226
  2.9 0.8 copy.12.window
  3.7 1.0 copy-done
  4.7 1.0 copy-done.1
  5.7 0.7 copy-done.4
  6.4 1.9 %pack_slots.1 = (bf16[8,320,128]{2,1,0:T(8,128)(2,1)}, bf16[2,80,256]{2,1,0:T(8,128)(2,1)S(1)}, bf16[2,80,256]{2,1,0:T(8,128)(2,1)S(1)}, bf16[2,80,256]{2,1,0:T(...) custom-call(s32[32,2]{1,0:T(8,128)S(1)} %copy.12.window, ...), custom_call_target="tpu_custom_call" | custom-call | tf_op jit(solution)/shard_map/pack_slots/pallas_call | solution.py:228
  8.3 0.6 copy-done.3
  8.9 7.7 %all-to-all-start = ((bf16[8,320,128]{2,1,0:T(8,128)(2,1)}), bf16[8,320,128]{2,1,0:T(8,128)(2,1)S(1)}, u32[]{:S(2)}, u32[]{:S(2)}) async-start(bf16[8,320,128]{2,1,0:T(8,128)(2,1)} %get-tuple-element.43), calls=%async_computation | async-start | bytes 1310720 | tf_op jit(solution)/shard_map/all_to_all | solution.py:237
  16.5 0.0 collective-permute-start.1
  16.5 1.6 %collective-permute-start.2 = (bf16[2,80,256]{2,1,0:T(8,128)(2,1)S(1)}, bf16[2,80,256]{2,1,0:T(8,128)(2,1)S(1)}, u32[]{:S(2)}, u32[]{:S(2)}) collective-permute-start(bf16[2,80,256]{2,1,0:T(8,128)(2,1)S(1)} %get-tuple-element.46), channel_id=1, source_target_pairs={{0,32},{16,48},{32,64},{48,80},{64,96},{80,112},{96,0},{112,16},{1... | collective-permute-start | bytes 245768 | tf_op jit(solution)/shard_map/ppermute | solution.py:211
  18.1 2.1 %collective-permute-start.3 = (bf16[2,80,256]{2,1,0:T(8,128)(2,1)S(1)}, bf16[2,80,256]{2,1,0:T(8,128)(2,1)S(1)}, u32[]{:S(2)}, u32[]{:S(2)}) collective-permute-start(bf16[2,80,256]{2,1,0:T(8,128)(2,1)S(1)} %get-tuple-element.47), channel_id=1, source_target_pairs={{0,48},{16,64},{32,80},{48,96},{64,112},{80,0},{96,16},{112,32},{1... | collective-permute-start | bytes 245768 | tf_op jit(solution)/shard_map/ppermute | solution.py:211
  20.1 2.0 %collective-permute-start.4 = (bf16[2,80,256]{2,1,0:T(8,128)(2,1)S(1)}, bf16[2,80,256]{2,1,0:T(8,128)(2,1)S(1)}, u32[]{:S(2)}, u32[]{:S(2)}) collective-permute-start(bf16[2,80,256]{2,1,0:T(8,128)(2,1)S(1)} %get-tuple-element.48), channel_id=1, source_target_pairs={{0,64},{16,80},{32,96},{48,112},{64,0},{80,16},{96,32},{112,48},{1... | collective-permute-start | bytes 245768 | tf_op jit(solution)/shard_map/ppermute | solution.py:211
  22.2 0.0 collective-permute-done.1.refs_1_
  22.2 1.6 %collective-permute-start.5 = (bf16[2,80,256]{2,1,0:T(8,128)(2,1)S(1)}, bf16[2,80,256]{2,1,0:T(8,128)(2,1)S(1)}, u32[]{:S(2)}, u32[]{:S(2)}) collective-permute-start(bf16[2,80,256]{2,1,0:T(8,128)(2,1)S(1)} %get-tuple-element.49), channel_id=1, source_target_pairs={{0,80},{16,96},{32,112},{48,0},{64,16},{80,32},{96,48},{112,64},{1... | collective-permute-start | bytes 245768 | tf_op jit(solution)/shard_map/ppermute | solution.py:211
  23.8 0.0 collective-permute-done.2.refs_2_
  23.8 1.4 collective-permute-start.6
  25.2 1.1 collective-permute-done.3.refs_3_
  26.4 1.2 collective-permute-done.4.refs_4_
  27.6 1.5 collective-permute-done.6.refs_6_
  29.1 5.2 %all-to-all-done.by_head = bf16[8,320,128]{2,1,0:T(8,128)(2,1)S(1)} async-done(((bf16[8,320,128]{2,1,0:T(8,128)(2,1)}), bf16[8,320,128]{2,1,0:T(8,128)(2,1)S(1)}, u32[]{:S(2)}, u32[]{:S(2)}) %all-to-all-start) | async-done | bytes 655392 | tf_op jit(solution)/shard_map/all_to_all | solution.py:237
  34.3 0.0 collective-permute-done.refs_0_
  34.4 0.8 copy-done.7
  35.1 4.7 %pack_all.1 = (bf16[8,1280,128]{2,1,0:T(8,128)(2,1)}, bf16[19,80,128]{2,1,0:T(8,128)(2,1)}, bf16[19,80,128]{2,1,0:T(8,128)(2,1)}, bf16[19,80,128]{2,1,0:T(8,128)...) custom-call(s32[32,2]{1,0:T(8,128)} %copy-done.2, ...), custom_call_target="tpu_custom_call" | custom-call | tf_op jit(solution)/shard_map/pack_all/pallas_call | solution.py:242
  39.9 4.3 %all-to-all-start.1 = ((bf16[8,1280,128]{2,1,0:T(8,128)(2,1)}), bf16[8,1280,128]{2,1,0:T(8,128)(2,1)S(1)}, u32[]{:S(2)}, u32[]{:S(2)}) async-start(bf16[8,1280,128]{2,1,0:T(8,128)(2,1)} %get-tuple-element.62), calls=%async_computation.1 | async-start | bytes 5242880 | tf_op jit(solution)/shard_map/all_to_all | solution.py:257
  44.2 0.6 collective-permute-start.9
  44.8 3.6 %collective-permute-start.10 = (bf16[19,80,128]{2,1,0:T(8,128)(2,1)}, bf16[19,80,128]{2,1,0:T(8,128)(2,1)S(1)}, u32[]{:S(2)}, u32[]{:S(2)}) collective-permute-start(bf16[19,80,128]{2,1,0:T(8,128)(2,1)} %get-tuple-element.66), channel_id=1, source_target_pairs={{0,6},{2,8},{4,10},{6,12},{8,14},{10,0},{12,2},{14,4},{1,7},{3,9},... | collective-permute-start | bytes 1167368 | tf_op jit(solution)/shard_map/ppermute | solution.py:211
  48.4 2.9 %collective-permute-start.11 = (bf16[19,80,128]{2,1,0:T(8,128)(2,1)}, bf16[19,80,128]{2,1,0:T(8,128)(2,1)S(1)}, u32[]{:S(2)}, u32[]{:S(2)}) collective-permute-start(bf16[19,80,128]{2,1,0:T(8,128)(2,1)} %get-tuple-element.67), channel_id=1, source_target_pairs={{0,8},{2,10},{4,12},{6,14},{8,0},{10,2},{12,4},{14,6},{1,9},{3,11}... | collective-permute-start | bytes 1167368 | tf_op jit(solution)/shard_map/ppermute | solution.py:211
  51.3 1.5 collective-permute-start.12
  52.8 8.2 %collective-permute-done.8.refs_1_ = bf16[19,80,128]{2,1,0:T(8,128)(2,1)S(1)} collective-permute-done((bf16[19,80,128]{2,1,0:T(8,128)(2,1)}, bf16[19,80,128]{2,1,0:T(8,128)(2,1)S(1)}, u32[]{:S(2)}, u32[]{:S(2)}) %collective-permute-start.8) | collective-permute-done | bytes 389152 | tf_op jit(solution)/shard_map/ppermute | solution.py:211
  61.0 0.0 collective-permute-start.13
  61.0 21.0 %collective-permute-done.9.refs_2_ = bf16[19,80,128]{2,1,0:T(8,128)(2,1)S(1)} collective-permute-done((bf16[19,80,128]{2,1,0:T(8,128)(2,1)}, bf16[19,80,128]{2,1,0:T(8,128)(2,1)S(1)}, u32[]{:S(2)}, u32[]{:S(2)}) %collective-permute-start.9) | collective-permute-done | bytes 389152 | tf_op jit(solution)/shard_map/ppermute | solution.py:211
  82.1 3.3 %collective-permute-done.13.refs_6_ = bf16[19,80,128]{2,1,0:T(8,128)(2,1)S(1)} collective-permute-done((bf16[19,80,128]{2,1,0:T(8,128)(2,1)}, bf16[19,80,128]{2,1,0:T(8,128)(2,1)S(1)}, u32[]{:S(2)}, u32[]{:S(2)}) %collective-permute-start.13) | collective-permute-done | bytes 389152 | tf_op jit(solution)/shard_map/ppermute | solution.py:211
  85.4 0.7 copy-done.15
  86.2 8.3 %collective-permute-done.14.refs_7_ = bf16[19,80,128]{2,1,0:T(8,128)(2,1)} collective-permute-done((bf16[19,80,128]{2,1,0:T(8,128)(2,1)}, bf16[19,80,128]{2,1,0:T(8,128)(2,1)}, u32[]{:S(2)}, u32[]{:S(2)}) %collective-permute-start.14) | collective-permute-done | bytes 389152 | tf_op jit(solution)/shard_map/ppermute | solution.py:211
  94.5 0.3 collective-permute-start.17
  94.8 1.2 collective-permute-start.16
  95.9 0.9 collective-permute-start.15
  96.8 12.8 %attend.1 = bf16[16,5,80,128]{3,2,1,0:T(8,128)(2,1)} custom-call(s32[32,2]{1,0:T(8,128)} %copy-done.2, s32[16]{0:T(128)} %span_slot.5, s32[16]{0:T(128)} %counts.1, bf16[19,80,128]{2,1,0:T(8,128)(2,1)} %get-tuple-element.71.refs_0_, bf16[19,80,128]{2,1,0:T(8,128)(2,1)} %copy-done.10, bf16[19,80,128]{2,1,0:T(8,128)(2,1)} %copy-done.11, ...), custom_call_target="tpu_custom_call" | custom-call | tf_op jit(solution)/shard_map/attend/pallas_call | solution.py:264
  109.7 3.7 %all-to-all-start.2 = ((bf16[16,400,128]{2,1,0:T(8,128)(2,1)}), bf16[16,400,128]{2,1,0:T(8,128)(2,1)S(1)}, u32[]{:S(2)}, u32[]{:S(2)}) async-start(bf16[16,400,128]{2,1,0:T(8,128)(2,1)} %bitcast.4), calls=%async_computation.2 | async-start | bytes 3276800 | tf_op jit(solution)/shard_map/all_to_all | solution.py:282
  113.4 0.1 collective-permute-start.18
  113.5 3.8 %collective-permute-done.17.refs_3_ = bf16[160,2560]{1,0:T(8,128)(2,1)} collective-permute-done((bf16[160,2560]{1,0:T(8,128)(2,1)S(1)}, bf16[160,2560]{1,0:T(8,128)(2,1)}, u32[]{:S(2)}, u32[]{:S(2)}) %collective-permute-start.17) | collective-permute-done | bytes 819232 | tf_op jit(solution)/shard_map/ppermute | solution.py:211
  117.3 7.5 %collective-permute-done.16.refs_2_ = bf16[160,2560]{1,0:T(8,128)(2,1)} collective-permute-done((bf16[160,2560]{1,0:T(8,128)(2,1)S(1)}, bf16[160,2560]{1,0:T(8,128)(2,1)}, u32[]{:S(2)}, u32[]{:S(2)}) %collective-permute-start.16) | collective-permute-done | bytes 819232 | tf_op jit(solution)/shard_map/ppermute | solution.py:211
  124.8 7.7 %collective-permute-done.15.refs_1_ = bf16[160,2560]{1,0:T(8,128)(2,1)} collective-permute-done((bf16[160,2560]{1,0:T(8,128)(2,1)S(1)}, bf16[160,2560]{1,0:T(8,128)(2,1)}, u32[]{:S(2)}, u32[]{:S(2)}) %collective-permute-start.15) | collective-permute-done | bytes 819232 | tf_op jit(solution)/shard_map/ppermute | solution.py:211
  132.6 0.0 collective-permute-start.19
  132.6 3.6 %all-to-all-done.2.came = bf16[16,400,128]{2,1,0:T(8,128)(2,1)S(1)} async-done(((bf16[16,400,128]{2,1,0:T(8,128)(2,1)}), bf16[16,400,128]{2,1,0:T(8,128)(2,1)S(1)}, u32[]{:S(2)}, u32[]{:S(2)}) %all-to-all-start.2) | async-done | bytes 1638432 | tf_op jit(solution)/shard_map/all_to_all | solution.py:282
  136.2 1.2 copy-done.6
  137.4 11.8 %project.1 = bf16[320,2560]{1,0:T(8,128)(2,1)} custom-call(bf16[16,400,128]{2,1,0:T(8,128)(2,1)} %copy-done.6, bf16[1280,5120]{1,0:T(8,128)(2,1)} %own_weight.1, bf16[160,2560]{1,0:T(8,128)(2,1)} %copy-done.8, bf16[160,2560]{1,0:T(8,128)(2,1)} %collective-permute-done.15.refs_1_, bf16[160,2560]{1,0:T(8,128)(2,1)} %collective-permute-done.16.refs_2_, ...), custom_call_target="tpu_custom_call" | custom-call | tf_op jit(solution)/shard_map/project/pallas_call | solution.py:288
  (54 shorter events, 0.1 us)
Async XLA Ops:
  1.2 33.1 %collective-permute-start = (bf16[160,2560]{1,0:T(8,128)(2,1)S(1)}, bf16[160,2560]{1,0:T(8,128)(2,1)S(1)}, u32[]{:S(2)}, u32[]{:S(2)}) collective-permute-start(bf16[160,2560]{1,0:T(8,128)(2,1)S(1)} %dynamic_slice.3), channel_id=1, source_target_pairs={{0,1},{1,0},{2,3},{3,2},{4,5},{5,4},{6,7},{7,6},{8,9},{9,8},{10,11... | collective-permute-start | bytes 2457608 | tf_op jit(solution)/shard_map/ppermute | solution.py:226
  3.7 1.0 copy-start
  4.7 1.0 copy-start.1
  5.7 0.7 copy-start.4
  6.4 27.9 %copy-start.2 = (s32[32,2]{1,0:T(8,128)}, s32[32,2]{1,0:T(8,128)S(1)}, u32[]{:S(2)}) copy-start(s32[32,2]{1,0:T(8,128)S(1)} %copy.12.window) | copy-start | bytes 772
  8.3 0.6 copy-start.3
  8.9 25.4 %all-to-all-start = ((bf16[8,320,128]{2,1,0:T(8,128)(2,1)}), bf16[8,320,128]{2,1,0:T(8,128)(2,1)S(1)}, u32[]{:S(2)}, u32[]{:S(2)}) async-start(bf16[8,320,128]{2,1,0:T(8,128)(2,1)} %get-tuple-element.43), calls=%async_computation | async-start | bytes 1310720 | tf_op jit(solution)/shard_map/all_to_all | solution.py:237
  16.5 5.6 %collective-permute-start.1 = (bf16[2,80,256]{2,1,0:T(8,128)(2,1)S(1)}, bf16[2,80,256]{2,1,0:T(8,128)(2,1)S(1)}, u32[]{:S(2)}, u32[]{:S(2)}) collective-permute-start(bf16[2,80,256]{2,1,0:T(8,128)(2,1)S(1)} %get-tuple-element.45), channel_id=1, source_target_pairs={{0,16},{16,32},{32,48},{48,64},{64,80},{80,96},{96,112},{112,0},{1... | collective-permute-start | bytes 245768 | tf_op jit(solution)/shard_map/ppermute | solution.py:211
  16.5 7.3 %collective-permute-start.2 = (bf16[2,80,256]{2,1,0:T(8,128)(2,1)S(1)}, bf16[2,80,256]{2,1,0:T(8,128)(2,1)S(1)}, u32[]{:S(2)}, u32[]{:S(2)}) collective-permute-start(bf16[2,80,256]{2,1,0:T(8,128)(2,1)S(1)} %get-tuple-element.46), channel_id=1, source_target_pairs={{0,32},{16,48},{32,64},{48,80},{64,96},{80,112},{96,0},{112,16},{1... | collective-permute-start | bytes 245768 | tf_op jit(solution)/shard_map/ppermute | solution.py:211
  18.1 8.3 %collective-permute-start.3 = (bf16[2,80,256]{2,1,0:T(8,128)(2,1)S(1)}, bf16[2,80,256]{2,1,0:T(8,128)(2,1)S(1)}, u32[]{:S(2)}, u32[]{:S(2)}) collective-permute-start(bf16[2,80,256]{2,1,0:T(8,128)(2,1)S(1)} %get-tuple-element.47), channel_id=1, source_target_pairs={{0,48},{16,64},{32,80},{48,96},{64,112},{80,0},{96,16},{112,32},{1... | collective-permute-start | bytes 245768 | tf_op jit(solution)/shard_map/ppermute | solution.py:211
  20.1 7.4 %collective-permute-start.4 = (bf16[2,80,256]{2,1,0:T(8,128)(2,1)S(1)}, bf16[2,80,256]{2,1,0:T(8,128)(2,1)S(1)}, u32[]{:S(2)}, u32[]{:S(2)}) collective-permute-start(bf16[2,80,256]{2,1,0:T(8,128)(2,1)S(1)} %get-tuple-element.48), channel_id=1, source_target_pairs={{0,64},{16,80},{32,96},{48,112},{64,0},{80,16},{96,32},{112,48},{1... | collective-permute-start | bytes 245768 | tf_op jit(solution)/shard_map/ppermute | solution.py:211
  22.2 12.2 %copy-start.16 = (bf16[2,80,256]{2,1,0:T(8,128)(2,1)}, bf16[2,80,256]{2,1,0:T(8,128)(2,1)S(1)}, u32[]{:S(2)}) copy-start(bf16[2,80,256]{2,1,0:T(8,128)(2,1)S(1)} %collective-permute-done.1.refs_1_) | copy-start | bytes 245764
  22.2 5.4 %collective-permute-start.5 = (bf16[2,80,256]{2,1,0:T(8,128)(2,1)S(1)}, bf16[2,80,256]{2,1,0:T(8,128)(2,1)S(1)}, u32[]{:S(2)}, u32[]{:S(2)}) collective-permute-start(bf16[2,80,256]{2,1,0:T(8,128)(2,1)S(1)} %get-tuple-element.49), channel_id=1, source_target_pairs={{0,80},{16,96},{32,112},{48,0},{64,16},{80,32},{96,48},{112,64},{1... | collective-permute-start | bytes 245768 | tf_op jit(solution)/shard_map/ppermute | solution.py:211
  23.8 10.5 %copy-start.17 = (bf16[2,80,256]{2,1,0:T(8,128)(2,1)}, bf16[2,80,256]{2,1,0:T(8,128)(2,1)S(1)}, u32[]{:S(2)}) copy-start(bf16[2,80,256]{2,1,0:T(8,128)(2,1)S(1)} %collective-permute-done.2.refs_2_) | copy-start | bytes 245764
  23.8 5.3 %collective-permute-start.6 = (bf16[2,80,256]{2,1,0:T(8,128)(2,1)S(1)}, bf16[2,80,256]{2,1,0:T(8,128)(2,1)S(1)}, u32[]{:S(2)}, u32[]{:S(2)}) collective-permute-start(bf16[2,80,256]{2,1,0:T(8,128)(2,1)S(1)} %get-tuple-element.50), channel_id=1, source_target_pairs={{0,96},{16,112},{32,0},{48,16},{64,32},{80,48},{96,64},{112,80},{1... | collective-permute-start | bytes 245768 | tf_op jit(solution)/shard_map/ppermute | solution.py:211
  26.4 8.0 %copy-start.18 = (bf16[2,80,256]{2,1,0:T(8,128)(2,1)}, bf16[2,80,256]{2,1,0:T(8,128)(2,1)S(1)}, u32[]{:S(2)}) copy-start(bf16[2,80,256]{2,1,0:T(8,128)(2,1)S(1)} %collective-permute-done.3.refs_3_) | copy-start | bytes 245764
  26.4 2.7 %collective-permute-start.7 = (bf16[2,80,256]{2,1,0:T(8,128)(2,1)S(1)}, bf16[2,80,256]{2,1,0:T(8,128)(2,1)S(1)}, u32[]{:S(2)}, u32[]{:S(2)}) collective-permute-start(bf16[2,80,256]{2,1,0:T(8,128)(2,1)S(1)} %get-tuple-element.51), channel_id=1, source_target_pairs={{0,112},{16,0},{32,16},{48,32},{64,48},{80,64},{96,80},{112,96},{1... | collective-permute-start | bytes 245768 | tf_op jit(solution)/shard_map/ppermute | solution.py:211
  27.6 6.8 %copy-start.19 = (bf16[2,80,256]{2,1,0:T(8,128)(2,1)}, bf16[2,80,256]{2,1,0:T(8,128)(2,1)S(1)}, u32[]{:S(2)}) copy-start(bf16[2,80,256]{2,1,0:T(8,128)(2,1)S(1)} %collective-permute-done.4.refs_4_) | copy-start | bytes 245764
  27.6 6.8 %copy-start.20 = (bf16[2,80,256]{2,1,0:T(8,128)(2,1)}, bf16[2,80,256]{2,1,0:T(8,128)(2,1)S(1)}, u32[]{:S(2)}) copy-start(bf16[2,80,256]{2,1,0:T(8,128)(2,1)S(1)} %collective-permute-done.5.refs_5_) | copy-start | bytes 245764
  29.1 5.3 %copy-start.21 = (bf16[2,80,256]{2,1,0:T(8,128)(2,1)}, bf16[2,80,256]{2,1,0:T(8,128)(2,1)S(1)}, u32[]{:S(2)}) copy-start(bf16[2,80,256]{2,1,0:T(8,128)(2,1)S(1)} %collective-permute-done.6.refs_6_) | copy-start | bytes 245764
  29.1 5.3 %copy-start.22 = (bf16[2,80,256]{2,1,0:T(8,128)(2,1)}, bf16[2,80,256]{2,1,0:T(8,128)(2,1)S(1)}, u32[]{:S(2)}) copy-start(bf16[2,80,256]{2,1,0:T(8,128)(2,1)S(1)} %collective-permute-done.7.refs_7_) | copy-start | bytes 245764
  34.3 0.8 copy-start.7
  34.3 79.1 %copy-start.8 = (bf16[160,2560]{1,0:T(8,128)(2,1)}, bf16[160,2560]{1,0:T(8,128)(2,1)S(1)}, u32[]{:S(2)}) copy-start(bf16[160,2560]{1,0:T(8,128)(2,1)S(1)} %collective-permute-done.refs_0_) | copy-start | bytes 2457604
  39.9 54.6 %all-to-all-start.1 = ((bf16[8,1280,128]{2,1,0:T(8,128)(2,1)}), bf16[8,1280,128]{2,1,0:T(8,128)(2,1)S(1)}, u32[]{:S(2)}, u32[]{:S(2)}) async-start(bf16[8,1280,128]{2,1,0:T(8,128)(2,1)} %get-tuple-element.62), calls=%async_computation.1 | async-start | bytes 5242880 | tf_op jit(solution)/shard_map/all_to_all | solution.py:257
  44.2 16.8 %collective-permute-start.8 = (bf16[19,80,128]{2,1,0:T(8,128)(2,1)}, bf16[19,80,128]{2,1,0:T(8,128)(2,1)S(1)}, u32[]{:S(2)}, u32[]{:S(2)}) collective-permute-start(bf16[19,80,128]{2,1,0:T(8,128)(2,1)} %get-tuple-element.64), channel_id=1, source_target_pairs={{0,2},{2,4},{4,6},{6,8},{8,10},{10,12},{12,14},{14,0},{1,3},{3,5},... | collective-permute-start | bytes 1167368 | tf_op jit(solution)/shard_map/ppermute | solution.py:211
  44.2 37.9 %collective-permute-start.9 = (bf16[19,80,128]{2,1,0:T(8,128)(2,1)}, bf16[19,80,128]{2,1,0:T(8,128)(2,1)S(1)}, u32[]{:S(2)}, u32[]{:S(2)}) collective-permute-start(bf16[19,80,128]{2,1,0:T(8,128)(2,1)} %get-tuple-element.65), channel_id=1, source_target_pairs={{0,4},{2,6},{4,8},{6,10},{8,12},{10,14},{12,0},{14,2},{1,5},{3,7},... | collective-permute-start | bytes 1167368 | tf_op jit(solution)/shard_map/ppermute | solution.py:211
  44.8 37.3 %collective-permute-start.10 = (bf16[19,80,128]{2,1,0:T(8,128)(2,1)}, bf16[19,80,128]{2,1,0:T(8,128)(2,1)S(1)}, u32[]{:S(2)}, u32[]{:S(2)}) collective-permute-start(bf16[19,80,128]{2,1,0:T(8,128)(2,1)} %get-tuple-element.66), channel_id=1, source_target_pairs={{0,6},{2,8},{4,10},{6,12},{8,14},{10,0},{12,2},{14,4},{1,7},{3,9},... | collective-permute-start | bytes 1167368 | tf_op jit(solution)/shard_map/ppermute | solution.py:211
  48.4 33.7 %collective-permute-start.11 = (bf16[19,80,128]{2,1,0:T(8,128)(2,1)}, bf16[19,80,128]{2,1,0:T(8,128)(2,1)S(1)}, u32[]{:S(2)}, u32[]{:S(2)}) collective-permute-start(bf16[19,80,128]{2,1,0:T(8,128)(2,1)} %get-tuple-element.67), channel_id=1, source_target_pairs={{0,8},{2,10},{4,12},{6,14},{8,0},{10,2},{12,4},{14,6},{1,9},{3,11}... | collective-permute-start | bytes 1167368 | tf_op jit(solution)/shard_map/ppermute | solution.py:211
  51.3 30.8 %collective-permute-start.12 = (bf16[19,80,128]{2,1,0:T(8,128)(2,1)}, bf16[19,80,128]{2,1,0:T(8,128)(2,1)S(1)}, u32[]{:S(2)}, u32[]{:S(2)}) collective-permute-start(bf16[19,80,128]{2,1,0:T(8,128)(2,1)} %get-tuple-element.68), channel_id=1, source_target_pairs={{0,10},{2,12},{4,14},{6,0},{8,2},{10,4},{12,6},{14,8},{1,11},{3,13... | collective-permute-start | bytes 1167368 | tf_op jit(solution)/shard_map/ppermute | solution.py:211
  61.0 24.4 %copy-start.10 = (bf16[19,80,128]{2,1,0:T(8,128)(2,1)}, bf16[19,80,128]{2,1,0:T(8,128)(2,1)S(1)}, u32[]{:S(2)}) copy-start(bf16[19,80,128]{2,1,0:T(8,128)(2,1)S(1)} %collective-permute-done.8.refs_1_) | copy-start | bytes 1167364
  61.0 24.4 %collective-permute-start.13 = (bf16[19,80,128]{2,1,0:T(8,128)(2,1)}, bf16[19,80,128]{2,1,0:T(8,128)(2,1)S(1)}, u32[]{:S(2)}, u32[]{:S(2)}) collective-permute-start(bf16[19,80,128]{2,1,0:T(8,128)(2,1)} %get-tuple-element.69), channel_id=1, source_target_pairs={{0,12},{2,14},{4,0},{6,2},{8,4},{10,6},{12,8},{14,10},{1,13},{3,15... | collective-permute-start | bytes 1167368 | tf_op jit(solution)/shard_map/ppermute | solution.py:211
  82.1 3.3 %copy-start.11 = (bf16[19,80,128]{2,1,0:T(8,128)(2,1)}, bf16[19,80,128]{2,1,0:T(8,128)(2,1)S(1)}, u32[]{:S(2)}) copy-start(bf16[19,80,128]{2,1,0:T(8,128)(2,1)S(1)} %collective-permute-done.9.refs_2_) | copy-start | bytes 1167364
  82.1 12.4 %collective-permute-start.14 = (bf16[19,80,128]{2,1,0:T(8,128)(2,1)}, bf16[19,80,128]{2,1,0:T(8,128)(2,1)}, u32[]{:S(2)}, u32[]{:S(2)}) collective-permute-start(bf16[19,80,128]{2,1,0:T(8,128)(2,1)} %get-tuple-element.70), channel_id=1, source_target_pairs={{0,14},{2,0},{4,2},{6,4},{8,6},{10,8},{12,10},{14,12},{1,15},{3,1}... | collective-permute-start | bytes 1167368 | tf_op jit(solution)/shard_map/ppermute | solution.py:211
  82.1 3.3 %copy-start.12 = (bf16[19,80,128]{2,1,0:T(8,128)(2,1)}, bf16[19,80,128]{2,1,0:T(8,128)(2,1)S(1)}, u32[]{:S(2)}) copy-start(bf16[19,80,128]{2,1,0:T(8,128)(2,1)S(1)} %collective-permute-done.10.refs_3_) | copy-start | bytes 1167364
  82.1 3.3 %copy-start.13 = (bf16[19,80,128]{2,1,0:T(8,128)(2,1)}, bf16[19,80,128]{2,1,0:T(8,128)(2,1)S(1)}, u32[]{:S(2)}) copy-start(bf16[19,80,128]{2,1,0:T(8,128)(2,1)S(1)} %collective-permute-done.11.refs_4_) | copy-start | bytes 1167364
  82.1 3.3 %copy-start.14 = (bf16[19,80,128]{2,1,0:T(8,128)(2,1)}, bf16[19,80,128]{2,1,0:T(8,128)(2,1)S(1)}, u32[]{:S(2)}) copy-start(bf16[19,80,128]{2,1,0:T(8,128)(2,1)S(1)} %collective-permute-done.12.refs_5_) | copy-start | bytes 1167364
  85.4 0.7 copy-start.15
  94.5 2.3 %copy-start.5 = (bf16[8,1280,128]{2,1,0:T(8,128)(2,1)}, bf16[8,1280,128]{2,1,0:T(8,128)(2,1)S(1)}, u32[]{:S(2)}) copy-start(bf16[8,1280,128]{2,1,0:T(8,128)(2,1)S(1)} %all-to-all-done.1) | copy-start | bytes 7864324
  94.5 22.8 %collective-permute-start.17 = (bf16[160,2560]{1,0:T(8,128)(2,1)S(1)}, bf16[160,2560]{1,0:T(8,128)(2,1)}, u32[]{:S(2)}, u32[]{:S(2)}) collective-permute-start(bf16[160,2560]{1,0:T(8,128)(2,1)S(1)} %collective-permute-done.refs_0_), channel_id=1, source_target_pairs={{0,64},{16,80},{32,96},{48,112},{64,0},{80,16},{96,32},{112,48},{1... | collective-permute-start | bytes 2457608 | tf_op jit(solution)/shard_map/ppermute | solution.py:211
  94.8 30.0 %collective-permute-start.16 = (bf16[160,2560]{1,0:T(8,128)(2,1)S(1)}, bf16[160,2560]{1,0:T(8,128)(2,1)}, u32[]{:S(2)}, u32[]{:S(2)}) collective-permute-start(bf16[160,2560]{1,0:T(8,128)(2,1)S(1)} %collective-permute-done.refs_0_), channel_id=1, source_target_pairs={{0,96},{16,112},{32,0},{48,16},{64,32},{80,48},{96,64},{112,80},{1... | collective-permute-start | bytes 2457608 | tf_op jit(solution)/shard_map/ppermute | solution.py:211
  95.9 36.6 %collective-permute-start.15 = (bf16[160,2560]{1,0:T(8,128)(2,1)S(1)}, bf16[160,2560]{1,0:T(8,128)(2,1)}, u32[]{:S(2)}, u32[]{:S(2)}) collective-permute-start(bf16[160,2560]{1,0:T(8,128)(2,1)S(1)} %collective-permute-done.refs_0_), channel_id=1, source_target_pairs={{0,32},{16,48},{32,64},{48,80},{64,96},{80,112},{96,0},{112,16},{1... | collective-permute-start | bytes 2457608 | tf_op jit(solution)/shard_map/ppermute | solution.py:211
  109.7 26.5 %all-to-all-start.2 = ((bf16[16,400,128]{2,1,0:T(8,128)(2,1)}), bf16[16,400,128]{2,1,0:T(8,128)(2,1)S(1)}, u32[]{:S(2)}, u32[]{:S(2)}) async-start(bf16[16,400,128]{2,1,0:T(8,128)(2,1)} %bitcast.4), calls=%async_computation.2 | async-start | bytes 3276800 | tf_op jit(solution)/shard_map/all_to_all | solution.py:282
  113.4 19.2 %collective-permute-start.18 = (bf16[160,2560]{1,0:T(8,128)(2,1)S(1)}, bf16[160,2560]{1,0:T(8,128)(2,1)S(1)}, u32[]{:S(2)}, u32[]{:S(2)}) collective-permute-start(bf16[160,2560]{1,0:T(8,128)(2,1)S(1)} %collective-permute-done.refs_0_), channel_id=1, source_target_pairs={{0,16},{16,0},{32,48},{48,32},{64,80},{80,64},{96,112},{112,96},{1... | collective-permute-start | bytes 2457608 | tf_op jit(solution)/shard_map/ppermute | solution.py:262
  117.3 18.9 %collective-permute-start.21 = (bf16[160,2560]{1,0:T(8,128)(2,1)}, bf16[160,2560]{1,0:T(8,128)(2,1)}, u32[]{:S(2)}, u32[]{:S(2)}) collective-permute-start(bf16[160,2560]{1,0:T(8,128)(2,1)} %collective-permute-done.17.refs_3_), channel_id=1, source_target_pairs={{0,16},{16,0},{32,48},{48,32},{64,80},{80,64},{96,112},{112,96},{1... | collective-permute-start | bytes 2457608 | tf_op jit(solution)/shard_map/ppermute | solution.py:262
  124.8 11.4 %collective-permute-start.20 = (bf16[160,2560]{1,0:T(8,128)(2,1)}, bf16[160,2560]{1,0:T(8,128)(2,1)}, u32[]{:S(2)}, u32[]{:S(2)}) collective-permute-start(bf16[160,2560]{1,0:T(8,128)(2,1)} %collective-permute-done.16.refs_2_), channel_id=1, source_target_pairs={{0,16},{16,0},{32,48},{48,32},{64,80},{80,64},{96,112},{112,96},{1... | collective-permute-start | bytes 2457608 | tf_op jit(solution)/shard_map/ppermute | solution.py:262
  132.6 3.6 %collective-permute-start.19 = (bf16[160,2560]{1,0:T(8,128)(2,1)}, bf16[160,2560]{1,0:T(8,128)(2,1)}, u32[]{:S(2)}, u32[]{:S(2)}) collective-permute-start(bf16[160,2560]{1,0:T(8,128)(2,1)} %collective-permute-done.15.refs_1_), channel_id=1, source_target_pairs={{0,16},{16,0},{32,48},{48,32},{64,80},{80,64},{96,112},{112,96},{1... | collective-permute-start | bytes 2457608 | tf_op jit(solution)/shard_map/ppermute | solution.py:262
  132.6 3.6 %copy-start.9 = (bf16[160,2560]{1,0:T(8,128)(2,1)}, bf16[160,2560]{1,0:T(8,128)(2,1)S(1)}, u32[]{:S(2)}) copy-start(bf16[160,2560]{1,0:T(8,128)(2,1)S(1)} %collective-permute-done.18.refs_4_) | copy-start | bytes 2457604
  136.2 1.2 copy-start.6

commit v3 on v2

v3 whole, which is shorter than its diff:
```python
import math

import jax
import jax.numpy as jnp
from jax import lax
from jax.experimental import pallas as pl
from jax.experimental.pallas import tpu as pltpu
from jax.sharding import PartitionSpec as P

HD = 128
WIN = 2
SPANS = 4
GROUPS = 8
SPACE = 8
ROWS = 80
SPAN = SPACE * ROWS
HEADS = 10
WIDE = SPACE * HD
PAIRS = 5
LENT = (0, 2, 3, 4)
UNITS = 3 * PAIRS + 2 * WIN
AHEAD = 2
STEPS = ((0, 0), (0, 1), (1, 0), (3, 0), (2, 0), (1, 1), (3, 1), (2, 1))
VMEM = pl.BlockSpec(memory_space=pltpu.VMEM)
HBM = pl.BlockSpec(memory_space=pltpu.HBM)
SMEM = pl.BlockSpec(memory_space=pltpu.SMEM)
MIB = 1 << 20


def params(mib):
    return pltpu.CompilerParams(vmem_limit_bytes=mib * MIB)


def goes_to(me, step):
    ring, cross = STEPS[step]
    return ((((me >> 1) + ring) & 3) << 1) | ((me & 1) ^ cross)


def came_from(me, step):
    ring, cross = STEPS[step]
    return ((((me >> 1) - ring) & 3) << 1) | ((me & 1) ^ cross)


def shift(x, axis, step):
    return lax.ppermute(x, axis, [(i, goes_to(i, step)) for i in range(8)])


def wait_for(ref, sem):
    pltpu.make_async_copy(ref, ref, sem).wait()


def picked(window, span_slot, block, group):
    place = jnp.int32(0)
    for span in range(SPANS):
        for w in range(WIN):
            slot = span_slot[window[w, block * SPANS + span]]
            place = jnp.where((slot >> 1) == group, slot & 1, place)
    return place


def pack_slots(window, span_slot, cache_keys, cache_values, by_head, *refs):
    rest, held, held_sems, sems = refs[:GROUPS], *refs[GROUPS:]
    me = lax.axis_index("cache")
    for kv, source in enumerate((cache_keys, cache_values)):
        pltpu.make_async_copy(source, held.at[kv], held_sems.at[kv]).start()
    for kv, source in enumerate((cache_keys, cache_values)):
        pltpu.make_async_copy(source, held.at[kv], held_sems.at[kv]).wait()
    for head in range(SPACE):
        source = held.at[:, :, :, pl.ds(head * HD, HD)]
        pltpu.make_async_copy(source, by_head.at[head], sems.at[0]).start()
    for step in range(GROUPS):
        slot = picked(window, span_slot, goes_to(me, step), me)
        source = held.at[:, slot, :, pl.ds(WIDE, 2 * HD)]
        pltpu.make_async_copy(source, rest[step], sems.at[1 + step]).start()
    wait_for(by_head, sems.at[0])
    for step in range(GROUPS):
        wait_for(rest[step], sems.at[1 + step])


def pack_pairs(queries, keys, values, out_weight, sent, *refs):
    lent, held, rows_held, held_sems, sems = refs[:2], *refs[2:]
    rows, columns = lent[0].shape
    column = pl.multiple_of((1 - lax.axis_index("head")) * columns, HD)
    loads = [
        pltpu.make_async_copy(source, held.at[kind], held_sems.at[kind])
        for kind, source in enumerate((queries, keys, values))
    ]
    for part in range(2):
        row = pl.multiple_of((2 * lax.axis_index("cache") + part) * rows, 16)
        source = out_weight.at[pl.ds(row, rows), pl.ds(column, columns)]
        loads.append(pltpu.make_async_copy(source, rows_held.at[part], held_sems.at[3 + part]))
    for load in loads:
        load.start()
    for kind in range(3):
        loads[kind].wait()
        for to in range(SPACE):
            wide, last = pl.ds(to * HD, HD), pl.ds(WIDE + to % 2 * HD, HD)
            pltpu.make_async_copy(
                held.at[kind, :, :, wide], sent.at[to, pl.ds(kind * PAIRS, SPANS)], sems.at[kind]
            ).start()
            pltpu.make_async_copy(
                held.at[kind, to // 2, :, last], sent.at[to, kind * PAIRS + SPANS], sems.at[kind]
            ).start()
    for part in range(2):
        loads[3 + part].wait()
        pltpu.make_async_copy(rows_held.at[part], lent[part], sems.at[3 + part]).start()
    for kind in range(3):
        wait_for(sent.at[:, pl.ds(kind * PAIRS, PAIRS)], sems.at[kind])
    for part in range(2):
        wait_for(lent[part], sems.at[3 + part])


def pack_cached(window, span_slot, by_head, *refs):
    rest, sent, wide = refs[:GROUPS], refs[GROUPS + 1], refs[GROUPS + 2 : 2 * GROUPS + 2]
    held, heads, held_sems, wide_sems, sent_sem = refs[2 * GROUPS + 2 :]
    group = lax.axis_index("cache")
    loads = [pltpu.make_async_copy(by_head, heads, held_sems.at[GROUPS])]
    for step in range(GROUPS):
        target = held.at[came_from(group, step)]
        loads.append(pltpu.make_async_copy(rest[step], target, held_sems.at[step]))
    for load in loads:
        load.start()
    loads[0].wait()
    for step in range(GROUPS):
        slot = picked(window, span_slot, goes_to(group, step), group)
        for kv in range(2):
            source = heads.at[:, kv, slot]
            pltpu.make_async_copy(source, wide[step].at[kv], wide_sems.at[step]).start()
    for load in loads[1:]:
        load.wait()
    for to in range(SPACE):
        for w in range(WIN):
            owner = span_slot[window[w, group * SPANS + to // 2]] >> 1
            pltpu.make_async_copy(
                held.at[owner, :, :, pl.ds(to % 2 * HD, HD)],
                sent.at[to, pl.ds(3 * PAIRS + 2 * w, 2)],
                sent_sem.at[0],
            ).start()
    for step in range(GROUPS):
        wait_for(wide[step], wide_sems.at[step])
    wait_for(sent.at[:, pl.ds(3 * PAIRS, 2 * WIN)], sent_sem.at[0])


def attend(window, span_slot, counts, *refs):
    came, wide = refs[0], refs[1 : 1 + GROUPS]
    out, own, sent, k_all, v_all, done, ready, left = refs[1 + GROUPS :]
    group = lax.axis_index("cache")
    me = lax.axis_index("space")
    factor = math.log2(math.e) / math.sqrt(HD)
    spots = lax.broadcasted_iota(jnp.int32, (SPAN, HD), 0)
    v_all[0:SPAN, HD:] = jnp.ones((SPAN, HD), jnp.bfloat16)

    def fetch(pair, source, target):
        pltpu.make_async_copy(source, target, ready.at[pair]).start()

    def fetch_pair(pair):
        for kind in range(3):
            fetch(pair, came.at[:, kind * PAIRS + pair], own.at[pair, kind])

    fetch_pair(0)
    for step in range(GROUPS):
        owner = came_from(group, step)
        place = jnp.int32(0)
        for entry in range(SPANS * WIN):
            slot = span_slot[window[entry % 2, group * SPANS + entry // 2]]
            place = jnp.where((slot >> 1) == owner, entry, place)
        fetch(place >> 1, wide[step], own.at[place >> 1, pl.ds(3 + 2 * (place & 1), 2)])
    for pair in range(1, PAIRS):
        fetch_pair(pair)
    for unit in range(2 * WIN):
        fetch(SPANS, came.at[:, 3 * PAIRS + unit], own.at[SPANS, 3 + unit])

    @pl.loop(0, PAIRS)
    def _(pair):
        pltpu.make_async_copy(own.at[pair], own.at[pair], ready.at[pair]).wait()
        span = jnp.where(pair < SPANS, pair, me >> 1)
        k_all[0:SPAN] = own[pair, 1].reshape(SPAN, HD)
        v_all[0:SPAN, 0:HD] = own[pair, 2].reshape(SPAN, HD)
        for w in range(WIN):
            limit = counts[window[w, group * SPANS + span]]
            part = slice((1 + w) * SPAN, (2 + w) * SPAN)
            valid = spots < limit
            held = own[pair, 3 + 2 * w].reshape(SPAN, HD).astype(jnp.float32)
            first = jnp.broadcast_to(held[0:1], (SPAN, HD))
            k_all[part] = jnp.where(valid, held, first).astype(jnp.bfloat16)
            held = own[pair, 4 + 2 * w].reshape(SPAN, HD).astype(jnp.float32)
            v_all[part, 0:HD] = jnp.where(valid, held, 0.0).astype(jnp.bfloat16)
            v_all[part, HD:] = jnp.where(valid, 1.0, 0.0).astype(jnp.bfloat16)
        share = SPACE // 2
        block = share * ROWS
        for first in range(0, SPACE, share):
            start = first * ROWS
            scores = lax.dot_general(
                own[pair, 0, first : first + share].reshape(block, HD),
                k_all[...],
                (((1,), (1,)), ((), ())),
                preferred_element_type=jnp.float32,
            )
            top = jnp.max(scores, axis=1, keepdims=True)
            weights = jnp.exp2((scores - top) * factor).astype(jnp.bfloat16)
            both = jnp.dot(weights, v_all[...], preferred_element_type=jnp.float32)
            done[start : start + block] = (both[:, 0:HD] / both[:, HD:]).astype(jnp.bfloat16)
        for step in range(SPACE):
            for half in range(2):
                sent[2 * step + half, pair] = done[step * ROWS : (step + 1) * ROWS]
        pltpu.make_async_copy(sent.at[:, pair], out.at[:, pair], left.at[pair]).start()

    for pair in range(PAIRS):
        pltpu.make_async_copy(sent.at[:, pair], out.at[:, pair], left.at[pair]).wait()


def project(came, own_weight, *refs):
    lent, out, features, own, other, mixed, came_sems, weight_sems, out_sems = (
        refs[:GROUPS],
        *refs[GROUPS:],
    )
    group = lax.axis_index("cache")
    half = lax.axis_index("head")
    columns = out.shape[1]
    rows = lent[0].shape[0]
    tiles = weight_sems.shape[0]
    tile = columns // tiles
    for part in range(2):
        source = half if part == 0 else 1 - half
        for space in range(SPACE):
            pltpu.make_async_copy(
                came.at[2 * space + source, pl.ds(0, SPANS * ROWS)],
                features.at[part, :, pl.ds(space * HD, HD)],
                came_sems.at[part],
            ).start()
            pltpu.make_async_copy(
                came.at[2 * space + source, pl.ds(SPANS * ROWS, ROWS)],
                features.at[
                    part, pl.ds(space // 2 * ROWS, ROWS), pl.ds(WIDE + space % 2 * HD, HD)
                ],
                came_sems.at[part],
            ).start()

    def fetch(step):
        here = pl.ds(step * tile, tile)
        start = pl.multiple_of(half * columns + step * tile, 128)
        pltpu.make_async_copy(
            own_weight.at[:, pl.ds(start, tile)], own.at[step], weight_sems.at[step, 0]
        ).start()
        for place, chunk in enumerate(lent):
            holder = group ^ (place // 4)
            start = pl.multiple_of(came_from(holder, LENT[place % 4]) * rows, 16)
            pltpu.make_async_copy(
                chunk.at[:, here], other.at[step, pl.ds(start, rows)], weight_sems.at[step, 1]
            ).start()

    for step in range(AHEAD):
        fetch(step)
    for part in range(2):
        wait_for(features.at[part], came_sems.at[part])
    for step in range(tiles):
        here = pl.ds(step * tile, tile)
        wait_for(own.at[step], weight_sems.at[step, 0])
        wait_for(other.at[step], weight_sems.at[step, 1])
        if step + AHEAD < tiles:
            fetch(step + AHEAD)
        total = jnp.dot(features[0], own[step], preferred_element_type=jnp.float32)
        total += jnp.dot(features[1], other[step], preferred_element_type=jnp.float32)
        mixed[step] = total.astype(jnp.bfloat16)
        pltpu.make_async_copy(mixed.at[step], out.at[:, here], out_sems.at[step]).start()
    for step in range(tiles):
        here = pl.ds(step * tile, tile)
        pltpu.make_async_copy(mixed.at[step], out.at[:, here], out_sems.at[step]).wait()


def on_device(
    queries, keys, values, cache_keys, cache_values, window, span_slot, counts, out_weight
):
    bf16 = jnp.bfloat16
    shape = jax.ShapeDtypeStruct
    depth, width = out_weight.shape
    columns = width // 2

    rows = depth // GROUPS // 2
    window = window.T

    by_head, *rest = pl.pallas_call(
        pack_slots,
        out_shape=[shape((SPACE, 2, 2, ROWS, HD), bf16)]
        + [shape((2, ROWS, 2 * HD), bf16)] * GROUPS,
        in_specs=[SMEM] * 2 + [HBM] * 2,
        out_specs=[HBM] * (1 + GROUPS),
        scratch_shapes=[
            pltpu.VMEM((2, 2, ROWS, HEADS * HD), bf16),
            pltpu.SemaphoreType.DMA((2,)),
            pltpu.SemaphoreType.DMA((1 + GROUPS,)),
        ],
        compiler_params=params(60),
        name="pack_slots",
    )(window, span_slot, cache_keys, cache_values)
    by_head, *rest, queries = lax.optimization_barrier((by_head, *rest, queries))
    by_head = lax.all_to_all(
        by_head.reshape(SPACE, 4 * ROWS, HD), "space", split_axis=0, concat_axis=0, tiled=True
    ).reshape(by_head.shape)
    rest = [rest[0]] + [shift(rest[step], "cache", step) for step in range(1, GROUPS)]

    pairs, *lent = pl.pallas_call(
        pack_pairs,
        out_shape=[shape((SPACE, UNITS, ROWS, HD), bf16)] + [shape((rows, columns), bf16)] * 2,
        in_specs=[HBM] * 4,
        out_specs=[HBM] * 3,
        scratch_shapes=[
            pltpu.VMEM((3, SPANS, ROWS, HEADS * HD), bf16),
            pltpu.VMEM((2, rows, columns), bf16),
            pltpu.SemaphoreType.DMA((5,)),
            pltpu.SemaphoreType.DMA((5,)),
        ],
        compiler_params=params(60),
        name="pack_pairs",
    )(queries, keys, values, out_weight)
    lent = [
        lax.ppermute(lent[0], "head", [(0, 1), (1, 0)]),
        lax.ppermute(lent[1], ("space", "head"), [(i, i ^ 3) for i in range(2 * SPACE)]),
    ]
    lent = jnp.concatenate(lent, 0)
    by_head, lent, *rest = lax.optimization_barrier((by_head, lent, *rest))
    pairs, *wide = pl.pallas_call(
        pack_cached,
        out_shape=[shape(pairs.shape, bf16)] + [shape((2, SPACE, ROWS, HD), bf16)] * GROUPS,
        in_specs=[SMEM] * 2 + [HBM] * (2 + GROUPS),
        out_specs=[HBM] * (1 + GROUPS),
        input_output_aliases={3 + GROUPS: 0},
        scratch_shapes=[
            pltpu.VMEM((GROUPS, 2, ROWS, 2 * HD), bf16),
            pltpu.VMEM(by_head.shape, bf16),
            pltpu.SemaphoreType.DMA((GROUPS + 1,)),
            pltpu.SemaphoreType.DMA((GROUPS,)),
            pltpu.SemaphoreType.DMA((1,)),
        ],
        compiler_params=params(60),
        name="pack_cached",
    )(window, span_slot, by_head, *rest, pairs)
    came = lax.all_to_all(
        pairs.reshape(SPACE, UNITS * ROWS, HD), "space", split_axis=0, concat_axis=0, tiled=True
    ).reshape(pairs.shape)
    wide = [wide[0]] + [shift(wide[step], "cache", step) for step in range(1, GROUPS)]
    came, lent, *wide = lax.optimization_barrier((came, lent, *wide))
    lent = [lent] + [shift(lent, "cache", step) for step in LENT[1:]]
    lent += [lax.ppermute(chunk, "cache", [(i, i ^ 1) for i in range(8)]) for chunk in lent]

    attended = pl.pallas_call(
        attend,
        out_shape=shape((2 * SPACE, PAIRS, ROWS, HD), bf16),
        in_specs=[SMEM] * 3 + [HBM] * (1 + GROUPS),
        out_specs=HBM,
        scratch_shapes=[
            pltpu.VMEM((PAIRS, 3 + 2 * WIN, SPACE, ROWS, HD), bf16),
            pltpu.VMEM((2 * SPACE, PAIRS, ROWS, HD), bf16),
            pltpu.VMEM((3 * SPAN, HD), bf16),
            pltpu.VMEM((3 * SPAN, 2 * HD), bf16),
            pltpu.VMEM((SPAN, HD), bf16),
            pltpu.SemaphoreType.DMA((PAIRS,)),
            pltpu.SemaphoreType.DMA((PAIRS,)),
        ],
        compiler_params=params(60),
        name="attend",
    )(window, span_slot, counts, came, *wide)
    attended = attended.reshape(2 * SPACE, PAIRS * ROWS, HD)
    attended = lax.all_to_all(
        attended, ("space", "head"), split_axis=0, concat_axis=0, tiled=True
    )

    tile = 512
    tiles = columns // tile
    mixed = pl.pallas_call(
        project,
        out_shape=shape((SPANS * ROWS, columns), bf16),
        in_specs=[HBM] * (2 + GROUPS),
        out_specs=HBM,
        scratch_shapes=[
            pltpu.VMEM((2, SPANS * ROWS, depth), bf16),
            pltpu.VMEM((tiles, depth, tile), bf16),
            pltpu.VMEM((tiles, depth, tile), bf16),
            pltpu.VMEM((tiles, SPANS * ROWS, tile), bf16),
            pltpu.SemaphoreType.DMA((2,)),
            pltpu.SemaphoreType.DMA((tiles, 2)),
            pltpu.SemaphoreType.DMA((tiles,)),
        ],
        compiler_params=params(52),
        name="project",
    )(attended, out_weight, *lent)
    return mixed.reshape(SPANS, ROWS, columns)


def solution(mesh):
    in_specs = (
        P("cache", "space", "head"),
        P("cache", "space", "head"),
        P("cache", "space", "head"),
        P("cache", "space", "head"),
        P("cache", "space", "head"),
        P(),
        P(),
        P(),
        P("head", None),
    )
    out_specs = P("cache", "space", "head")
    return jax.shard_map(
        on_device, mesh=mesh, in_specs=in_specs, out_specs=out_specs, check_vma=False
    )
```

time: 150 us -> 137 us (0.913)
  waiting for transfers between devices: 72.6 us -> 62.3 us
  local copies, waits for them, and re-layouts: 7.94 us -> 2.05 us
  starting transfers between devices: 37.1 us -> 40.6 us
    ppermute x18 -> x19, waiting for transfers between devices: 63.8 us -> 50.6 us  [the longest x17 49.4 us: shift(): return lax.ppermute(x, axis, [(i, goes_to(i, step)) for i in range(8)])]
    unnamed x47 -> x46, local copies, waits for them, and re-layouts: 6.75 us -> 2.05 us
    pallas_call x1, Pallas kernels: 11.8 us -> 8.24 us  [on_device(): pl.pallas_call(project, out_shape=shape((SPANS * ROWS, columns), bf16), i...]
    pallas_call x2 -> x3, Pallas kernels: 6.6 us -> 9.59 us  [the longest x1 3.6 us: on_device(): pl.pallas_call(pack_cached, out_shape=[shape(pairs.shape, bf16)] + [shape...]
    all_to_all x2, waiting for transfers between devices: 5.23 us -> 7.24 us  [the longest x1 7.24 us: on_device(): lax.all_to_all(pairs.reshape(SPACE, UNITS * ROWS, HD), 'space', split_axi...]
    ppermute x18 -> x19, starting transfers between devices: 21.4 us -> 23.2 us  [the longest x17 19.3 us: shift(): return lax.ppermute(x, axis, [(i, goes_to(i, step)) for i in range(8)])]
  transfers between devices with their start and end apart: 25 -> 26, of which waited for: 12 -> 14; matrix products, arithmetic and copies ran while one was open for 1% -> 0% of each run, Pallas kernels for 10% -> 10%
where the time goes in v3:
time: 137 us; the launch traced here: 136 us
  waiting for transfers between devices  62.3 us (45%)
  starting transfers between devices  40.6 us (30%)
  Pallas kernels  30.9 us (23%)
  local copies, waits for them, and re-layouts  2.05 us (1%)
    ppermute x17, waiting for transfers between devices, shift(): return lax.ppermute(x, axis, [(i, goes_to(i, step)) for i in range(8)])  49.4 us
    ppermute x17, starting transfers between devices, shift(): return lax.ppermute(x, axis, [(i, goes_to(i, step)) for i in range(8)])  19.3 us
    pallas_call x1, Pallas kernels, on_device(): pl.pallas_call(attend, out_shape=shape((2 * SPACE, PAIRS, ROWS, HD), bf16...  13.1 us
    pallas_call x1, Pallas kernels, on_device(): pl.pallas_call(project, out_shape=shape((SPANS * ROWS, columns), bf16), i...  8.24 us
    all_to_all x1, starting transfers between devices, on_device(): lax.all_to_all(pairs.reshape(SPACE, UNITS * ROWS, HD), 'space', split_axi...  7.99 us
    all_to_all x1, waiting for transfers between devices, on_device(): lax.all_to_all(pairs.reshape(SPACE, UNITS * ROWS, HD), 'space', split_axi...  7.24 us
    all_to_all x1, starting transfers between devices, on_device(): lax.all_to_all(by_head.reshape(SPACE, 4 * ROWS, HD), 'space', split_axis=...  5.47 us
    all_to_all x1, waiting for transfers between devices, on_device(): lax.all_to_all(attended, ('space', 'head'), split_axis=0, concat_axis=0,...  4.47 us
  transfers between devices with their start and end apart: 26, of which 14 were waited for; matrix products, arithmetic and copies ran while one was open for 0% of the time, Pallas kernels for 10%

profile of v3, /device:TPU:0, one launch (start us, length us, event | category | flops | bytes accessed | tf_op | source)
XLA Modules:
  0.0 136.4 jit_solution(9424407454262338060)
XLA Ops:
  0.0 2.9 %pack_slots.1 = (bf16[8,2,2,80,128]{4,3,2,1,0:T(8,128)(2,1)}, bf16[2,80,256]{2,1,0:T(8,128)(2,1)}, bf16[2,80,256]{2,1,0:T(8,128)(2,1)}, bf16[2,80,256]{2,1,0:T(8...) custom-call(s32[2,32]{1,0:T(2,128)} %bitcast.10, ...), custom_call_target="tpu_custom_call" | custom-call | tf_op jit(solution)/shard_map/pack_slots/pallas_call | solution.py:282
  3.0 3.0 %pack_pairs.1 = (bf16[8,19,80,128]{3,2,1,0:T(8,128)(2,1)}, bf16[80,2560]{1,0:T(8,128)(2,1)}, bf16[80,2560]{1,0:T(8,128)(2,1)}) custom-call(bf16[4,80,1280]{2,1,0:T(8,128)(2,1)} %queries, bf16[4,80,1280]{2,1,0:T(8,128)(2,1)} %keys.1, bf16[4,80,1280]{2,1,0:T(8,128)(2,1)} %values.1, bf16[1280,5120]{1,0:T(8,128)(2,1)} %own_weight.1), custom_call_target="tpu_custom_call" | custom-call | tf_op jit(solution)/shard_map/pack_pairs/pallas_call | solution.py:302
  6.1 1.7 %collective-permute-start = (bf16[80,2560]{1,0:T(8,128)(2,1)}, bf16[80,2560]{1,0:T(8,128)(2,1)S(1)}, u32[]{:S(2)}, u32[]{:S(2)}) collective-permute-start(bf16[80,2560]{1,0:T(8,128)(2,1)} %get-tuple-element.67), channel_id=1, source_target_pairs={{0,1},{1,0},{2,3},{3,2},{4,5},{5,4},{6,7},{7,6},{8,9},{9,8},{10,11... | collective-permute-start | bytes 1228808 | tf_op jit(solution)/shard_map/ppermute | solution.py:317
  7.8 2.2 %collective-permute-start.1 = (bf16[80,2560]{1,0:T(8,128)(2,1)}, bf16[80,2560]{1,0:T(8,128)(2,1)S(1)}, u32[]{:S(2)}, u32[]{:S(2)}) collective-permute-start(bf16[80,2560]{1,0:T(8,128)(2,1)} %get-tuple-element.68), channel_id=1, source_target_pairs={{0,3},{1,2},{2,1},{3,0},{4,7},{5,6},{6,5},{7,4},{8,11},{9,10},{10,... | collective-permute-start | bytes 1228808 | tf_op jit(solution)/shard_map/ppermute | solution.py:318
  10.0 5.5 %all-to-all-start = ((bf16[8,320,128]{2,1,0:T(8,128)(2,1)}), bf16[8,320,128]{2,1,0:T(8,128)(2,1)S(1)}, u32[]{:S(2)}, u32[]{:S(2)}) async-start(bf16[8,320,128]{2,1,0:T(8,128)(2,1)} %bitcast.1), calls=%async_computation | async-start | bytes 1310720 | tf_op jit(solution)/shard_map/all_to_all | solution.py:297
  15.5 0.1 collective-permute-start.2
  15.6 1.6 %collective-permute-start.3 = (bf16[2,80,256]{2,1,0:T(8,128)(2,1)S(1)}, bf16[2,80,256]{2,1,0:T(8,128)(2,1)S(1)}, u32[]{:S(2)}, u32[]{:S(2)}) collective-permute-start(bf16[2,80,256]{2,1,0:T(8,128)(2,1)S(1)} %copy-done.21), channel_id=1, source_target_pairs={{0,32},{16,48},{32,64},{48,80},{64,96},{80,112},{96,0},{112,16},{1... | collective-permute-start | bytes 245768 | tf_op jit(solution)/shard_map/ppermute | solution.py:45
  17.1 1.7 %collective-permute-start.4 = (bf16[2,80,256]{2,1,0:T(8,128)(2,1)S(1)}, bf16[2,80,256]{2,1,0:T(8,128)(2,1)S(1)}, u32[]{:S(2)}, u32[]{:S(2)}) collective-permute-start(bf16[2,80,256]{2,1,0:T(8,128)(2,1)S(1)} %copy-done.20), channel_id=1, source_target_pairs={{0,96},{16,112},{32,0},{48,16},{64,32},{80,48},{96,64},{112,80},{1... | collective-permute-start | bytes 245768 | tf_op jit(solution)/shard_map/ppermute | solution.py:45
  18.9 0.0 collective-permute-done.2.refs_1_
  18.9 1.9 %collective-permute-start.5 = (bf16[2,80,256]{2,1,0:T(8,128)(2,1)S(1)}, bf16[2,80,256]{2,1,0:T(8,128)(2,1)S(1)}, u32[]{:S(2)}, u32[]{:S(2)}) collective-permute-start(bf16[2,80,256]{2,1,0:T(8,128)(2,1)S(1)} %copy-done.19), channel_id=1, source_target_pairs={{0,64},{16,80},{32,96},{48,112},{64,0},{80,16},{96,32},{112,48},{1... | collective-permute-start | bytes 245768 | tf_op jit(solution)/shard_map/ppermute | solution.py:45
  20.8 0.9 collective-permute-done.3.refs_2_
  21.7 0.0 collective-permute-start.6
  21.7 2.9 %collective-permute-start.7 = (bf16[2,80,256]{2,1,0:T(8,128)(2,1)S(1)}, bf16[2,80,256]{2,1,0:T(8,128)(2,1)S(1)}, u32[]{:S(2)}, u32[]{:S(2)}) collective-permute-start(bf16[2,80,256]{2,1,0:T(8,128)(2,1)S(1)} %copy-done.17), channel_id=1, source_target_pairs={{0,112},{16,96},{32,16},{48,0},{64,48},{80,32},{96,80},{112,64},{1... | collective-permute-start | bytes 245768 | tf_op jit(solution)/shard_map/ppermute | solution.py:45
  24.6 1.2 collective-permute-done.1
  25.8 1.1 collective-permute-start.8
  26.9 0.1 pad_maximum_fusion.refs_0_
  27.0 0.0 collective-permute-done.5.refs_4_
  27.0 0.4 collective-permute-done.6.refs_5_
  27.4 4.5 %collective-permute-done.8.refs_7_ = bf16[2,80,256]{2,1,0:T(8,128)(2,1)S(1)} collective-permute-done((bf16[2,80,256]{2,1,0:T(8,128)(2,1)S(1)}, bf16[2,80,256]{2,1,0:T(8,128)(2,1)S(1)}, u32[]{:S(2)}, u32[]{:S(2)}) %collective-permute-start.8) | collective-permute-done | bytes 81952 | tf_op jit(solution)/shard_map/ppermute | solution.py:45
  32.0 0.6 copy-done.13
  32.6 0.2 copy-done.1
  32.8 3.6 %pack_cached.1 = (bf16[8,19,80,128]{3,2,1,0:T(8,128)(2,1)}, bf16[2,8,80,128]{3,2,1,0:T(8,128)(2,1)}, bf16[2,8,80,128]{3,2,1,0:T(8,128)(2,1)}, bf16[2,8,80,128]{3...) custom-call(s32[2,32]{1,0:T(2,128)} %bitcast.11, ...), custom_call_target="tpu_custom_call", output_to_operand_aliasing={{0}: (11, {})} | custom-call | tf_op jit(solution)/shard_map/pack_cached/pallas_call | solution.py:322
  36.4 8.0 %all-to-all-start.1 = ((bf16[8,1520,128]{2,1,0:T(8,128)(2,1)}), bf16[8,1520,128]{2,1,0:T(8,128)(2,1)}, u32[]{:S(2)}, u32[]{:S(2)}) async-start(bf16[8,1520,128]{2,1,0:T(8,128)(2,1)} %bitcast.7), calls=%async_computation.1 | async-start | bytes 6225920 | tf_op jit(solution)/shard_map/all_to_all | solution.py:338
  44.4 0.0 collective-permute-start.9
  44.4 0.8 collective-permute-start.10
  45.3 2.5 %collective-permute-start.11 = (bf16[2,8,80,128]{3,2,1,0:T(8,128)(2,1)}, bf16[2,8,80,128]{3,2,1,0:T(8,128)(2,1)S(1)}, u32[]{:S(2)}, u32[]{:S(2)}) collective-permute-start(bf16[2,8,80,128]{3,2,1,0:T(8,128)(2,1)} %get-tuple-element.92), channel_id=1, source_target_pairs={{0,96},{16,112},{32,0},{48,16},{64,32},{80,48},{96,64},{112,80},{1... | collective-permute-start | bytes 983048 | tf_op jit(solution)/shard_map/ppermute | solution.py:45
  47.8 1.0 collective-permute-start.12
  48.8 0.0 collective-permute-start.13
  48.8 0.0 collective-permute-done.9.refs_2_
  48.8 3.0 %collective-permute-start.14 = (bf16[2,8,80,128]{3,2,1,0:T(8,128)(2,1)S(1)}, bf16[2,8,80,128]{3,2,1,0:T(8,128)(2,1)}, u32[]{:S(2)}, u32[]{:S(2)}) collective-permute-start(bf16[2,8,80,128]{3,2,1,0:T(8,128)(2,1)S(1)} %copy-done.15), channel_id=1, source_target_pairs={{0,112},{16,96},{32,16},{48,0},{64,48},{80,32},{96,80},{112,64},{1... | collective-permute-start | bytes 983048 | tf_op jit(solution)/shard_map/ppermute | solution.py:45
  51.8 11.4 %collective-permute-done.10.refs_3_ = bf16[2,8,80,128]{3,2,1,0:T(8,128)(2,1)S(1)} collective-permute-done((bf16[2,8,80,128]{3,2,1,0:T(8,128)(2,1)}, bf16[2,8,80,128]{3,2,1,0:T(8,128)(2,1)S(1)}, u32[]{:S(2)}, u32[]{:S(2)}) %collective-permute-start.10) | collective-permute-done | bytes 327712 | tf_op jit(solution)/shard_map/ppermute | solution.py:45
  63.2 0.0 collective-permute-done.11.refs_4_
  63.3 0.4 collective-permute-done.12.refs_5_
  63.7 5.9 %collective-permute-done.13.refs_6_ = bf16[2,8,80,128]{3,2,1,0:T(8,128)(2,1)S(1)} collective-permute-done((bf16[2,8,80,128]{3,2,1,0:T(8,128)(2,1)}, bf16[2,8,80,128]{3,2,1,0:T(8,128)(2,1)S(1)}, u32[]{:S(2)}, u32[]{:S(2)}) %collective-permute-start.13) | collective-permute-done | bytes 327712 | tf_op jit(solution)/shard_map/ppermute | solution.py:45
  69.6 6.8 %collective-permute-done.14.refs_7_ = bf16[2,8,80,128]{3,2,1,0:T(8,128)(2,1)} collective-permute-done((bf16[2,8,80,128]{3,2,1,0:T(8,128)(2,1)S(1)}, bf16[2,8,80,128]{3,2,1,0:T(8,128)(2,1)}, u32[]{:S(2)}, u32[]{:S(2)}) %collective-permute-start.14) | collective-permute-done | bytes 327712 | tf_op jit(solution)/shard_map/ppermute | solution.py:45
  76.4 0.6 collective-permute-done.15.refs_8_
  76.9 7.2 %all-to-all-done.1 = bf16[8,1520,128]{2,1,0:T(8,128)(2,1)} async-done(((bf16[8,1520,128]{2,1,0:T(8,128)(2,1)}), bf16[8,1520,128]{2,1,0:T(8,128)(2,1)}, u32[]{:S(2)}, u32[]{:S(2)}) %all-to-all-start.1) | async-done | bytes 3112992 | tf_op jit(solution)/shard_map/all_to_all | solution.py:338
  84.2 2.6 %collective-permute-start.17 = (bf16[160,2560]{1,0:T(8,128)(2,1)S(1)}, bf16[160,2560]{1,0:T(8,128)(2,1)}, u32[]{:S(2)}, u32[]{:S(2)}) collective-permute-start(bf16[160,2560]{1,0:T(8,128)(2,1)S(1)} %pad_maximum_fusion.refs_0_), channel_id=1, source_target_pairs={{0,96},{16,112},{32,0},{48,16},{64,32},{80,48},{96,64},{112,80},{1... | collective-permute-start | bytes 2457608 | tf_op jit(solution)/shard_map/ppermute | solution.py:45
  86.8 13.1 %attend.1 = bf16[16,5,80,128]{3,2,1,0:T(8,128)(2,1)} custom-call(s32[2,32]{1,0:T(2,128)} %bitcast.12, s32[16]{0:T(128)} %span_slot.5, s32[16]{0:T(128)} %counts.1, bf16[8,19,80,128]{3,2,1,0:T(8,128)(2,1)} %bitcast.4.refs_0_, bf16[2,8,80,128]{3,2,1,0:T(8,128)(2,1)} %get-tuple-element.98.refs_1_, bf16[2,8,80,128]{3,2,1,0:T(8,128)(2,1)} %copy-done.2, ...), custom_call_target="tpu_custom_call" | custom-call | tf_op jit(solution)/shard_map/attend/pallas_call | solution.py:346
  99.9 3.8 %all-to-all-start.2 = ((bf16[16,400,128]{2,1,0:T(8,128)(2,1)}), bf16[16,400,128]{2,1,0:T(8,128)(2,1)S(1)}, u32[]{:S(2)}, u32[]{:S(2)}) async-start(bf16[16,400,128]{2,1,0:T(8,128)(2,1)} %bitcast.8), calls=%async_computation.2 | async-start | bytes 3276800 | tf_op jit(solution)/shard_map/all_to_all | solution.py:364
  103.7 0.1 collective-permute-start.19
  103.8 3.2 %collective-permute-done.18.refs_3_ = bf16[160,2560]{1,0:T(8,128)(2,1)} collective-permute-done((bf16[160,2560]{1,0:T(8,128)(2,1)S(1)}, bf16[160,2560]{1,0:T(8,128)(2,1)}, u32[]{:S(2)}, u32[]{:S(2)}) %collective-permute-start.18) | collective-permute-done | bytes 819232 | tf_op jit(solution)/shard_map/ppermute | solution.py:45
  107.0 11.3 %collective-permute-done.17.refs_2_ = bf16[160,2560]{1,0:T(8,128)(2,1)} collective-permute-done((bf16[160,2560]{1,0:T(8,128)(2,1)S(1)}, bf16[160,2560]{1,0:T(8,128)(2,1)}, u32[]{:S(2)}, u32[]{:S(2)}) %collective-permute-start.17) | collective-permute-done | bytes 819232 | tf_op jit(solution)/shard_map/ppermute | solution.py:45
  118.3 4.0 %collective-permute-done.16.refs_1_ = bf16[160,2560]{1,0:T(8,128)(2,1)S(1)} collective-permute-done((bf16[160,2560]{1,0:T(8,128)(2,1)S(1)}, bf16[160,2560]{1,0:T(8,128)(2,1)S(1)}, u32[]{:S(2)}, u32[]{:S(2)}) %collective-permute-start.16) | collective-permute-done | bytes 819232 | tf_op jit(solution)/shard_map/ppermute | solution.py:45
  122.3 0.0 collective-permute-start.20
  122.3 4.5 %all-to-all-done.2.came = bf16[16,400,128]{2,1,0:T(8,128)(2,1)S(1)} async-done(((bf16[16,400,128]{2,1,0:T(8,128)(2,1)}), bf16[16,400,128]{2,1,0:T(8,128)(2,1)S(1)}, u32[]{:S(2)}, u32[]{:S(2)}) %all-to-all-start.2) | async-done | bytes 1638432 | tf_op jit(solution)/shard_map/all_to_all | solution.py:364
  126.8 1.2 copy-done
  128.0 8.2 %project.1 = bf16[320,2560]{1,0:T(8,128)(2,1)} custom-call(bf16[16,400,128]{2,1,0:T(8,128)(2,1)} %copy-done, bf16[1280,5120]{1,0:T(8,128)(2,1)} %own_weight.1, bf16[160,2560]{1,0:T(8,128)(2,1)S(1)} %pad_maximum_fusion.refs_0_, bf16[160,2560]{1,0:T(8,128)(2,1)S(1)} %collective-permute-done.16.refs_1_, bf16[160,2560]{1,0:T(8,128)(2,1)} %collective-permute-done.17.refs_2_, ...), custom_call_target="tpu_custom_call" | custom-call | tf_op jit(solution)/shard_map/project/pallas_call | solution.py:370
  (56 shorter events, 0.1 us)
Async XLA Ops:
  3.0 12.5 %copy-start.22 = (bf16[2,80,256]{2,1,0:T(8,128)(2,1)S(1)}, bf16[2,80,256]{2,1,0:T(8,128)(2,1)}, u32[]{:S(2)}) copy-start(bf16[2,80,256]{2,1,0:T(8,128)(2,1)} %get-tuple-element.70) | copy-start | bytes 245764
  3.0 12.6 %copy-start.21 = (bf16[2,80,256]{2,1,0:T(8,128)(2,1)S(1)}, bf16[2,80,256]{2,1,0:T(8,128)(2,1)}, u32[]{:S(2)}) copy-start(bf16[2,80,256]{2,1,0:T(8,128)(2,1)} %get-tuple-element.71) | copy-start | bytes 245764
  3.0 14.2 %copy-start.20 = (bf16[2,80,256]{2,1,0:T(8,128)(2,1)S(1)}, bf16[2,80,256]{2,1,0:T(8,128)(2,1)}, u32[]{:S(2)}) copy-start(bf16[2,80,256]{2,1,0:T(8,128)(2,1)} %get-tuple-element.72) | copy-start | bytes 245764
  3.0 15.9 %copy-start.19 = (bf16[2,80,256]{2,1,0:T(8,128)(2,1)S(1)}, bf16[2,80,256]{2,1,0:T(8,128)(2,1)}, u32[]{:S(2)}) copy-start(bf16[2,80,256]{2,1,0:T(8,128)(2,1)} %get-tuple-element.73) | copy-start | bytes 245764
  3.0 18.7 %copy-start.18 = (bf16[2,80,256]{2,1,0:T(8,128)(2,1)S(1)}, bf16[2,80,256]{2,1,0:T(8,128)(2,1)}, u32[]{:S(2)}) copy-start(bf16[2,80,256]{2,1,0:T(8,128)(2,1)} %get-tuple-element.74) | copy-start | bytes 245764
  3.0 18.7 %copy-start.17 = (bf16[2,80,256]{2,1,0:T(8,128)(2,1)S(1)}, bf16[2,80,256]{2,1,0:T(8,128)(2,1)}, u32[]{:S(2)}) copy-start(bf16[2,80,256]{2,1,0:T(8,128)(2,1)} %get-tuple-element.75) | copy-start | bytes 245764
  3.0 22.8 %copy-start.16 = (bf16[2,80,256]{2,1,0:T(8,128)(2,1)S(1)}, bf16[2,80,256]{2,1,0:T(8,128)(2,1)}, u32[]{:S(2)}) copy-start(bf16[2,80,256]{2,1,0:T(8,128)(2,1)} %get-tuple-element.76) | copy-start | bytes 245764
  6.1 15.6 %collective-permute-start = (bf16[80,2560]{1,0:T(8,128)(2,1)}, bf16[80,2560]{1,0:T(8,128)(2,1)S(1)}, u32[]{:S(2)}, u32[]{:S(2)}) collective-permute-start(bf16[80,2560]{1,0:T(8,128)(2,1)} %get-tuple-element.67), channel_id=1, source_target_pairs={{0,1},{1,0},{2,3},{3,2},{4,5},{5,4},{6,7},{7,6},{8,9},{9,8},{10,11... | collective-permute-start | bytes 1228808 | tf_op jit(solution)/shard_map/ppermute | solution.py:317
  7.8 18.0 %collective-permute-start.1 = (bf16[80,2560]{1,0:T(8,128)(2,1)}, bf16[80,2560]{1,0:T(8,128)(2,1)S(1)}, u32[]{:S(2)}, u32[]{:S(2)}) collective-permute-start(bf16[80,2560]{1,0:T(8,128)(2,1)} %get-tuple-element.68), channel_id=1, source_target_pairs={{0,3},{1,2},{2,1},{3,0},{4,7},{5,6},{6,5},{7,4},{8,11},{9,10},{10,... | collective-permute-start | bytes 1228808 | tf_op jit(solution)/shard_map/ppermute | solution.py:318
  10.0 22.0 %all-to-all-start = ((bf16[8,320,128]{2,1,0:T(8,128)(2,1)}), bf16[8,320,128]{2,1,0:T(8,128)(2,1)S(1)}, u32[]{:S(2)}, u32[]{:S(2)}) async-start(bf16[8,320,128]{2,1,0:T(8,128)(2,1)} %bitcast.1), calls=%async_computation | async-start | bytes 1310720 | tf_op jit(solution)/shard_map/all_to_all | solution.py:297
  15.5 3.4 %collective-permute-start.2 = (bf16[2,80,256]{2,1,0:T(8,128)(2,1)S(1)}, bf16[2,80,256]{2,1,0:T(8,128)(2,1)S(1)}, u32[]{:S(2)}, u32[]{:S(2)}) collective-permute-start(bf16[2,80,256]{2,1,0:T(8,128)(2,1)S(1)} %copy-done.22), channel_id=1, source_target_pairs={{0,16},{16,0},{32,48},{48,32},{64,80},{80,64},{96,112},{112,96},{1... | collective-permute-start | bytes 245768 | tf_op jit(solution)/shard_map/ppermute | solution.py:45
  15.6 6.1 %collective-permute-start.3 = (bf16[2,80,256]{2,1,0:T(8,128)(2,1)S(1)}, bf16[2,80,256]{2,1,0:T(8,128)(2,1)S(1)}, u32[]{:S(2)}, u32[]{:S(2)}) collective-permute-start(bf16[2,80,256]{2,1,0:T(8,128)(2,1)S(1)} %copy-done.21), channel_id=1, source_target_pairs={{0,32},{16,48},{32,64},{48,80},{64,96},{80,112},{96,0},{112,16},{1... | collective-permute-start | bytes 245768 | tf_op jit(solution)/shard_map/ppermute | solution.py:45
  17.1 9.8 %collective-permute-start.4 = (bf16[2,80,256]{2,1,0:T(8,128)(2,1)S(1)}, bf16[2,80,256]{2,1,0:T(8,128)(2,1)S(1)}, u32[]{:S(2)}, u32[]{:S(2)}) collective-permute-start(bf16[2,80,256]{2,1,0:T(8,128)(2,1)S(1)} %copy-done.20), channel_id=1, source_target_pairs={{0,96},{16,112},{32,0},{48,16},{64,32},{80,48},{96,64},{112,80},{1... | collective-permute-start | bytes 245768 | tf_op jit(solution)/shard_map/ppermute | solution.py:45
  18.9 13.1 %copy-start.7 = (bf16[2,80,256]{2,1,0:T(8,128)(2,1)}, bf16[2,80,256]{2,1,0:T(8,128)(2,1)S(1)}, u32[]{:S(2)}) copy-start(bf16[2,80,256]{2,1,0:T(8,128)(2,1)S(1)} %collective-permute-done.2.refs_1_) | copy-start | bytes 245764
  18.9 8.1 %collective-permute-start.5 = (bf16[2,80,256]{2,1,0:T(8,128)(2,1)S(1)}, bf16[2,80,256]{2,1,0:T(8,128)(2,1)S(1)}, u32[]{:S(2)}, u32[]{:S(2)}) collective-permute-start(bf16[2,80,256]{2,1,0:T(8,128)(2,1)S(1)} %copy-done.19), channel_id=1, source_target_pairs={{0,64},{16,80},{32,96},{48,112},{64,0},{80,16},{96,32},{112,48},{1... | collective-permute-start | bytes 245768 | tf_op jit(solution)/shard_map/ppermute | solution.py:45
  21.6 10.3 %copy-start.8 = (bf16[2,80,256]{2,1,0:T(8,128)(2,1)}, bf16[2,80,256]{2,1,0:T(8,128)(2,1)S(1)}, u32[]{:S(2)}) copy-start(bf16[2,80,256]{2,1,0:T(8,128)(2,1)S(1)} %collective-permute-done.3.refs_2_) | copy-start | bytes 245764
  21.7 5.8 %collective-permute-start.6 = (bf16[2,80,256]{2,1,0:T(8,128)(2,1)S(1)}, bf16[2,80,256]{2,1,0:T(8,128)(2,1)S(1)}, u32[]{:S(2)}, u32[]{:S(2)}) collective-permute-start(bf16[2,80,256]{2,1,0:T(8,128)(2,1)S(1)} %copy-done.18), channel_id=1, source_target_pairs={{0,48},{16,32},{32,80},{48,64},{64,112},{80,96},{96,16},{112,0},{1... | collective-permute-start | bytes 245768 | tf_op jit(solution)/shard_map/ppermute | solution.py:45
  21.7 5.8 %collective-permute-start.7 = (bf16[2,80,256]{2,1,0:T(8,128)(2,1)S(1)}, bf16[2,80,256]{2,1,0:T(8,128)(2,1)S(1)}, u32[]{:S(2)}, u32[]{:S(2)}) collective-permute-start(bf16[2,80,256]{2,1,0:T(8,128)(2,1)S(1)} %copy-done.17), channel_id=1, source_target_pairs={{0,112},{16,96},{32,16},{48,0},{64,48},{80,32},{96,80},{112,64},{1... | collective-permute-start | bytes 245768 | tf_op jit(solution)/shard_map/ppermute | solution.py:45
  25.8 6.2 %collective-permute-start.8 = (bf16[2,80,256]{2,1,0:T(8,128)(2,1)S(1)}, bf16[2,80,256]{2,1,0:T(8,128)(2,1)S(1)}, u32[]{:S(2)}, u32[]{:S(2)}) collective-permute-start(bf16[2,80,256]{2,1,0:T(8,128)(2,1)S(1)} %copy-done.16), channel_id=1, source_target_pairs={{0,80},{16,64},{32,112},{48,96},{64,16},{80,0},{96,48},{112,32},{1... | collective-permute-start | bytes 245768 | tf_op jit(solution)/shard_map/ppermute | solution.py:45
  27.0 5.0 %copy-start.9 = (bf16[2,80,256]{2,1,0:T(8,128)(2,1)}, bf16[2,80,256]{2,1,0:T(8,128)(2,1)S(1)}, u32[]{:S(2)}) copy-start(bf16[2,80,256]{2,1,0:T(8,128)(2,1)S(1)} %collective-permute-done.4.refs_3_) | copy-start | bytes 245764
  27.0 5.0 %copy-start.10 = (bf16[2,80,256]{2,1,0:T(8,128)(2,1)}, bf16[2,80,256]{2,1,0:T(8,128)(2,1)S(1)}, u32[]{:S(2)}) copy-start(bf16[2,80,256]{2,1,0:T(8,128)(2,1)S(1)} %collective-permute-done.5.refs_4_) | copy-start | bytes 245764
  27.4 4.6 %copy-start.11 = (bf16[2,80,256]{2,1,0:T(8,128)(2,1)}, bf16[2,80,256]{2,1,0:T(8,128)(2,1)S(1)}, u32[]{:S(2)}) copy-start(bf16[2,80,256]{2,1,0:T(8,128)(2,1)S(1)} %collective-permute-done.6.refs_5_) | copy-start | bytes 245764
  27.4 4.6 %copy-start.12 = (bf16[2,80,256]{2,1,0:T(8,128)(2,1)}, bf16[2,80,256]{2,1,0:T(8,128)(2,1)S(1)}, u32[]{:S(2)}) copy-start(bf16[2,80,256]{2,1,0:T(8,128)(2,1)S(1)} %collective-permute-done.7.refs_6_) | copy-start | bytes 245764
  32.0 0.9 copy-start.1
  36.4 12.4 %copy-start.15 = (bf16[2,8,80,128]{3,2,1,0:T(8,128)(2,1)S(1)}, bf16[2,8,80,128]{3,2,1,0:T(8,128)(2,1)}, u32[]{:S(2)}) copy-start(bf16[2,8,80,128]{3,2,1,0:T(8,128)(2,1)} %get-tuple-element.95) | copy-start | bytes 983044
  36.4 26.8 %copy-start.14 = (bf16[2,8,80,128]{3,2,1,0:T(8,128)(2,1)S(1)}, bf16[2,8,80,128]{3,2,1,0:T(8,128)(2,1)}, u32[]{:S(2)}) copy-start(bf16[2,8,80,128]{3,2,1,0:T(8,128)(2,1)} %get-tuple-element.96) | copy-start | bytes 983044
  36.4 47.7 %all-to-all-start.1 = ((bf16[8,1520,128]{2,1,0:T(8,128)(2,1)}), bf16[8,1520,128]{2,1,0:T(8,128)(2,1)}, u32[]{:S(2)}, u32[]{:S(2)}) async-start(bf16[8,1520,128]{2,1,0:T(8,128)(2,1)} %bitcast.7), calls=%async_computation.1 | async-start | bytes 6225920 | tf_op jit(solution)/shard_map/all_to_all | solution.py:338
  44.4 4.3 %collective-permute-start.9 = (bf16[2,8,80,128]{3,2,1,0:T(8,128)(2,1)}, bf16[2,8,80,128]{3,2,1,0:T(8,128)(2,1)S(1)}, u32[]{:S(2)}, u32[]{:S(2)}) collective-permute-start(bf16[2,8,80,128]{3,2,1,0:T(8,128)(2,1)} %get-tuple-element.90), channel_id=1, source_target_pairs={{0,16},{16,0},{32,48},{48,32},{64,80},{80,64},{96,112},{112,96},{1... | collective-permute-start | bytes 983048 | tf_op jit(solution)/shard_map/ppermute | solution.py:45
  44.4 18.8 %collective-permute-start.10 = (bf16[2,8,80,128]{3,2,1,0:T(8,128)(2,1)}, bf16[2,8,80,128]{3,2,1,0:T(8,128)(2,1)S(1)}, u32[]{:S(2)}, u32[]{:S(2)}) collective-permute-start(bf16[2,8,80,128]{3,2,1,0:T(8,128)(2,1)} %get-tuple-element.91), channel_id=1, source_target_pairs={{0,32},{16,48},{32,64},{48,80},{64,96},{80,112},{96,0},{112,16},{1... | collective-permute-start | bytes 983048 | tf_op jit(solution)/shard_map/ppermute | solution.py:45
  45.3 18.0 %collective-permute-start.11 = (bf16[2,8,80,128]{3,2,1,0:T(8,128)(2,1)}, bf16[2,8,80,128]{3,2,1,0:T(8,128)(2,1)S(1)}, u32[]{:S(2)}, u32[]{:S(2)}) collective-permute-start(bf16[2,8,80,128]{3,2,1,0:T(8,128)(2,1)} %get-tuple-element.92), channel_id=1, source_target_pairs={{0,96},{16,112},{32,0},{48,16},{64,32},{80,48},{96,64},{112,80},{1... | collective-permute-start | bytes 983048 | tf_op jit(solution)/shard_map/ppermute | solution.py:45
  47.8 15.9 %collective-permute-start.12 = (bf16[2,8,80,128]{3,2,1,0:T(8,128)(2,1)}, bf16[2,8,80,128]{3,2,1,0:T(8,128)(2,1)S(1)}, u32[]{:S(2)}, u32[]{:S(2)}) collective-permute-start(bf16[2,8,80,128]{3,2,1,0:T(8,128)(2,1)} %get-tuple-element.93), channel_id=1, source_target_pairs={{0,64},{16,80},{32,96},{48,112},{64,0},{80,16},{96,32},{112,48},{1... | collective-permute-start | bytes 983048 | tf_op jit(solution)/shard_map/ppermute | solution.py:45
  48.8 20.8 %collective-permute-start.13 = (bf16[2,8,80,128]{3,2,1,0:T(8,128)(2,1)}, bf16[2,8,80,128]{3,2,1,0:T(8,128)(2,1)S(1)}, u32[]{:S(2)}, u32[]{:S(2)}) collective-permute-start(bf16[2,8,80,128]{3,2,1,0:T(8,128)(2,1)} %get-tuple-element.94), channel_id=1, source_target_pairs={{0,48},{16,32},{32,80},{48,64},{64,112},{80,96},{96,16},{112,0},{1... | collective-permute-start | bytes 983048 | tf_op jit(solution)/shard_map/ppermute | solution.py:45
  48.8 38.0 %copy-start.2 = (bf16[2,8,80,128]{3,2,1,0:T(8,128)(2,1)}, bf16[2,8,80,128]{3,2,1,0:T(8,128)(2,1)S(1)}, u32[]{:S(2)}) copy-start(bf16[2,8,80,128]{3,2,1,0:T(8,128)(2,1)S(1)} %collective-permute-done.9.refs_2_) | copy-start | bytes 983044
  48.8 27.6 %collective-permute-start.14 = (bf16[2,8,80,128]{3,2,1,0:T(8,128)(2,1)S(1)}, bf16[2,8,80,128]{3,2,1,0:T(8,128)(2,1)}, u32[]{:S(2)}, u32[]{:S(2)}) collective-permute-start(bf16[2,8,80,128]{3,2,1,0:T(8,128)(2,1)S(1)} %copy-done.15), channel_id=1, source_target_pairs={{0,112},{16,96},{32,16},{48,0},{64,48},{80,32},{96,80},{112,64},{1... | collective-permute-start | bytes 983048 | tf_op jit(solution)/shard_map/ppermute | solution.py:45
  63.2 23.6 %copy-start.3 = (bf16[2,8,80,128]{3,2,1,0:T(8,128)(2,1)}, bf16[2,8,80,128]{3,2,1,0:T(8,128)(2,1)S(1)}, u32[]{:S(2)}) copy-start(bf16[2,8,80,128]{3,2,1,0:T(8,128)(2,1)S(1)} %collective-permute-done.10.refs_3_) | copy-start | bytes 983044
  63.2 13.7 %collective-permute-start.15 = (bf16[2,8,80,128]{3,2,1,0:T(8,128)(2,1)S(1)}, bf16[2,8,80,128]{3,2,1,0:T(8,128)(2,1)}, u32[]{:S(2)}, u32[]{:S(2)}) collective-permute-start(bf16[2,8,80,128]{3,2,1,0:T(8,128)(2,1)S(1)} %copy-done.14), channel_id=1, source_target_pairs={{0,80},{16,64},{32,112},{48,96},{64,16},{80,0},{96,48},{112,32},{1... | collective-permute-start | bytes 983048 | tf_op jit(solution)/shard_map/ppermute | solution.py:45
  63.3 23.6 %copy-start.4 = (bf16[2,8,80,128]{3,2,1,0:T(8,128)(2,1)}, bf16[2,8,80,128]{3,2,1,0:T(8,128)(2,1)S(1)}, u32[]{:S(2)}) copy-start(bf16[2,8,80,128]{3,2,1,0:T(8,128)(2,1)S(1)} %collective-permute-done.11.refs_4_) | copy-start | bytes 983044
  63.7 23.1 %copy-start.5 = (bf16[2,8,80,128]{3,2,1,0:T(8,128)(2,1)}, bf16[2,8,80,128]{3,2,1,0:T(8,128)(2,1)S(1)}, u32[]{:S(2)}) copy-start(bf16[2,8,80,128]{3,2,1,0:T(8,128)(2,1)S(1)} %collective-permute-done.12.refs_5_) | copy-start | bytes 983044
  69.6 17.2 %copy-start.6 = (bf16[2,8,80,128]{3,2,1,0:T(8,128)(2,1)}, bf16[2,8,80,128]{3,2,1,0:T(8,128)(2,1)S(1)}, u32[]{:S(2)}) copy-start(bf16[2,8,80,128]{3,2,1,0:T(8,128)(2,1)S(1)} %collective-permute-done.13.refs_6_) | copy-start | bytes 983044
  84.2 22.8 %collective-permute-start.18 = (bf16[160,2560]{1,0:T(8,128)(2,1)S(1)}, bf16[160,2560]{1,0:T(8,128)(2,1)}, u32[]{:S(2)}, u32[]{:S(2)}) collective-permute-start(bf16[160,2560]{1,0:T(8,128)(2,1)S(1)} %pad_maximum_fusion.refs_0_), channel_id=1, source_target_pairs={{0,64},{16,80},{32,96},{48,112},{64,0},{80,16},{96,32},{112,48},{1... | collective-permute-start | bytes 2457608 | tf_op jit(solution)/shard_map/ppermute | solution.py:45
  84.2 34.1 %collective-permute-start.17 = (bf16[160,2560]{1,0:T(8,128)(2,1)S(1)}, bf16[160,2560]{1,0:T(8,128)(2,1)}, u32[]{:S(2)}, u32[]{:S(2)}) collective-permute-start(bf16[160,2560]{1,0:T(8,128)(2,1)S(1)} %pad_maximum_fusion.refs_0_), channel_id=1, source_target_pairs={{0,96},{16,112},{32,0},{48,16},{64,32},{80,48},{96,64},{112,80},{1... | collective-permute-start | bytes 2457608 | tf_op jit(solution)/shard_map/ppermute | solution.py:45
  86.8 35.5 %collective-permute-start.16 = (bf16[160,2560]{1,0:T(8,128)(2,1)S(1)}, bf16[160,2560]{1,0:T(8,128)(2,1)S(1)}, u32[]{:S(2)}, u32[]{:S(2)}) collective-permute-start(bf16[160,2560]{1,0:T(8,128)(2,1)S(1)} %pad_maximum_fusion.refs_0_), channel_id=1, source_target_pairs={{0,32},{16,48},{32,64},{48,80},{64,96},{80,112},{96,0},{112,16},{1... | collective-permute-start | bytes 2457608 | tf_op jit(solution)/shard_map/ppermute | solution.py:45
  99.9 26.9 %all-to-all-start.2 = ((bf16[16,400,128]{2,1,0:T(8,128)(2,1)}), bf16[16,400,128]{2,1,0:T(8,128)(2,1)S(1)}, u32[]{:S(2)}, u32[]{:S(2)}) async-start(bf16[16,400,128]{2,1,0:T(8,128)(2,1)} %bitcast.8), calls=%async_computation.2 | async-start | bytes 3276800 | tf_op jit(solution)/shard_map/all_to_all | solution.py:364
  103.7 18.6 %collective-permute-start.19 = (bf16[160,2560]{1,0:T(8,128)(2,1)S(1)}, bf16[160,2560]{1,0:T(8,128)(2,1)}, u32[]{:S(2)}, u32[]{:S(2)}) collective-permute-start(bf16[160,2560]{1,0:T(8,128)(2,1)S(1)} %pad_maximum_fusion.refs_0_), channel_id=1, source_target_pairs={{0,16},{16,0},{32,48},{48,32},{64,80},{80,64},{96,112},{112,96},{1... | collective-permute-start | bytes 2457608 | tf_op jit(solution)/shard_map/ppermute | solution.py:344
  107.0 19.8 %collective-permute-start.22 = (bf16[160,2560]{1,0:T(8,128)(2,1)}, bf16[160,2560]{1,0:T(8,128)(2,1)}, u32[]{:S(2)}, u32[]{:S(2)}) collective-permute-start(bf16[160,2560]{1,0:T(8,128)(2,1)} %collective-permute-done.18.refs_3_), channel_id=1, source_target_pairs={{0,16},{16,0},{32,48},{48,32},{64,80},{80,64},{96,112},{112,96},{1... | collective-permute-start | bytes 2457608 | tf_op jit(solution)/shard_map/ppermute | solution.py:344
  118.3 8.5 %collective-permute-start.21 = (bf16[160,2560]{1,0:T(8,128)(2,1)}, bf16[160,2560]{1,0:T(8,128)(2,1)}, u32[]{:S(2)}, u32[]{:S(2)}) collective-permute-start(bf16[160,2560]{1,0:T(8,128)(2,1)} %collective-permute-done.17.refs_2_), channel_id=1, source_target_pairs={{0,16},{16,0},{32,48},{48,32},{64,80},{80,64},{96,112},{112,96},{1... | collective-permute-start | bytes 2457608 | tf_op jit(solution)/shard_map/ppermute | solution.py:344
  122.3 4.5 %collective-permute-start.20 = (bf16[160,2560]{1,0:T(8,128)(2,1)S(1)}, bf16[160,2560]{1,0:T(8,128)(2,1)}, u32[]{:S(2)}, u32[]{:S(2)}) collective-permute-start(bf16[160,2560]{1,0:T(8,128)(2,1)S(1)} %collective-permute-done.16.refs_1_), channel_id=1, source_target_pairs={{0,16},{16,0},{32,48},{48,32},{64,80},{80,64},{96,112},{112,96},{1... | collective-permute-start | bytes 2457608 | tf_op jit(solution)/shard_map/ppermute | solution.py:344
  126.8 1.2 copy-start
  (1 other events, 0.6 us)

commit v4 on v3

--- a/solution.py
+++ b/solution.py
@@ -19,6 +19,7 @@
 PAIRS = 5
 LENT = (0, 2, 3, 4)
 UNITS = 3 * PAIRS + 2 * WIN
+BLOCKS = 4
 AHEAD = 2
 STEPS = ((0, 0), (0, 1), (1, 0), (3, 0), (2, 0), (1, 1), (3, 1), (2, 1))
 VMEM = pl.BlockSpec(memory_space=pltpu.VMEM)
@@ -58,11 +59,20 @@
     return place
 
 
-def pack_slots(window, span_slot, cache_keys, cache_values, by_head, *refs):
-    rest, held, held_sems, sems = refs[:GROUPS], *refs[GROUPS:]
+def pack_slots(window, span_slot, cache_keys, cache_values, out_weight, by_head, *refs):
+    rest, lent = refs[:GROUPS], refs[GROUPS : GROUPS + 2]
+    held, lent_held, held_sems, sems = refs[GROUPS + 2 :]
     me = lax.axis_index("cache")
+    rows, columns = lent[0].shape
+    column = pl.multiple_of((1 - lax.axis_index("head")) * columns, HD)
     for kv, source in enumerate((cache_keys, cache_values)):
         pltpu.make_async_copy(source, held.at[kv], held_sems.at[kv]).start()
+    loads = []
+    for part in range(2):
+        row = pl.multiple_of((2 * me + part) * rows, 16)
+        source = out_weight.at[pl.ds(row, rows), pl.ds(column, columns)]
+        loads.append(pltpu.make_async_copy(source, lent_held.at[part], held_sems.at[2 + part]))
+        loads[part].start()
     for kv, source in enumerate((cache_keys, cache_values)):
         pltpu.make_async_copy(source, held.at[kv], held_sems.at[kv]).wait()
     for head in range(SPACE):
@@ -72,23 +82,21 @@
         slot = picked(window, span_slot, goes_to(me, step), me)
         source = held.at[:, slot, :, pl.ds(WIDE, 2 * HD)]
         pltpu.make_async_copy(source, rest[step], sems.at[1 + step]).start()
+    for part in range(2):
+        loads[part].wait()
+        pltpu.make_async_copy(lent_held.at[part], lent[part], sems.at[1 + GROUPS + part]).start()
     wait_for(by_head, sems.at[0])
+    for part in range(2):
+        wait_for(lent[part], sems.at[1 + GROUPS + part])
     for step in range(GROUPS):
         wait_for(rest[step], sems.at[1 + step])
 
 
-def pack_pairs(queries, keys, values, out_weight, sent, *refs):
-    lent, held, rows_held, held_sems, sems = refs[:2], *refs[2:]
-    rows, columns = lent[0].shape
-    column = pl.multiple_of((1 - lax.axis_index("head")) * columns, HD)
+def pack_pairs(queries, keys, values, sent, held, held_sems, sems):
     loads = [
         pltpu.make_async_copy(source, held.at[kind], held_sems.at[kind])
         for kind, source in enumerate((queries, keys, values))
     ]
-    for part in range(2):
-        row = pl.multiple_of((2 * lax.axis_index("cache") + part) * rows, 16)
-        source = out_weight.at[pl.ds(row, rows), pl.ds(column, columns)]
-        loads.append(pltpu.make_async_copy(source, rows_held.at[part], held_sems.at[3 + part]))
     for load in loads:
         load.start()
     for kind in range(3):
@@ -101,13 +109,8 @@
             pltpu.make_async_copy(
                 held.at[kind, to // 2, :, last], sent.at[to, kind * PAIRS + SPANS], sems.at[kind]
             ).start()
-    for part in range(2):
-        loads[3 + part].wait()
-        pltpu.make_async_copy(rows_held.at[part], lent[part], sems.at[3 + part]).start()
     for kind in range(3):
         wait_for(sent.at[:, pl.ds(kind * PAIRS, PAIRS)], sems.at[kind])
-    for part in range(2):
-        wait_for(lent[part], sems.at[3 + part])
 
 
 def pack_cached(window, span_slot, by_head, *refs):
@@ -143,67 +146,102 @@
 
 def attend(window, span_slot, counts, *refs):
     came, wide = refs[0], refs[1 : 1 + GROUPS]
-    out, own, sent, k_all, v_all, done, ready, left = refs[1 + GROUPS :]
+    out, q_all, k_all, v_all, sent, ready, left = refs[1 + GROUPS :]
     group = lax.axis_index("cache")
     me = lax.axis_index("space")
     factor = math.log2(math.e) / math.sqrt(HD)
-    spots = lax.broadcasted_iota(jnp.int32, (SPAN, HD), 0)
-    v_all[0:SPAN, HD:] = jnp.ones((SPAN, HD), jnp.bfloat16)
-
-    def fetch(pair, source, target):
-        pltpu.make_async_copy(source, target, ready.at[pair]).start()
+
+    def fetch(pair, kind, source, target):
+        pltpu.make_async_copy(source, target, ready.at[pair, kind]).start()
+
+    def share(pair, kind, segment):
+        if kind == 0:
+            return q_all.at[pair]
+        chunks = pl.ds(segment * SPACE, SPACE)
+        if kind == 1:
+            return k_all.at[pair, chunks]
+        return v_all.at[pair, chunks, :, pl.ds(0, HD)]
 
     def fetch_pair(pair):
         for kind in range(3):
-            fetch(pair, came.at[:, kind * PAIRS + pair], own.at[pair, kind])
+            fetch(pair, kind, came.at[:, kind * PAIRS + pair], share(pair, kind, 0))
+
+    def fetch_wide(step, place):
+        pair, segment = place >> 1, 1 + (place & 1)
+        for kv in range(2):
+            fetch(pair, 1 + kv, wide[step].at[kv], share(pair, 1 + kv, segment))
 
     fetch_pair(0)
+    places = []
     for step in range(GROUPS):
         owner = came_from(group, step)
         place = jnp.int32(0)
         for entry in range(SPANS * WIN):
             slot = span_slot[window[entry % 2, group * SPANS + entry // 2]]
             place = jnp.where((slot >> 1) == owner, entry, place)
-        fetch(place >> 1, wide[step], own.at[place >> 1, pl.ds(3 + 2 * (place & 1), 2)])
+        places.append(place)
+        pl.when(place < WIN)(lambda: fetch_wide(step, place))
+    v_all[:, :, :, HD:] = jnp.ones((PAIRS, 3 * SPACE, ROWS, HD), jnp.bfloat16)
+
+    def prepare(pair):
+        for kind in range(3):
+            wait_for(q_all.at[pair] if kind == 0 else k_all.at[pair], ready.at[pair, kind])
+        span = me >> 1 if pair == SPANS else pair
+        for w in range(WIN):
+            limit = counts[window[w, group * SPANS + span]]
+            first = (1 + w) * SPACE
+            half = slice(first + SPACE // 2, first + SPACE)
+            extent = (SPACE // 2, ROWS, HD)
+            spots = SPAN // 2 + lax.broadcasted_iota(jnp.int32, extent, 1)
+            valid = spots + ROWS * lax.broadcasted_iota(jnp.int32, extent, 0) < limit
+            key = k_all[pair, first, 0:1].astype(jnp.float32)
+            key = jnp.broadcast_to(key[None], extent)
+            held = k_all[pair, half].astype(jnp.float32)
+            k_all[pair, half] = jnp.where(valid, held, key).astype(jnp.bfloat16)
+            held = v_all[pair, half, :, 0:HD].astype(jnp.float32)
+            v_all[pair, half, :, 0:HD] = jnp.where(valid, held, 0.0).astype(jnp.bfloat16)
+            v_all[pair, half, :, HD:] = jnp.where(valid, 1.0, 0.0).astype(jnp.bfloat16)
+
+    block = SPACE // BLOCKS
+
+    def score(pair, part):
+        query = q_all[pair, part * block : (part + 1) * block].reshape(block * ROWS, HD)
+        key = k_all[pair].reshape(3 * SPAN, HD)
+        return lax.dot_general(
+            query, key, (((1,), (1,)), ((), ())), preferred_element_type=jnp.float32
+        )
+
+    def finish(pair, part, scores):
+        top = jnp.max(scores, axis=1, keepdims=True)
+        weights = jnp.exp2((scores - top) * factor).astype(jnp.bfloat16)
+        value = v_all[pair].reshape(3 * SPAN, 2 * HD)
+        both = jnp.dot(weights, value, preferred_element_type=jnp.float32)
+        done = (both[:, 0:HD] / both[:, HD:]).astype(jnp.bfloat16).reshape(block, ROWS, HD)
+        for place in range(block):
+            for half in range(2):
+                sent[2 * (part * block + place) + half, pair] = done[place]
+
+    steps = [(pair, part) for pair in range(PAIRS) for part in range(BLOCKS)]
+    prepare(0)
+    for step, place in enumerate(places):
+        pl.when(place >= WIN)(lambda: fetch_wide(step, place))
     for pair in range(1, PAIRS):
         fetch_pair(pair)
-    for unit in range(2 * WIN):
-        fetch(SPANS, came.at[:, 3 * PAIRS + unit], own.at[SPANS, 3 + unit])
-
-    @pl.loop(0, PAIRS)
-    def _(pair):
-        pltpu.make_async_copy(own.at[pair], own.at[pair], ready.at[pair]).wait()
-        span = jnp.where(pair < SPANS, pair, me >> 1)
-        k_all[0:SPAN] = own[pair, 1].reshape(SPAN, HD)
-        v_all[0:SPAN, 0:HD] = own[pair, 2].reshape(SPAN, HD)
-        for w in range(WIN):
-            limit = counts[window[w, group * SPANS + span]]
-            part = slice((1 + w) * SPAN, (2 + w) * SPAN)
-            valid = spots < limit
-            held = own[pair, 3 + 2 * w].reshape(SPAN, HD).astype(jnp.float32)
-            first = jnp.broadcast_to(held[0:1], (SPAN, HD))
-            k_all[part] = jnp.where(valid, held, first).astype(jnp.bfloat16)
-            held = own[pair, 4 + 2 * w].reshape(SPAN, HD).astype(jnp.float32)
-            v_all[part, 0:HD] = jnp.where(valid, held, 0.0).astype(jnp.bfloat16)
-            v_all[part, HD:] = jnp.where(valid, 1.0, 0.0).astype(jnp.bfloat16)
-        share = SPACE // 2
-        block = share * ROWS
-        for first in range(0, SPACE, share):
-            start = first * ROWS
-            scores = lax.dot_general(
-                own[pair, 0, first : first + share].reshape(block, HD),
-                k_all[...],
-                (((1,), (1,)), ((), ())),
-                preferred_element_type=jnp.float32,
-            )
-            top = jnp.max(scores, axis=1, keepdims=True)
-            weights = jnp.exp2((scores - top) * factor).astype(jnp.bfloat16)
-            both = jnp.dot(weights, v_all[...], preferred_element_type=jnp.float32)
-            done[start : start + block] = (both[:, 0:HD] / both[:, HD:]).astype(jnp.bfloat16)
-        for step in range(SPACE):
-            for half in range(2):
-                sent[2 * step + half, pair] = done[step * ROWS : (step + 1) * ROWS]
-        pltpu.make_async_copy(sent.at[:, pair], out.at[:, pair], left.at[pair]).start()
+    for w in range(WIN):
+        for kv in range(2):
+            source = came.at[:, 3 * PAIRS + 2 * w + kv]
+            fetch(SPANS, 1 + kv, source, share(SPANS, 1 + kv, 1 + w))
+    scores = score(0, 0)
+    for now, later in zip(steps, steps[1:] + [None]):
+        held = scores
+        if later is not None:
+            if later[1] == 0:
+                prepare(later[0])
+            scores = score(*later)
+        finish(*now, held)
+        if now[1] == BLOCKS - 1:
+            pair = now[0]
+            pltpu.make_async_copy(sent.at[:, pair], out.at[:, pair], left.at[pair]).start()
 
     for pair in range(PAIRS):
         pltpu.make_async_copy(sent.at[:, pair], out.at[:, pair], left.at[pair]).wait()
@@ -279,46 +317,46 @@
     rows = depth // GROUPS // 2
     window = window.T
 
-    by_head, *rest = pl.pallas_call(
+    by_head, *sent = pl.pallas_call(
         pack_slots,
         out_shape=[shape((SPACE, 2, 2, ROWS, HD), bf16)]
-        + [shape((2, ROWS, 2 * HD), bf16)] * GROUPS,
-        in_specs=[SMEM] * 2 + [HBM] * 2,
-        out_specs=[HBM] * (1 + GROUPS),
+        + [shape((2, ROWS, 2 * HD), bf16)] * GROUPS
+        + [shape((rows, columns), bf16)] * 2,
+        in_specs=[SMEM] * 2 + [HBM] * 3,
+        out_specs=[HBM] * (3 + GROUPS),
         scratch_shapes=[
             pltpu.VMEM((2, 2, ROWS, HEADS * HD), bf16),
-            pltpu.SemaphoreType.DMA((2,)),
-            pltpu.SemaphoreType.DMA((1 + GROUPS,)),
+            pltpu.VMEM((2, rows, columns), bf16),
+            pltpu.SemaphoreType.DMA((4,)),
+            pltpu.SemaphoreType.DMA((3 + GROUPS,)),
         ],
         compiler_params=params(60),
         name="pack_slots",
-    )(window, span_slot, cache_keys, cache_values)
-    by_head, *rest, queries = lax.optimization_barrier((by_head, *rest, queries))
+    )(window, span_slot, cache_keys, cache_values, out_weight)
+    by_head, *sent, queries = lax.optimization_barrier((by_head, *sent, queries))
+    rest, lent = sent[:GROUPS], sent[GROUPS:]
     by_head = lax.all_to_all(
         by_head.reshape(SPACE, 4 * ROWS, HD), "space", split_axis=0, concat_axis=0, tiled=True
     ).reshape(by_head.shape)
     rest = [rest[0]] + [shift(rest[step], "cache", step) for step in range(1, GROUPS)]
-
-    pairs, *lent = pl.pallas_call(
-        pack_pairs,
-        out_shape=[shape((SPACE, UNITS, ROWS, HD), bf16)] + [shape((rows, columns), bf16)] * 2,
-        in_specs=[HBM] * 4,
-        out_specs=[HBM] * 3,
-        scratch_shapes=[
-            pltpu.VMEM((3, SPANS, ROWS, HEADS * HD), bf16),
-            pltpu.VMEM((2, rows, columns), bf16),
-            pltpu.SemaphoreType.DMA((5,)),
-            pltpu.SemaphoreType.DMA((5,)),
-        ],
-        compiler_params=params(60),
-        name="pack_pairs",
-    )(queries, keys, values, out_weight)
     lent = [
         lax.ppermute(lent[0], "head", [(0, 1), (1, 0)]),
         lax.ppermute(lent[1], ("space", "head"), [(i, i ^ 3) for i in range(2 * SPACE)]),
     ]
-    lent = jnp.concatenate(lent, 0)
-    by_head, lent, *rest = lax.optimization_barrier((by_head, lent, *rest))
+    pairs = pl.pallas_call(
+        pack_pairs,
+        out_shape=shape((SPACE, UNITS, ROWS, HD), bf16),
+        in_specs=[HBM] * 3,
+        out_specs=HBM,
+        scratch_shapes=[
+            pltpu.VMEM((3, SPANS, ROWS, HEADS * HD), bf16),
+            pltpu.SemaphoreType.DMA((3,)),
+            pltpu.SemaphoreType.DMA((3,)),
+        ],
+        compiler_params=params(60),
+        name="pack_pairs",
+    )(queries, keys, values)
+    by_head, *rest = lax.optimization_barrier((by_head, *rest))
     pairs, *wide = pl.pallas_call(
         pack_cached,
         out_shape=[shape(pairs.shape, bf16)] + [shape((2, SPACE, ROWS, HD), bf16)] * GROUPS,
@@ -335,11 +373,13 @@
         compiler_params=params(60),
         name="pack_cached",
     )(window, span_slot, by_head, *rest, pairs)
+    pairs, *lent = lax.optimization_barrier((pairs, *lent))
     came = lax.all_to_all(
         pairs.reshape(SPACE, UNITS * ROWS, HD), "space", split_axis=0, concat_axis=0, tiled=True
     ).reshape(pairs.shape)
     wide = [wide[0]] + [shift(wide[step], "cache", step) for step in range(1, GROUPS)]
-    came, lent, *wide = lax.optimization_barrier((came, lent, *wide))
+    lent = jnp.concatenate(lent, 0)
+    lent, *wide = lax.optimization_barrier((lent, *wide))
     lent = [lent] + [shift(lent, "cache", step) for step in LENT[1:]]
     lent += [lax.ppermute(chunk, "cache", [(i, i ^ 1) for i in range(8)]) for chunk in lent]
 
@@ -349,12 +389,11 @@
         in_specs=[SMEM] * 3 + [HBM] * (1 + GROUPS),
         out_specs=HBM,
         scratch_shapes=[
-            pltpu.VMEM((PAIRS, 3 + 2 * WIN, SPACE, ROWS, HD), bf16),
+            pltpu.VMEM((PAIRS, SPACE, ROWS, HD), bf16),
+            pltpu.VMEM((PAIRS, 3 * SPACE, ROWS, HD), bf16),
+            pltpu.VMEM((PAIRS, 3 * SPACE, ROWS, 2 * HD), bf16),
             pltpu.VMEM((2 * SPACE, PAIRS, ROWS, HD), bf16),
-            pltpu.VMEM((3 * SPAN, HD), bf16),
-            pltpu.VMEM((3 * SPAN, 2 * HD), bf16),
-            pltpu.VMEM((SPAN, HD), bf16),
-            pltpu.SemaphoreType.DMA((PAIRS,)),
+            pltpu.SemaphoreType.DMA((PAIRS, 3)),
             pltpu.SemaphoreType.DMA((PAIRS,)),
         ],
         compiler_params=params(60),

time: 137 us -> 133 us (0.971)
  waiting for transfers between devices: 62.3 us -> 57 us
    ppermute x17, waiting for transfers between devices: 49.4 us -> 43.9 us  [shift(): return lax.ppermute(x, axis, [(i, goes_to(i, step)) for i in range(8)])]
    all_to_all x1, starting transfers between devices: 7.99 us -> 4.59 us  [on_device(): lax.all_to_all(pairs.reshape(SPACE, UNITS * ROWS, HD), 'space', split_axi...]
    all_to_all x1, waiting for transfers between devices: 7.24 us -> 3.85 us  [on_device(): lax.all_to_all(pairs.reshape(SPACE, UNITS * ROWS, HD), 'space', split_axi...]
    all_to_all x1, waiting for transfers between devices: 4.47 us -> 7.79 us  [on_device(): lax.all_to_all(attended, ('space', 'head'), split_axis=0, concat_axis=0,...]
    all_to_all x1, starting transfers between devices: 5.47 us -> 8.04 us  [on_device(): lax.all_to_all(by_head.reshape(SPACE, 4 * ROWS, HD), 'space', split_axis=...]
    ppermute x4, starting transfers between devices: 0.11 us -> 1.82 us  [on_device(): lax.ppermute(chunk, 'cache', [(i, i ^ 1) for i in range(8)])]
    ppermute x4, waiting for transfers between devices: 0.01 us -> 1.52 us  [on_device(): lax.ppermute(chunk, 'cache', [(i, i ^ 1) for i in range(8)])]
    unnamed x46 -> x42, local copies, waits for them, and re-layouts: 2.05 us -> 2.98 us
  transfers between devices with their start and end apart: 26 -> 26, of which waited for: 14 -> 13; matrix products, arithmetic and copies ran while one was open for 0% -> 0% of each run, Pallas kernels for 10% -> 14%
where the time goes in v4:
time: 133 us; the launch traced here: 132 us
  waiting for transfers between devices  57 us (43%)
  starting transfers between devices  41.9 us (32%)
  Pallas kernels  30 us (23%)
  local copies, waits for them, and re-layouts  2.98 us (2%)
    ppermute x17, waiting for transfers between devices, shift(): return lax.ppermute(x, axis, [(i, goes_to(i, step)) for i in range(8)])  43.9 us
    ppermute x17, starting transfers between devices, shift(): return lax.ppermute(x, axis, [(i, goes_to(i, step)) for i in range(8)])  19.7 us
    pallas_call x1, Pallas kernels, on_device(): pl.pallas_call(attend, out_shape=shape((2 * SPACE, PAIRS, ROWS, HD), bf16...  12.2 us
    pallas_call x1, Pallas kernels, on_device(): pl.pallas_call(project, out_shape=shape((SPANS * ROWS, columns), bf16), i...  8.25 us
    all_to_all x1, starting transfers between devices, on_device(): lax.all_to_all(by_head.reshape(SPACE, 4 * ROWS, HD), 'space', split_axis=...  8.04 us
    all_to_all x1, waiting for transfers between devices, on_device(): lax.all_to_all(attended, ('space', 'head'), split_axis=0, concat_axis=0,...  7.79 us
    all_to_all x1, starting transfers between devices, on_device(): lax.all_to_all(pairs.reshape(SPACE, UNITS * ROWS, HD), 'space', split_axi...  4.59 us
    all_to_all x1, waiting for transfers between devices, on_device(): lax.all_to_all(pairs.reshape(SPACE, UNITS * ROWS, HD), 'space', split_axi...  3.85 us
  transfers between devices with their start and end apart: 26, of which 13 were waited for; matrix products, arithmetic and copies ran while one was open for 0% of the time, Pallas kernels for 14%

profile of v4, /device:TPU:0, one launch (start us, length us, event | category | flops | bytes accessed | tf_op | source)
XLA Modules:
  0.0 132.5 jit_solution(7088500427211696993)
XLA Ops:
  0.0 3.3 %pack_slots.1 = (bf16[8,2,2,80,128]{4,3,2,1,0:T(8,128)(2,1)}, bf16[2,80,256]{2,1,0:T(8,128)(2,1)}, bf16[2,80,256]{2,1,0:T(8,128)(2,1)}, bf16[2,80,256]{2,1,0:T(8...) custom-call(s32[2,32]{1,0:T(2,128)} %bitcast.11, ...), custom_call_target="tpu_custom_call" | custom-call | tf_op jit(solution)/shard_map/pack_slots/pallas_call | solution.py:320
  3.3 8.0 %all-to-all-start = ((bf16[8,320,128]{2,1,0:T(8,128)(2,1)}), bf16[8,320,128]{2,1,0:T(8,128)(2,1)S(1)}, u32[]{:S(2)}, u32[]{:S(2)}) async-start(bf16[8,320,128]{2,1,0:T(8,128)(2,1)} %bitcast.10), calls=%async_computation | async-start | bytes 1310720 | tf_op jit(solution)/shard_map/all_to_all | solution.py:338
  11.3 0.7 collective-permute-start.7
  12.0 3.4 %collective-permute-start.8 = (bf16[80,2560]{1,0:T(8,128)(2,1)}, bf16[80,2560]{1,0:T(8,128)(2,1)S(1)}, u32[]{:S(2)}, u32[]{:S(2)}) collective-permute-start(bf16[80,2560]{1,0:T(8,128)(2,1)} %get-tuple-element.90), channel_id=1, source_target_pairs={{0,3},{1,2},{2,1},{3,0},{4,7},{5,6},{6,5},{7,4},{8,11},{9,10},{10,... | collective-permute-start | bytes 1228808 | tf_op jit(solution)/shard_map/ppermute | solution.py:344
  15.4 0.0 collective-permute-start
  15.4 1.5 %collective-permute-start.1 = (bf16[2,80,256]{2,1,0:T(8,128)(2,1)}, bf16[2,80,256]{2,1,0:T(8,128)(2,1)S(1)}, u32[]{:S(2)}, u32[]{:S(2)}) collective-permute-start(bf16[2,80,256]{2,1,0:T(8,128)(2,1)} %get-tuple-element.72), channel_id=1, source_target_pairs={{0,32},{16,48},{32,64},{48,80},{64,96},{80,112},{96,0},{112,16},{1... | collective-permute-start | bytes 245768 | tf_op jit(solution)/shard_map/ppermute | solution.py:46
  16.9 1.7 %collective-permute-start.2 = (bf16[2,80,256]{2,1,0:T(8,128)(2,1)}, bf16[2,80,256]{2,1,0:T(8,128)(2,1)S(1)}, u32[]{:S(2)}, u32[]{:S(2)}) collective-permute-start(bf16[2,80,256]{2,1,0:T(8,128)(2,1)} %get-tuple-element.73), channel_id=1, source_target_pairs={{0,96},{16,112},{32,0},{48,16},{64,32},{80,48},{96,64},{112,80},{1... | collective-permute-start | bytes 245768 | tf_op jit(solution)/shard_map/ppermute | solution.py:46
  18.7 0.0 collective-permute-done.refs_1_
  18.7 1.8 %collective-permute-start.3 = (bf16[2,80,256]{2,1,0:T(8,128)(2,1)}, bf16[2,80,256]{2,1,0:T(8,128)(2,1)S(1)}, u32[]{:S(2)}, u32[]{:S(2)}) collective-permute-start(bf16[2,80,256]{2,1,0:T(8,128)(2,1)} %get-tuple-element.74), channel_id=1, source_target_pairs={{0,64},{16,80},{32,96},{48,112},{64,0},{80,16},{96,32},{112,48},{1... | collective-permute-start | bytes 245768 | tf_op jit(solution)/shard_map/ppermute | solution.py:46
  20.5 1.2 collective-permute-done.1.refs_2_
  21.7 0.0 collective-permute-start.4
  21.7 2.9 %collective-permute-start.5 = (bf16[2,80,256]{2,1,0:T(8,128)(2,1)}, bf16[2,80,256]{2,1,0:T(8,128)(2,1)S(1)}, u32[]{:S(2)}, u32[]{:S(2)}) collective-permute-start(bf16[2,80,256]{2,1,0:T(8,128)(2,1)} %get-tuple-element.76), channel_id=1, source_target_pairs={{0,112},{16,96},{32,16},{48,0},{64,48},{80,32},{96,80},{112,64},{1... | collective-permute-start | bytes 245768 | tf_op jit(solution)/shard_map/ppermute | solution.py:46
  24.7 0.2 collective-permute-done.3.refs_4_
  24.8 0.5 collective-permute-start.6
  25.3 2.6 %pack_pairs.1.refs_8_ = bf16[8,19,80,128]{3,2,1,0:T(8,128)(2,1)} custom-call(bf16[4,80,1280]{2,1,0:T(8,128)(2,1)} %queries, bf16[4,80,1280]{2,1,0:T(8,128)(2,1)} %keys.1, bf16[4,80,1280]{2,1,0:T(8,128)(2,1)} %values.1), custom_call_target="tpu_custom_call" | custom-call | tf_op jit(solution)/shard_map/pack_pairs/pallas_call | solution.py:346
  28.1 2.3 %collective-permute-done.6.refs_7_ = bf16[2,80,256]{2,1,0:T(8,128)(2,1)S(1)} collective-permute-done((bf16[2,80,256]{2,1,0:T(8,128)(2,1)}, bf16[2,80,256]{2,1,0:T(8,128)(2,1)S(1)}, u32[]{:S(2)}, u32[]{:S(2)}) %collective-permute-start.6) | collective-permute-done | bytes 81952 | tf_op jit(solution)/shard_map/ppermute | solution.py:46
  30.4 0.6 copy-done.18
  31.0 0.2 copy-done.1
  31.3 3.6 %pack_cached.1 = (bf16[8,19,80,128]{3,2,1,0:T(8,128)(2,1)}, bf16[2,8,80,128]{3,2,1,0:T(8,128)(2,1)}, bf16[2,8,80,128]{3,2,1,0:T(8,128)(2,1)}, bf16[2,8,80,128]{3...) custom-call(s32[2,32]{1,0:T(2,128)} %bitcast.12, ...), custom_call_target="tpu_custom_call", output_to_operand_aliasing={{0}: (11, {})} | custom-call | tf_op jit(solution)/shard_map/pack_cached/pallas_call | solution.py:360
  35.0 4.6 %all-to-all-start.1 = ((bf16[8,1520,128]{2,1,0:T(8,128)(2,1)}), bf16[8,1520,128]{2,1,0:T(8,128)(2,1)}, u32[]{:S(2)}, u32[]{:S(2)}) async-start(bf16[8,1520,128]{2,1,0:T(8,128)(2,1)} %bitcast.7), calls=%async_computation.1 | async-start | bytes 6225920 | tf_op jit(solution)/shard_map/all_to_all | solution.py:377
  39.6 1.3 collective-permute-start.9
  40.8 0.2 collective-permute-start.10
  41.1 3.0 %collective-permute-start.11 = (bf16[2,8,80,128]{3,2,1,0:T(8,128)(2,1)}, bf16[2,8,80,128]{3,2,1,0:T(8,128)(2,1)S(1)}, u32[]{:S(2)}, u32[]{:S(2)}) collective-permute-start(bf16[2,8,80,128]{3,2,1,0:T(8,128)(2,1)} %get-tuple-element.97), channel_id=1, source_target_pairs={{0,96},{16,112},{32,0},{48,16},{64,32},{80,48},{96,64},{112,80},{1... | collective-permute-start | bytes 983048 | tf_op jit(solution)/shard_map/ppermute | solution.py:46
  44.1 0.5 collective-permute-start.13
  44.6 2.4 %collective-permute-start.14 = (bf16[2,8,80,128]{3,2,1,0:T(8,128)(2,1)}, bf16[2,8,80,128]{3,2,1,0:T(8,128)(2,1)S(1)}, u32[]{:S(2)}, u32[]{:S(2)}) collective-permute-start(bf16[2,8,80,128]{3,2,1,0:T(8,128)(2,1)} %get-tuple-element.100), channel_id=1, source_target_pairs={{0,112},{16,96},{32,16},{48,0},{64,48},{80,32},{96,80},{112,64},{1... | collective-permute-start | bytes 983048 | tf_op jit(solution)/shard_map/ppermute | solution.py:46
  47.0 12.6 %collective-permute-done.10.refs_3_ = bf16[2,8,80,128]{3,2,1,0:T(8,128)(2,1)S(1)} collective-permute-done((bf16[2,8,80,128]{3,2,1,0:T(8,128)(2,1)S(1)}, bf16[2,8,80,128]{3,2,1,0:T(8,128)(2,1)S(1)}, u32[]{:S(2)}, u32[]{:S(2)}) %collective-permute-start.10) | collective-permute-done | bytes 327712 | tf_op jit(solution)/shard_map/ppermute | solution.py:46
  59.6 0.1 pad_maximum_fusion.refs_0_
  59.7 5.2 %collective-permute-done.13.refs_6_ = bf16[2,8,80,128]{3,2,1,0:T(8,128)(2,1)S(1)} collective-permute-done((bf16[2,8,80,128]{3,2,1,0:T(8,128)(2,1)}, bf16[2,8,80,128]{3,2,1,0:T(8,128)(2,1)S(1)}, u32[]{:S(2)}, u32[]{:S(2)}) %collective-permute-start.13) | collective-permute-done | bytes 327712 | tf_op jit(solution)/shard_map/ppermute | solution.py:46
  64.9 7.5 %collective-permute-done.14.refs_7_ = bf16[2,8,80,128]{3,2,1,0:T(8,128)(2,1)S(1)} collective-permute-done((bf16[2,8,80,128]{3,2,1,0:T(8,128)(2,1)}, bf16[2,8,80,128]{3,2,1,0:T(8,128)(2,1)S(1)}, u32[]{:S(2)}, u32[]{:S(2)}) %collective-permute-start.14) | collective-permute-done | bytes 327712 | tf_op jit(solution)/shard_map/ppermute | solution.py:46
  72.4 0.2 collective-permute-done.15.refs_8_
  72.7 0.6 collective-permute-start.18
  73.3 3.1 %collective-permute-start.17 = (bf16[160,2560]{1,0:T(8,128)(2,1)S(1)}, bf16[160,2560]{1,0:T(8,128)(2,1)}, u32[]{:S(2)}, u32[]{:S(2)}) collective-permute-start(bf16[160,2560]{1,0:T(8,128)(2,1)S(1)} %pad_maximum_fusion.refs_0_), channel_id=1, source_target_pairs={{0,96},{16,112},{32,0},{48,16},{64,32},{80,48},{96,64},{112,80},{1... | collective-permute-start | bytes 2457608 | tf_op jit(solution)/shard_map/ppermute | solution.py:46
  76.4 0.0 collective-permute-start.16
  76.4 3.9 %all-to-all-done.1 = bf16[8,1520,128]{2,1,0:T(8,128)(2,1)} async-done(((bf16[8,1520,128]{2,1,0:T(8,128)(2,1)}), bf16[8,1520,128]{2,1,0:T(8,128)(2,1)}, u32[]{:S(2)}, u32[]{:S(2)}) %all-to-all-start.1) | async-done | bytes 3112992 | tf_op jit(solution)/shard_map/all_to_all | solution.py:377
  80.3 12.2 %attend.1 = bf16[16,5,80,128]{3,2,1,0:T(8,128)(2,1)} custom-call(s32[2,32]{1,0:T(2,128)} %bitcast.13, s32[16]{0:T(128)} %span_slot.5, s32[16]{0:T(128)} %counts.1, bf16[8,19,80,128]{3,2,1,0:T(8,128)(2,1)} %bitcast.4.refs_0_, bf16[2,8,80,128]{3,2,1,0:T(8,128)(2,1)} %get-tuple-element.102.refs_1_, bf16[2,8,80,128]{3,2,1,0:T(8,128)(2,1)} %copy-done.5, ...), custom_call_target="tpu_custom_call" | custom-call | tf_op jit(solution)/shard_map/attend/pallas_call | solution.py:386
  92.5 3.7 %all-to-all-start.2 = ((bf16[16,400,128]{2,1,0:T(8,128)(2,1)}), bf16[16,400,128]{2,1,0:T(8,128)(2,1)S(1)}, u32[]{:S(2)}, u32[]{:S(2)}) async-start(bf16[16,400,128]{2,1,0:T(8,128)(2,1)} %bitcast.8), calls=%async_computation.2 | async-start | bytes 3276800 | tf_op jit(solution)/shard_map/all_to_all | solution.py:403
  96.2 0.2 collective-permute-start.19
  96.4 0.4 collective-permute-start.22
  96.8 13.8 %collective-permute-done.17.refs_2_ = bf16[160,2560]{1,0:T(8,128)(2,1)} collective-permute-done((bf16[160,2560]{1,0:T(8,128)(2,1)S(1)}, bf16[160,2560]{1,0:T(8,128)(2,1)}, u32[]{:S(2)}, u32[]{:S(2)}) %collective-permute-start.17) | collective-permute-done | bytes 819232 | tf_op jit(solution)/shard_map/ppermute | solution.py:46
  110.6 1.2 collective-permute-start.21
  111.8 0.8 collective-permute-done.16.refs_1_
  112.6 0.1 collective-permute-start.20
  112.6 1.3 collective-permute-done.21.refs_6_
  114.0 0.9 copy-done.4
  114.9 0.2 collective-permute-done.20.refs_5_
  115.1 7.8 %all-to-all-done.2.came = bf16[16,400,128]{2,1,0:T(8,128)(2,1)S(1)} async-done(((bf16[16,400,128]{2,1,0:T(8,128)(2,1)}), bf16[16,400,128]{2,1,0:T(8,128)(2,1)S(1)}, u32[]{:S(2)}, u32[]{:S(2)}) %all-to-all-start.2) | async-done | bytes 1638432 | tf_op jit(solution)/shard_map/all_to_all | solution.py:403
  122.8 1.2 copy-done
  124.0 8.2 %project.1 = bf16[320,2560]{1,0:T(8,128)(2,1)} custom-call(bf16[16,400,128]{2,1,0:T(8,128)(2,1)} %copy-done, bf16[1280,5120]{1,0:T(8,128)(2,1)} %own_weight.1, bf16[160,2560]{1,0:T(8,128)(2,1)S(1)} %pad_maximum_fusion.refs_0_, bf16[160,2560]{1,0:T(8,128)(2,1)S(1)} %collective-permute-done.16.refs_1_, bf16[160,2560]{1,0:T(8,128)(2,1)} %collective-permute-done.17.refs_2_, ...), custom_call_target="tpu_custom_call" | custom-call | tf_op jit(solution)/shard_map/project/pallas_call | solution.py:409
  (52 shorter events, 0.1 us)
Async XLA Ops:
  3.3 27.1 %all-to-all-start = ((bf16[8,320,128]{2,1,0:T(8,128)(2,1)}), bf16[8,320,128]{2,1,0:T(8,128)(2,1)S(1)}, u32[]{:S(2)}, u32[]{:S(2)}) async-start(bf16[8,320,128]{2,1,0:T(8,128)(2,1)} %bitcast.10), calls=%async_computation | async-start | bytes 1310720 | tf_op jit(solution)/shard_map/all_to_all | solution.py:338
  11.3 23.6 %collective-permute-start.7 = (bf16[80,2560]{1,0:T(8,128)(2,1)}, bf16[80,2560]{1,0:T(8,128)(2,1)S(1)}, u32[]{:S(2)}, u32[]{:S(2)}) collective-permute-start(bf16[80,2560]{1,0:T(8,128)(2,1)} %get-tuple-element.89), channel_id=1, source_target_pairs={{0,1},{1,0},{2,3},{3,2},{4,5},{5,4},{6,7},{7,6},{8,9},{9,8},{10,11... | collective-permute-start | bytes 1228808 | tf_op jit(solution)/shard_map/ppermute | solution.py:343
  12.0 22.9 %collective-permute-start.8 = (bf16[80,2560]{1,0:T(8,128)(2,1)}, bf16[80,2560]{1,0:T(8,128)(2,1)S(1)}, u32[]{:S(2)}, u32[]{:S(2)}) collective-permute-start(bf16[80,2560]{1,0:T(8,128)(2,1)} %get-tuple-element.90), channel_id=1, source_target_pairs={{0,3},{1,2},{2,1},{3,0},{4,7},{5,6},{6,5},{7,4},{8,11},{9,10},{10,... | collective-permute-start | bytes 1228808 | tf_op jit(solution)/shard_map/ppermute | solution.py:344
  15.4 3.2 %collective-permute-start = (bf16[2,80,256]{2,1,0:T(8,128)(2,1)}, bf16[2,80,256]{2,1,0:T(8,128)(2,1)S(1)}, u32[]{:S(2)}, u32[]{:S(2)}) collective-permute-start(bf16[2,80,256]{2,1,0:T(8,128)(2,1)} %get-tuple-element.71), channel_id=1, source_target_pairs={{0,16},{16,0},{32,48},{48,32},{64,80},{80,64},{96,112},{112,96},{1... | collective-permute-start | bytes 245768 | tf_op jit(solution)/shard_map/ppermute | solution.py:46
  15.4 6.3 %collective-permute-start.1 = (bf16[2,80,256]{2,1,0:T(8,128)(2,1)}, bf16[2,80,256]{2,1,0:T(8,128)(2,1)S(1)}, u32[]{:S(2)}, u32[]{:S(2)}) collective-permute-start(bf16[2,80,256]{2,1,0:T(8,128)(2,1)} %get-tuple-element.72), channel_id=1, source_target_pairs={{0,32},{16,48},{32,64},{48,80},{64,96},{80,112},{96,0},{112,16},{1... | collective-permute-start | bytes 245768 | tf_op jit(solution)/shard_map/ppermute | solution.py:46
  16.9 4.8 %collective-permute-start.2 = (bf16[2,80,256]{2,1,0:T(8,128)(2,1)}, bf16[2,80,256]{2,1,0:T(8,128)(2,1)S(1)}, u32[]{:S(2)}, u32[]{:S(2)}) collective-permute-start(bf16[2,80,256]{2,1,0:T(8,128)(2,1)} %get-tuple-element.73), channel_id=1, source_target_pairs={{0,96},{16,112},{32,0},{48,16},{64,32},{80,48},{96,64},{112,80},{1... | collective-permute-start | bytes 245768 | tf_op jit(solution)/shard_map/ppermute | solution.py:46
  18.7 9.3 %copy-start.12 = (bf16[2,80,256]{2,1,0:T(8,128)(2,1)}, bf16[2,80,256]{2,1,0:T(8,128)(2,1)S(1)}, u32[]{:S(2)}) copy-start(bf16[2,80,256]{2,1,0:T(8,128)(2,1)S(1)} %collective-permute-done.refs_1_) | copy-start | bytes 245764
  18.7 6.2 %collective-permute-start.3 = (bf16[2,80,256]{2,1,0:T(8,128)(2,1)}, bf16[2,80,256]{2,1,0:T(8,128)(2,1)S(1)}, u32[]{:S(2)}, u32[]{:S(2)}) collective-permute-start(bf16[2,80,256]{2,1,0:T(8,128)(2,1)} %get-tuple-element.74), channel_id=1, source_target_pairs={{0,64},{16,80},{32,96},{48,112},{64,0},{80,16},{96,32},{112,48},{1... | collective-permute-start | bytes 245768 | tf_op jit(solution)/shard_map/ppermute | solution.py:46
  21.7 6.3 %copy-start.13 = (bf16[2,80,256]{2,1,0:T(8,128)(2,1)}, bf16[2,80,256]{2,1,0:T(8,128)(2,1)S(1)}, u32[]{:S(2)}) copy-start(bf16[2,80,256]{2,1,0:T(8,128)(2,1)S(1)} %collective-permute-done.1.refs_2_) | copy-start | bytes 245764
  21.7 6.3 %collective-permute-start.4 = (bf16[2,80,256]{2,1,0:T(8,128)(2,1)}, bf16[2,80,256]{2,1,0:T(8,128)(2,1)S(1)}, u32[]{:S(2)}, u32[]{:S(2)}) collective-permute-start(bf16[2,80,256]{2,1,0:T(8,128)(2,1)} %get-tuple-element.75), channel_id=1, source_target_pairs={{0,48},{16,32},{32,80},{48,64},{64,112},{80,96},{96,16},{112,0},{1... | collective-permute-start | bytes 245768 | tf_op jit(solution)/shard_map/ppermute | solution.py:46
  21.7 6.3 %copy-start.14 = (bf16[2,80,256]{2,1,0:T(8,128)(2,1)}, bf16[2,80,256]{2,1,0:T(8,128)(2,1)S(1)}, u32[]{:S(2)}) copy-start(bf16[2,80,256]{2,1,0:T(8,128)(2,1)S(1)} %collective-permute-done.2.refs_3_) | copy-start | bytes 245764
  21.7 6.3 %collective-permute-start.5 = (bf16[2,80,256]{2,1,0:T(8,128)(2,1)}, bf16[2,80,256]{2,1,0:T(8,128)(2,1)S(1)}, u32[]{:S(2)}, u32[]{:S(2)}) collective-permute-start(bf16[2,80,256]{2,1,0:T(8,128)(2,1)} %get-tuple-element.76), channel_id=1, source_target_pairs={{0,112},{16,96},{32,16},{48,0},{64,48},{80,32},{96,80},{112,64},{1... | collective-permute-start | bytes 245768 | tf_op jit(solution)/shard_map/ppermute | solution.py:46
  24.8 3.2 %copy-start.15 = (bf16[2,80,256]{2,1,0:T(8,128)(2,1)}, bf16[2,80,256]{2,1,0:T(8,128)(2,1)S(1)}, u32[]{:S(2)}) copy-start(bf16[2,80,256]{2,1,0:T(8,128)(2,1)S(1)} %collective-permute-done.3.refs_4_) | copy-start | bytes 245764
  24.8 5.6 %collective-permute-start.6 = (bf16[2,80,256]{2,1,0:T(8,128)(2,1)}, bf16[2,80,256]{2,1,0:T(8,128)(2,1)S(1)}, u32[]{:S(2)}, u32[]{:S(2)}) collective-permute-start(bf16[2,80,256]{2,1,0:T(8,128)(2,1)} %get-tuple-element.77), channel_id=1, source_target_pairs={{0,80},{16,64},{32,112},{48,96},{64,16},{80,0},{96,48},{112,32},{1... | collective-permute-start | bytes 245768 | tf_op jit(solution)/shard_map/ppermute | solution.py:46
  28.0 2.4 %copy-start.16 = (bf16[2,80,256]{2,1,0:T(8,128)(2,1)}, bf16[2,80,256]{2,1,0:T(8,128)(2,1)S(1)}, u32[]{:S(2)}) copy-start(bf16[2,80,256]{2,1,0:T(8,128)(2,1)S(1)} %collective-permute-done.4.refs_5_) | copy-start | bytes 245764
  28.1 2.4 %copy-start.17 = (bf16[2,80,256]{2,1,0:T(8,128)(2,1)}, bf16[2,80,256]{2,1,0:T(8,128)(2,1)S(1)}, u32[]{:S(2)}) copy-start(bf16[2,80,256]{2,1,0:T(8,128)(2,1)S(1)} %collective-permute-done.5.refs_6_) | copy-start | bytes 245764
  30.4 0.6 copy-start.18
  30.4 0.9 copy-start.1
  34.9 4.6 %copy-start.20 = (bf16[2,8,80,128]{3,2,1,0:T(8,128)(2,1)S(1)}, bf16[2,8,80,128]{3,2,1,0:T(8,128)(2,1)}, u32[]{:S(2)}) copy-start(bf16[2,8,80,128]{3,2,1,0:T(8,128)(2,1)} %get-tuple-element.95) | copy-start | bytes 983044
  35.0 5.9 %copy-start.19 = (bf16[2,8,80,128]{3,2,1,0:T(8,128)(2,1)S(1)}, bf16[2,8,80,128]{3,2,1,0:T(8,128)(2,1)}, u32[]{:S(2)}) copy-start(bf16[2,8,80,128]{3,2,1,0:T(8,128)(2,1)} %get-tuple-element.96) | copy-start | bytes 983044
  35.0 45.3 %all-to-all-start.1 = ((bf16[8,1520,128]{2,1,0:T(8,128)(2,1)}), bf16[8,1520,128]{2,1,0:T(8,128)(2,1)}, u32[]{:S(2)}, u32[]{:S(2)}) async-start(bf16[8,1520,128]{2,1,0:T(8,128)(2,1)} %bitcast.7), calls=%async_computation.1 | async-start | bytes 6225920 | tf_op jit(solution)/shard_map/all_to_all | solution.py:377
  39.6 5.0 %collective-permute-start.9 = (bf16[2,8,80,128]{3,2,1,0:T(8,128)(2,1)S(1)}, bf16[2,8,80,128]{3,2,1,0:T(8,128)(2,1)S(1)}, u32[]{:S(2)}, u32[]{:S(2)}) collective-permute-start(bf16[2,8,80,128]{3,2,1,0:T(8,128)(2,1)S(1)} %copy-done.20), channel_id=1, source_target_pairs={{0,16},{16,0},{32,48},{48,32},{64,80},{80,64},{96,112},{112,96},{1... | collective-permute-start | bytes 983048 | tf_op jit(solution)/shard_map/ppermute | solution.py:46
  40.8 18.8 %collective-permute-start.10 = (bf16[2,8,80,128]{3,2,1,0:T(8,128)(2,1)S(1)}, bf16[2,8,80,128]{3,2,1,0:T(8,128)(2,1)S(1)}, u32[]{:S(2)}, u32[]{:S(2)}) collective-permute-start(bf16[2,8,80,128]{3,2,1,0:T(8,128)(2,1)S(1)} %copy-done.19), channel_id=1, source_target_pairs={{0,32},{16,48},{32,64},{48,80},{64,96},{80,112},{96,0},{112,16},{1... | collective-permute-start | bytes 983048 | tf_op jit(solution)/shard_map/ppermute | solution.py:46
  41.1 18.6 %collective-permute-start.11 = (bf16[2,8,80,128]{3,2,1,0:T(8,128)(2,1)}, bf16[2,8,80,128]{3,2,1,0:T(8,128)(2,1)S(1)}, u32[]{:S(2)}, u32[]{:S(2)}) collective-permute-start(bf16[2,8,80,128]{3,2,1,0:T(8,128)(2,1)} %get-tuple-element.97), channel_id=1, source_target_pairs={{0,96},{16,112},{32,0},{48,16},{64,32},{80,48},{96,64},{112,80},{1... | collective-permute-start | bytes 983048 | tf_op jit(solution)/shard_map/ppermute | solution.py:46
  44.1 15.6 %collective-permute-start.12 = (bf16[2,8,80,128]{3,2,1,0:T(8,128)(2,1)}, bf16[2,8,80,128]{3,2,1,0:T(8,128)(2,1)S(1)}, u32[]{:S(2)}, u32[]{:S(2)}) collective-permute-start(bf16[2,8,80,128]{3,2,1,0:T(8,128)(2,1)} %get-tuple-element.98), channel_id=1, source_target_pairs={{0,64},{16,80},{32,96},{48,112},{64,0},{80,16},{96,32},{112,48},{1... | collective-permute-start | bytes 983048 | tf_op jit(solution)/shard_map/ppermute | solution.py:46
  44.1 20.9 %collective-permute-start.13 = (bf16[2,8,80,128]{3,2,1,0:T(8,128)(2,1)}, bf16[2,8,80,128]{3,2,1,0:T(8,128)(2,1)S(1)}, u32[]{:S(2)}, u32[]{:S(2)}) collective-permute-start(bf16[2,8,80,128]{3,2,1,0:T(8,128)(2,1)} %get-tuple-element.99), channel_id=1, source_target_pairs={{0,48},{16,32},{32,80},{48,64},{64,112},{80,96},{96,16},{112,0},{1... | collective-permute-start | bytes 983048 | tf_op jit(solution)/shard_map/ppermute | solution.py:46
  44.6 35.6 %copy-start.5 = (bf16[2,8,80,128]{3,2,1,0:T(8,128)(2,1)}, bf16[2,8,80,128]{3,2,1,0:T(8,128)(2,1)S(1)}, u32[]{:S(2)}) copy-start(bf16[2,8,80,128]{3,2,1,0:T(8,128)(2,1)S(1)} %collective-permute-done.9.refs_2_) | copy-start | bytes 983044
  44.6 27.8 %collective-permute-start.14 = (bf16[2,8,80,128]{3,2,1,0:T(8,128)(2,1)}, bf16[2,8,80,128]{3,2,1,0:T(8,128)(2,1)S(1)}, u32[]{:S(2)}, u32[]{:S(2)}) collective-permute-start(bf16[2,8,80,128]{3,2,1,0:T(8,128)(2,1)} %get-tuple-element.100), channel_id=1, source_target_pairs={{0,112},{16,96},{32,16},{48,0},{64,48},{80,32},{96,80},{112,64},{1... | collective-permute-start | bytes 983048 | tf_op jit(solution)/shard_map/ppermute | solution.py:46
  59.6 20.6 %copy-start.6 = (bf16[2,8,80,128]{3,2,1,0:T(8,128)(2,1)}, bf16[2,8,80,128]{3,2,1,0:T(8,128)(2,1)S(1)}, u32[]{:S(2)}) copy-start(bf16[2,8,80,128]{3,2,1,0:T(8,128)(2,1)S(1)} %collective-permute-done.10.refs_3_) | copy-start | bytes 983044
  59.6 13.0 %collective-permute-start.15 = (bf16[2,8,80,128]{3,2,1,0:T(8,128)(2,1)}, bf16[2,8,80,128]{3,2,1,0:T(8,128)(2,1)S(1)}, u32[]{:S(2)}, u32[]{:S(2)}) collective-permute-start(bf16[2,8,80,128]{3,2,1,0:T(8,128)(2,1)} %get-tuple-element.101), channel_id=1, source_target_pairs={{0,80},{16,64},{32,112},{48,96},{64,16},{80,0},{96,48},{112,32},{1... | collective-permute-start | bytes 983048 | tf_op jit(solution)/shard_map/ppermute | solution.py:46
  59.7 20.5 %copy-start.7 = (bf16[2,8,80,128]{3,2,1,0:T(8,128)(2,1)}, bf16[2,8,80,128]{3,2,1,0:T(8,128)(2,1)S(1)}, u32[]{:S(2)}) copy-start(bf16[2,8,80,128]{3,2,1,0:T(8,128)(2,1)S(1)} %collective-permute-done.11.refs_4_) | copy-start | bytes 983044
  59.7 20.5 %copy-start.8 = (bf16[2,8,80,128]{3,2,1,0:T(8,128)(2,1)}, bf16[2,8,80,128]{3,2,1,0:T(8,128)(2,1)S(1)}, u32[]{:S(2)}) copy-start(bf16[2,8,80,128]{3,2,1,0:T(8,128)(2,1)S(1)} %collective-permute-done.12.refs_5_) | copy-start | bytes 983044
  64.9 15.3 %copy-start.9 = (bf16[2,8,80,128]{3,2,1,0:T(8,128)(2,1)}, bf16[2,8,80,128]{3,2,1,0:T(8,128)(2,1)S(1)}, u32[]{:S(2)}) copy-start(bf16[2,8,80,128]{3,2,1,0:T(8,128)(2,1)S(1)} %collective-permute-done.13.refs_6_) | copy-start | bytes 983044
  72.4 0.8 copy-start.10
  72.7 3.7 %copy-start.11 = (bf16[2,8,80,128]{3,2,1,0:T(8,128)(2,1)}, bf16[2,8,80,128]{3,2,1,0:T(8,128)(2,1)S(1)}, u32[]{:S(2)}) copy-start(bf16[2,8,80,128]{3,2,1,0:T(8,128)(2,1)S(1)} %collective-permute-done.15.refs_8_) | copy-start | bytes 983044
  72.7 23.7 %collective-permute-start.18 = (bf16[160,2560]{1,0:T(8,128)(2,1)S(1)}, bf16[160,2560]{1,0:T(8,128)(2,1)}, u32[]{:S(2)}, u32[]{:S(2)}) collective-permute-start(bf16[160,2560]{1,0:T(8,128)(2,1)S(1)} %pad_maximum_fusion.refs_0_), channel_id=1, source_target_pairs={{0,64},{16,80},{32,96},{48,112},{64,0},{80,16},{96,32},{112,48},{1... | collective-permute-start | bytes 2457608 | tf_op jit(solution)/shard_map/ppermute | solution.py:46
  73.3 37.4 %collective-permute-start.17 = (bf16[160,2560]{1,0:T(8,128)(2,1)S(1)}, bf16[160,2560]{1,0:T(8,128)(2,1)}, u32[]{:S(2)}, u32[]{:S(2)}) collective-permute-start(bf16[160,2560]{1,0:T(8,128)(2,1)S(1)} %pad_maximum_fusion.refs_0_), channel_id=1, source_target_pairs={{0,96},{16,112},{32,0},{48,16},{64,32},{80,48},{96,64},{112,80},{1... | collective-permute-start | bytes 2457608 | tf_op jit(solution)/shard_map/ppermute | solution.py:46
  76.4 36.2 %collective-permute-start.16 = (bf16[160,2560]{1,0:T(8,128)(2,1)S(1)}, bf16[160,2560]{1,0:T(8,128)(2,1)S(1)}, u32[]{:S(2)}, u32[]{:S(2)}) collective-permute-start(bf16[160,2560]{1,0:T(8,128)(2,1)S(1)} %pad_maximum_fusion.refs_0_), channel_id=1, source_target_pairs={{0,32},{16,48},{32,64},{48,80},{64,96},{80,112},{96,0},{112,16},{1... | collective-permute-start | bytes 2457608 | tf_op jit(solution)/shard_map/ppermute | solution.py:46
  92.5 30.4 %all-to-all-start.2 = ((bf16[16,400,128]{2,1,0:T(8,128)(2,1)}), bf16[16,400,128]{2,1,0:T(8,128)(2,1)S(1)}, u32[]{:S(2)}, u32[]{:S(2)}) async-start(bf16[16,400,128]{2,1,0:T(8,128)(2,1)} %bitcast.8), calls=%async_computation.2 | async-start | bytes 3276800 | tf_op jit(solution)/shard_map/all_to_all | solution.py:403
  96.2 16.4 %collective-permute-start.19 = (bf16[160,2560]{1,0:T(8,128)(2,1)S(1)}, bf16[160,2560]{1,0:T(8,128)(2,1)S(1)}, u32[]{:S(2)}, u32[]{:S(2)}) collective-permute-start(bf16[160,2560]{1,0:T(8,128)(2,1)S(1)} %pad_maximum_fusion.refs_0_), channel_id=1, source_target_pairs={{0,16},{16,0},{32,48},{48,32},{64,80},{80,64},{96,112},{112,96},{1... | collective-permute-start | bytes 2457608 | tf_op jit(solution)/shard_map/ppermute | solution.py:384
  96.4 16.3 %collective-permute-start.22 = (bf16[160,2560]{1,0:T(8,128)(2,1)}, bf16[160,2560]{1,0:T(8,128)(2,1)S(1)}, u32[]{:S(2)}, u32[]{:S(2)}) collective-permute-start(bf16[160,2560]{1,0:T(8,128)(2,1)} %collective-permute-done.18.refs_3_), channel_id=1, source_target_pairs={{0,16},{16,0},{32,48},{48,32},{64,80},{80,64},{96,112},{112,96},{1... | collective-permute-start | bytes 2457608 | tf_op jit(solution)/shard_map/ppermute | solution.py:384
  110.6 3.3 %collective-permute-start.21 = (bf16[160,2560]{1,0:T(8,128)(2,1)}, bf16[160,2560]{1,0:T(8,128)(2,1)S(1)}, u32[]{:S(2)}, u32[]{:S(2)}) collective-permute-start(bf16[160,2560]{1,0:T(8,128)(2,1)} %collective-permute-done.17.refs_2_), channel_id=1, source_target_pairs={{0,16},{16,0},{32,48},{48,32},{64,80},{80,64},{96,112},{112,96},{1... | collective-permute-start | bytes 2457608 | tf_op jit(solution)/shard_map/ppermute | solution.py:384
  112.6 2.5 %collective-permute-start.20 = (bf16[160,2560]{1,0:T(8,128)(2,1)S(1)}, bf16[160,2560]{1,0:T(8,128)(2,1)}, u32[]{:S(2)}, u32[]{:S(2)}) collective-permute-start(bf16[160,2560]{1,0:T(8,128)(2,1)S(1)} %collective-permute-done.16.refs_1_), channel_id=1, source_target_pairs={{0,16},{16,0},{32,48},{48,32},{64,80},{80,64},{96,112},{112,96},{1... | collective-permute-start | bytes 2457608 | tf_op jit(solution)/shard_map/ppermute | solution.py:384
  112.6 1.3 %copy-start.2 = (bf16[160,2560]{1,0:T(8,128)(2,1)}, bf16[160,2560]{1,0:T(8,128)(2,1)S(1)}, u32[]{:S(2)}) copy-start(bf16[160,2560]{1,0:T(8,128)(2,1)S(1)} %collective-permute-done.19.refs_4_) | copy-start | bytes 2457604
  112.6 1.3 %copy-start.3 = (bf16[160,2560]{1,0:T(8,128)(2,1)}, bf16[160,2560]{1,0:T(8,128)(2,1)S(1)}, u32[]{:S(2)}) copy-start(bf16[160,2560]{1,0:T(8,128)(2,1)S(1)} %collective-permute-done.22.refs_7_) | copy-start | bytes 2457604
  114.0 0.9 copy-start.4
  122.8 1.2 copy-start

commit v5 on v4

--- a/solution.py
+++ b/solution.py
@@ -17,11 +17,12 @@
 HEADS = 10
 WIDE = SPACE * HD
 PAIRS = 5
-LENT = (0, 2, 3, 4)
-UNITS = 3 * PAIRS + 2 * WIN
+LENT = (0, 1, 3, 4)
+EARLY = 2
+UNITS = 3 * PAIRS + 2 * WIN - EARLY
 BLOCKS = 4
 AHEAD = 2
-STEPS = ((0, 0), (0, 1), (1, 0), (3, 0), (2, 0), (1, 1), (3, 1), (2, 1))
+STEPS = ((0, 0), (2, 0), (2, 1), (1, 0), (3, 0), (1, 1), (3, 1), (0, 1))
 VMEM = pl.BlockSpec(memory_space=pltpu.VMEM)
 HBM = pl.BlockSpec(memory_space=pltpu.HBM)
 SMEM = pl.BlockSpec(memory_space=pltpu.SMEM)
@@ -59,37 +60,49 @@
     return place
 
 
-def pack_slots(window, span_slot, cache_keys, cache_values, out_weight, by_head, *refs):
+def pack_slots(window, span_slot, cache_keys, cache_values, queries, out_weight, by_head, *refs):
     rest, lent = refs[:GROUPS], refs[GROUPS : GROUPS + 2]
-    held, lent_held, held_sems, sems = refs[GROUPS + 2 :]
+    held, queries_held, lent_held, held_sems, sems = refs[GROUPS + 2 :]
     me = lax.axis_index("cache")
     rows, columns = lent[0].shape
     column = pl.multiple_of((1 - lax.axis_index("head")) * columns, HD)
-    for kv, source in enumerate((cache_keys, cache_values)):
-        pltpu.make_async_copy(source, held.at[kv], held_sems.at[kv]).start()
-    loads = []
+    loads = [
+        pltpu.make_async_copy(source, held.at[kv], held_sems.at[kv])
+        for kv, source in enumerate((cache_keys, cache_values))
+    ]
+    source = queries.at[pl.ds(0, EARLY), :, pl.ds(0, WIDE)]
+    loads.append(pltpu.make_async_copy(source, queries_held, held_sems.at[2]))
     for part in range(2):
         row = pl.multiple_of((2 * me + part) * rows, 16)
         source = out_weight.at[pl.ds(row, rows), pl.ds(column, columns)]
-        loads.append(pltpu.make_async_copy(source, lent_held.at[part], held_sems.at[2 + part]))
-        loads[part].start()
-    for kv, source in enumerate((cache_keys, cache_values)):
-        pltpu.make_async_copy(source, held.at[kv], held_sems.at[kv]).wait()
+        loads.append(pltpu.make_async_copy(source, lent_held.at[part], held_sems.at[3 + part]))
+    for load in loads:
+        load.start()
+    for load in loads[:2]:
+        load.wait()
     for head in range(SPACE):
-        source = held.at[:, :, :, pl.ds(head * HD, HD)]
-        pltpu.make_async_copy(source, by_head.at[head], sems.at[0]).start()
+        lanes = pl.ds(head * HD, HD)
+        for kv in range(2):
+            target = by_head.at[head, pl.ds(2 * kv, 2)]
+            pltpu.make_async_copy(held.at[kv, :, :, lanes], target, sems.at[0]).start()
     for step in range(GROUPS):
         slot = picked(window, span_slot, goes_to(me, step), me)
         source = held.at[:, slot, :, pl.ds(WIDE, 2 * HD)]
         pltpu.make_async_copy(source, rest[step], sems.at[1 + step]).start()
+    loads[2].wait()
+    for head in range(SPACE):
+        source = queries_held.at[:, :, pl.ds(head * HD, HD)]
+        target = by_head.at[head, pl.ds(4, EARLY)]
+        pltpu.make_async_copy(source, target, sems.at[0]).start()
     for part in range(2):
-        loads[part].wait()
+        loads[3 + part].wait()
         pltpu.make_async_copy(lent_held.at[part], lent[part], sems.at[1 + GROUPS + part]).start()
-    wait_for(by_head, sems.at[0])
-    for part in range(2):
-        wait_for(lent[part], sems.at[1 + GROUPS + part])
-    for step in range(GROUPS):
-        wait_for(rest[step], sems.at[1 + step])
+    for place, target in enumerate((by_head, *rest, *lent)):
+        wait_for(target, sems.at[place])
+
+
+def unit_of(kind, pair):
+    return kind * PAIRS + pair - EARLY
 
 
 def pack_pairs(queries, keys, values, sent, held, held_sems, sems):
@@ -100,24 +113,29 @@
     for load in loads:
         load.start()
     for kind in range(3):
+        first = EARLY if kind == 0 else 0
         loads[kind].wait()
         for to in range(SPACE):
             wide, last = pl.ds(to * HD, HD), pl.ds(WIDE + to % 2 * HD, HD)
+            if first < SPANS:
+                pltpu.make_async_copy(
+                    held.at[kind, pl.ds(first, SPANS - first), :, wide],
+                    sent.at[to, pl.ds(unit_of(kind, first), SPANS - first)],
+                    sems.at[kind],
+                ).start()
             pltpu.make_async_copy(
-                held.at[kind, :, :, wide], sent.at[to, pl.ds(kind * PAIRS, SPANS)], sems.at[kind]
-            ).start()
-            pltpu.make_async_copy(
-                held.at[kind, to // 2, :, last], sent.at[to, kind * PAIRS + SPANS], sems.at[kind]
+                held.at[kind, to // 2, :, last], sent.at[to, unit_of(kind, SPANS)], sems.at[kind]
             ).start()
     for kind in range(3):
-        wait_for(sent.at[:, pl.ds(kind * PAIRS, PAIRS)], sems.at[kind])
+        first = EARLY if kind == 0 else 0
+        wait_for(sent.at[:, pl.ds(unit_of(kind, first), PAIRS - first)], sems.at[kind])
 
 
 def pack_cached(window, span_slot, by_head, *refs):
     rest, sent, wide = refs[:GROUPS], refs[GROUPS + 1], refs[GROUPS + 2 : 2 * GROUPS + 2]
     held, heads, held_sems, wide_sems, sent_sem = refs[2 * GROUPS + 2 :]
     group = lax.axis_index("cache")
-    loads = [pltpu.make_async_copy(by_head, heads, held_sems.at[GROUPS])]
+    loads = [pltpu.make_async_copy(by_head.at[:, pl.ds(0, 4)], heads, held_sems.at[GROUPS])]
     for step in range(GROUPS):
         target = held.at[came_from(group, step)]
         loads.append(pltpu.make_async_copy(rest[step], target, held_sems.at[step]))
@@ -127,7 +145,7 @@
     for step in range(GROUPS):
         slot = picked(window, span_slot, goes_to(group, step), group)
         for kv in range(2):
-            source = heads.at[:, kv, slot]
+            source = heads.at[:, 2 * kv + slot]
             pltpu.make_async_copy(source, wide[step].at[kv], wide_sems.at[step]).start()
     for load in loads[1:]:
         load.wait()
@@ -136,17 +154,17 @@
             owner = span_slot[window[w, group * SPANS + to // 2]] >> 1
             pltpu.make_async_copy(
                 held.at[owner, :, :, pl.ds(to % 2 * HD, HD)],
-                sent.at[to, pl.ds(3 * PAIRS + 2 * w, 2)],
+                sent.at[to, pl.ds(unit_of(3, 2 * w), 2)],
                 sent_sem.at[0],
             ).start()
     for step in range(GROUPS):
         wait_for(wide[step], wide_sems.at[step])
-    wait_for(sent.at[:, pl.ds(3 * PAIRS, 2 * WIN)], sent_sem.at[0])
+    wait_for(sent.at[:, pl.ds(unit_of(3, 0), 2 * WIN)], sent_sem.at[0])
 
 
 def attend(window, span_slot, counts, *refs):
-    came, wide = refs[0], refs[1 : 1 + GROUPS]
-    out, q_all, k_all, v_all, sent, ready, left = refs[1 + GROUPS :]
+    early, came, wide = refs[0], refs[1], refs[2 : 2 + GROUPS]
+    out, q_all, k_all, v_all, sent, ready, left = refs[2 + GROUPS :]
     group = lax.axis_index("cache")
     me = lax.axis_index("space")
     factor = math.log2(math.e) / math.sqrt(HD)
@@ -164,7 +182,9 @@
 
     def fetch_pair(pair):
         for kind in range(3):
-            fetch(pair, kind, came.at[:, kind * PAIRS + pair], share(pair, kind, 0))
+            before = kind == 0 and pair < EARLY
+            source = early.at[:, 4 + pair] if before else came.at[:, unit_of(kind, pair)]
+            fetch(pair, kind, source, share(pair, kind, 0))
 
     def fetch_wide(step, place):
         pair, segment = place >> 1, 1 + (place & 1)
@@ -229,7 +249,7 @@
         fetch_pair(pair)
     for w in range(WIN):
         for kv in range(2):
-            source = came.at[:, 3 * PAIRS + 2 * w + kv]
+            source = came.at[:, unit_of(3, 2 * w + kv)]
             fetch(SPANS, 1 + kv, source, share(SPANS, 1 + kv, 1 + w))
     scores = score(0, 0)
     for now, later in zip(steps, steps[1:] + [None]):
@@ -319,24 +339,25 @@
 
     by_head, *sent = pl.pallas_call(
         pack_slots,
-        out_shape=[shape((SPACE, 2, 2, ROWS, HD), bf16)]
+        out_shape=[shape((SPACE, 4 + EARLY, ROWS, HD), bf16)]
         + [shape((2, ROWS, 2 * HD), bf16)] * GROUPS
         + [shape((rows, columns), bf16)] * 2,
-        in_specs=[SMEM] * 2 + [HBM] * 3,
+        in_specs=[SMEM] * 2 + [HBM] * 4,
         out_specs=[HBM] * (3 + GROUPS),
         scratch_shapes=[
             pltpu.VMEM((2, 2, ROWS, HEADS * HD), bf16),
+            pltpu.VMEM((EARLY, ROWS, WIDE), bf16),
             pltpu.VMEM((2, rows, columns), bf16),
-            pltpu.SemaphoreType.DMA((4,)),
+            pltpu.SemaphoreType.DMA((5,)),
             pltpu.SemaphoreType.DMA((3 + GROUPS,)),
         ],
         compiler_params=params(60),
         name="pack_slots",
-    )(window, span_slot, cache_keys, cache_values, out_weight)
+    )(window, span_slot, cache_keys, cache_values, queries, out_weight)
     by_head, *sent, queries = lax.optimization_barrier((by_head, *sent, queries))
     rest, lent = sent[:GROUPS], sent[GROUPS:]
     by_head = lax.all_to_all(
-        by_head.reshape(SPACE, 4 * ROWS, HD), "space", split_axis=0, concat_axis=0, tiled=True
+        by_head.reshape(SPACE, -1, HD), "space", split_axis=0, concat_axis=0, tiled=True
     ).reshape(by_head.shape)
     rest = [rest[0]] + [shift(rest[step], "cache", step) for step in range(1, GROUPS)]
     lent = [
@@ -365,7 +386,7 @@
         input_output_aliases={3 + GROUPS: 0},
         scratch_shapes=[
             pltpu.VMEM((GROUPS, 2, ROWS, 2 * HD), bf16),
-            pltpu.VMEM(by_head.shape, bf16),
+            pltpu.VMEM((SPACE, 4, ROWS, HD), bf16),
             pltpu.SemaphoreType.DMA((GROUPS + 1,)),
             pltpu.SemaphoreType.DMA((GROUPS,)),
             pltpu.SemaphoreType.DMA((1,)),
@@ -386,7 +407,7 @@
     attended = pl.pallas_call(
         attend,
         out_shape=shape((2 * SPACE, PAIRS, ROWS, HD), bf16),
-        in_specs=[SMEM] * 3 + [HBM] * (1 + GROUPS),
+        in_specs=[SMEM] * 3 + [HBM] * (2 + GROUPS),
         out_specs=HBM,
         scratch_shapes=[
             pltpu.VMEM((PAIRS, SPACE, ROWS, HD), bf16),
@@ -398,7 +419,7 @@
         ],
         compiler_params=params(60),
         name="attend",
-    )(window, span_slot, counts, came, *wide)
+    )(window, span_slot, counts, by_head, came, *wide)
     attended = attended.reshape(2 * SPACE, PAIRS * ROWS, HD)
     attended = lax.all_to_all(
         attended, ("space", "head"), split_axis=0, concat_axis=0, tiled=True

time: 133 us -> 132 us (level)
  waiting for transfers between devices: 57 us -> 50.7 us
  starting transfers between devices: 41.9 us -> 46.5 us
    all_to_all x1, waiting for transfers between devices: 7.79 us -> 2.58 us  [on_device(): lax.all_to_all(attended, ('space', 'head'), split_axis=0, concat_axis=0,...]
    all_to_all x1, waiting for transfers between devices: 3.85 us -> 0.01 us  [on_device(): lax.all_to_all(pairs.reshape(SPACE, UNITS * ROWS, HD), 'space', split_axi...]
    all_to_all x1, starting transfers between devices: 3.72 us -> 6.89 us  [on_device(): lax.all_to_all(attended, ('space', 'head'), split_axis=0, concat_axis=0,...]
    ppermute x17, starting transfers between devices: 19.7 us -> 22.1 us  [shift(): return lax.ppermute(x, axis, [(i, goes_to(i, step)) for i in range(8)])]
    ppermute x4, waiting for transfers between devices: 1.52 us -> 3.1 us  [on_device(): lax.ppermute(chunk, 'cache', [(i, i ^ 1) for i in range(8)])]
    unnamed x42 -> x60, local copies, waits for them, and re-layouts: 2.98 us -> 3.21 us
  transfers between devices with their start and end apart: 26 -> 26, of which waited for: 13 -> 12; matrix products, arithmetic and copies ran while one was open for 0% -> 0% of each run, Pallas kernels for 14% -> 14%
where the time goes in v5:
time: 132 us; the launch traced here: 131 us
  waiting for transfers between devices  50.7 us (38%)
  starting transfers between devices  46.5 us (35%)
  Pallas kernels  30.1 us (23%)
  local copies, waits for them, and re-layouts  3.21 us (2%)
    ppermute x17, waiting for transfers between devices, shift(): return lax.ppermute(x, axis, [(i, goes_to(i, step)) for i in range(8)])  45 us
    ppermute x17, starting transfers between devices, shift(): return lax.ppermute(x, axis, [(i, goes_to(i, step)) for i in range(8)])  22.1 us
    pallas_call x1, Pallas kernels, on_device(): pl.pallas_call(attend, out_shape=shape((2 * SPACE, PAIRS, ROWS, HD), bf16...  12.2 us
    pallas_call x1, Pallas kernels, on_device(): pl.pallas_call(project, out_shape=shape((SPANS * ROWS, columns), bf16), i...  8.25 us
    all_to_all x1, starting transfers between devices, on_device(): lax.all_to_all(by_head.reshape(SPACE, -1, HD), 'space', split_axis=0, con...  8.17 us
    all_to_all x1, starting transfers between devices, on_device(): lax.all_to_all(attended, ('space', 'head'), split_axis=0, concat_axis=0,...  6.89 us
    all_to_all x1, starting transfers between devices, on_device(): lax.all_to_all(pairs.reshape(SPACE, UNITS * ROWS, HD), 'space', split_axi...  4.61 us
    pallas_call x1, Pallas kernels, on_device(): pl.pallas_call(pack_cached, out_shape=[shape(pairs.shape, bf16)] + [shape...  3.6 us
  transfers between devices with their start and end apart: 26, of which 12 were waited for; matrix products, arithmetic and copies ran while one was open for 0% of the time, Pallas kernels for 14%

profile of v5, /device:TPU:0, one launch (start us, length us, event | category | flops | bytes accessed | tf_op | source)
XLA Modules:
  0.0 131.1 jit_solution(16014507091002575188)
XLA Ops:
  0.0 3.4 %pack_slots.1 = (bf16[8,6,80,128]{3,2,1,0:T(8,128)(2,1)}, bf16[2,80,256]{2,1,0:T(8,128)(2,1)}, bf16[2,80,256]{2,1,0:T(8,128)(2,1)}, bf16[2,80,256]{2,1,0:T(8,128...) custom-call(s32[2,32]{1,0:T(2,128)} %bitcast.12, ...), custom_call_target="tpu_custom_call" | custom-call | tf_op jit(solution)/shard_map/pack_slots/pallas_call | solution.py:340
  3.5 8.2 %all-to-all-start = ((bf16[8,480,128]{2,1,0:T(8,128)(2,1)}), bf16[8,480,128]{2,1,0:T(8,128)(2,1)S(1)}, u32[]{:S(2)}, u32[]{:S(2)}) async-start(bf16[8,480,128]{2,1,0:T(8,128)(2,1)} %bitcast.11), calls=%async_computation | async-start | bytes 1966080 | tf_op jit(solution)/shard_map/all_to_all | solution.py:359
  11.7 0.8 collective-permute-start.7
  12.4 3.3 %collective-permute-start.8 = (bf16[80,2560]{1,0:T(8,128)(2,1)S(1)}, bf16[80,2560]{1,0:T(8,128)(2,1)S(1)}, u32[]{:S(2)}, u32[]{:S(2)}) collective-permute-start(bf16[80,2560]{1,0:T(8,128)(2,1)S(1)} %copy-done.19), channel_id=1, source_target_pairs={{0,3},{1,2},{2,1},{3,0},{4,7},{5,6},{6,5},{7,4},{8,11},{9,10},{10,... | collective-permute-start | bytes 1228808 | tf_op jit(solution)/shard_map/ppermute | solution.py:365
  15.8 3.0 %collective-permute-start = (bf16[2,80,256]{2,1,0:T(8,128)(2,1)S(1)}, bf16[2,80,256]{2,1,0:T(8,128)(2,1)S(1)}, u32[]{:S(2)}, u32[]{:S(2)}) collective-permute-start(bf16[2,80,256]{2,1,0:T(8,128)(2,1)S(1)} %copy-done.29), channel_id=1, source_target_pairs={{0,64},{16,80},{32,96},{48,112},{64,0},{80,16},{96,32},{112,48},{1... | collective-permute-start | bytes 245768 | tf_op jit(solution)/shard_map/ppermute | solution.py:47
  18.8 0.0 collective-permute-start.1
  18.8 0.7 collective-permute-start.2
  19.5 2.2 %collective-permute-done.refs_1_ = bf16[2,80,256]{2,1,0:T(8,128)(2,1)S(1)} collective-permute-done((bf16[2,80,256]{2,1,0:T(8,128)(2,1)S(1)}, bf16[2,80,256]{2,1,0:T(8,128)(2,1)S(1)}, u32[]{:S(2)}, u32[]{:S(2)}) %collective-permute-start) | collective-permute-done | bytes 81952 | tf_op jit(solution)/shard_map/ppermute | solution.py:47
  21.7 2.8 %collective-permute-start.3 = (bf16[2,80,256]{2,1,0:T(8,128)(2,1)S(1)}, bf16[2,80,256]{2,1,0:T(8,128)(2,1)S(1)}, u32[]{:S(2)}, u32[]{:S(2)}) collective-permute-start(bf16[2,80,256]{2,1,0:T(8,128)(2,1)S(1)} %copy-done.26), channel_id=1, source_target_pairs={{0,96},{16,112},{32,0},{48,16},{64,32},{80,48},{96,64},{112,80},{1... | collective-permute-start | bytes 245768 | tf_op jit(solution)/shard_map/ppermute | solution.py:47
  24.6 0.4 collective-permute-done.1.refs_2_
  25.0 0.0 collective-permute-start.4
  25.0 0.9 collective-permute-done.2.refs_3_
  25.9 2.1 %collective-permute-start.5 = (bf16[2,80,256]{2,1,0:T(8,128)(2,1)S(1)}, bf16[2,80,256]{2,1,0:T(8,128)(2,1)S(1)}, u32[]{:S(2)}, u32[]{:S(2)}) collective-permute-start(bf16[2,80,256]{2,1,0:T(8,128)(2,1)S(1)} %copy-done.24), channel_id=1, source_target_pairs={{0,112},{16,96},{32,16},{48,0},{64,48},{80,32},{96,80},{112,64},{1... | collective-permute-start | bytes 245768 | tf_op jit(solution)/shard_map/ppermute | solution.py:47
  28.0 0.0 collective-permute-done.3.refs_4_
  28.0 0.1 collective-permute-start.6
  28.1 2.6 %pack_pairs.1.refs_8_ = bf16[8,17,80,128]{3,2,1,0:T(8,128)(2,1)} custom-call(bf16[4,80,1280]{2,1,0:T(8,128)(2,1)} %queries.2, bf16[4,80,1280]{2,1,0:T(8,128)(2,1)} %keys.1, bf16[4,80,1280]{2,1,0:T(8,128)(2,1)} %values.1), custom_call_target="tpu_custom_call" | custom-call | tf_op jit(solution)/shard_map/pack_pairs/pallas_call | solution.py:367
  30.9 0.6 copy-done.16
  31.4 0.1 copy-done.17
  31.5 0.0 copy-done.18
  31.5 0.3 copy-done
  31.9 3.6 %pack_cached.1 = (bf16[8,17,80,128]{3,2,1,0:T(8,128)(2,1)}, bf16[2,8,80,128]{3,2,1,0:T(8,128)(2,1)}, bf16[2,8,80,128]{3,2,1,0:T(8,128)(2,1)}, bf16[2,8,80,128]{3...) custom-call(s32[2,32]{1,0:T(2,128)} %bitcast.13, ...), custom_call_target="tpu_custom_call", output_to_operand_aliasing={{0}: (11, {})} | custom-call | tf_op jit(solution)/shard_map/pack_cached/pallas_call | solution.py:381
  35.5 0.0 copy-start.22
  35.5 4.6 %all-to-all-start.1 = ((bf16[8,1360,128]{2,1,0:T(8,128)(2,1)}), bf16[8,1360,128]{2,1,0:T(8,128)(2,1)}, u32[]{:S(2)}, u32[]{:S(2)}) async-start(bf16[8,1360,128]{2,1,0:T(8,128)(2,1)} %bitcast.7), calls=%async_computation.1 | async-start | bytes 5570560 | tf_op jit(solution)/shard_map/all_to_all | solution.py:398
  40.1 3.0 %collective-permute-start.9 = (bf16[2,8,80,128]{3,2,1,0:T(8,128)(2,1)S(1)}, bf16[2,8,80,128]{3,2,1,0:T(8,128)(2,1)S(1)}, u32[]{:S(2)}, u32[]{:S(2)}) collective-permute-start(bf16[2,8,80,128]{3,2,1,0:T(8,128)(2,1)S(1)} %copy-done.22), channel_id=1, source_target_pairs={{0,64},{16,80},{32,96},{48,112},{64,0},{80,16},{96,32},{112,48},{1... | collective-permute-start | bytes 983048 | tf_op jit(solution)/shard_map/ppermute | solution.py:47
  43.1 0.4 collective-permute-start.10
  43.5 0.3 collective-permute-start.11
  43.9 2.9 %collective-permute-start.12 = (bf16[2,8,80,128]{3,2,1,0:T(8,128)(2,1)}, bf16[2,8,80,128]{3,2,1,0:T(8,128)(2,1)S(1)}, u32[]{:S(2)}, u32[]{:S(2)}) collective-permute-start(bf16[2,8,80,128]{3,2,1,0:T(8,128)(2,1)} %get-tuple-element.98), channel_id=1, source_target_pairs={{0,96},{16,112},{32,0},{48,16},{64,32},{80,48},{96,64},{112,80},{1... | collective-permute-start | bytes 983048 | tf_op jit(solution)/shard_map/ppermute | solution.py:47
  46.8 5.6 %collective-permute-done.9.refs_3_ = bf16[2,8,80,128]{3,2,1,0:T(8,128)(2,1)S(1)} collective-permute-done((bf16[2,8,80,128]{3,2,1,0:T(8,128)(2,1)S(1)}, bf16[2,8,80,128]{3,2,1,0:T(8,128)(2,1)S(1)}, u32[]{:S(2)}, u32[]{:S(2)}) %collective-permute-start.9) | collective-permute-done | bytes 327712 | tf_op jit(solution)/shard_map/ppermute | solution.py:47
  52.3 1.1 collective-permute-start.14
  53.4 5.0 %collective-permute-done.10.refs_4_ = bf16[2,8,80,128]{3,2,1,0:T(8,128)(2,1)S(1)} collective-permute-done((bf16[2,8,80,128]{3,2,1,0:T(8,128)(2,1)S(1)}, bf16[2,8,80,128]{3,2,1,0:T(8,128)(2,1)S(1)}, u32[]{:S(2)}, u32[]{:S(2)}) %collective-permute-start.10) | collective-permute-done | bytes 327712 | tf_op jit(solution)/shard_map/ppermute | solution.py:47
  58.5 1.0 collective-permute-start.15
  59.5 0.1 pad_maximum_fusion.refs_0_
  59.6 6.3 %collective-permute-done.11.refs_5_ = bf16[2,8,80,128]{3,2,1,0:T(8,128)(2,1)S(1)} collective-permute-done((bf16[2,8,80,128]{3,2,1,0:T(8,128)(2,1)}, bf16[2,8,80,128]{3,2,1,0:T(8,128)(2,1)S(1)}, u32[]{:S(2)}, u32[]{:S(2)}) %collective-permute-start.11) | collective-permute-done | bytes 327712 | tf_op jit(solution)/shard_map/ppermute | solution.py:47
  65.9 0.4 collective-permute-done.12.refs_6_
  66.3 6.5 %collective-permute-done.13.refs_7_ = bf16[2,8,80,128]{3,2,1,0:T(8,128)(2,1)S(1)} collective-permute-done((bf16[2,8,80,128]{3,2,1,0:T(8,128)(2,1)}, bf16[2,8,80,128]{3,2,1,0:T(8,128)(2,1)S(1)}, u32[]{:S(2)}, u32[]{:S(2)}) %collective-permute-start.13) | collective-permute-done | bytes 327712 | tf_op jit(solution)/shard_map/ppermute | solution.py:47
  72.8 2.5 %collective-permute-start.18 = (bf16[160,2560]{1,0:T(8,128)(2,1)S(1)}, bf16[160,2560]{1,0:T(8,128)(2,1)}, u32[]{:S(2)}, u32[]{:S(2)}) collective-permute-start(bf16[160,2560]{1,0:T(8,128)(2,1)S(1)} %pad_maximum_fusion.refs_0_), channel_id=1, source_target_pairs={{0,96},{16,112},{32,0},{48,16},{64,32},{80,48},{96,64},{112,80},{1... | collective-permute-start | bytes 2457608 | tf_op jit(solution)/shard_map/ppermute | solution.py:47
  75.3 2.1 %collective-permute-start.16 = (bf16[160,2560]{1,0:T(8,128)(2,1)S(1)}, bf16[160,2560]{1,0:T(8,128)(2,1)S(1)}, u32[]{:S(2)}, u32[]{:S(2)}) collective-permute-start(bf16[160,2560]{1,0:T(8,128)(2,1)S(1)} %pad_maximum_fusion.refs_0_), channel_id=1, source_target_pairs={{0,64},{16,80},{32,96},{48,112},{64,0},{80,16},{96,32},{112,48},{1... | collective-permute-start | bytes 2457608 | tf_op jit(solution)/shard_map/ppermute | solution.py:47
  77.5 12.2 %attend.1 = bf16[16,5,80,128]{3,2,1,0:T(8,128)(2,1)} custom-call(s32[2,32]{1,0:T(2,128)} %bitcast.14, s32[16]{0:T(128)} %span_slot.5, s32[16]{0:T(128)} %counts.1, bf16[8,6,80,128]{3,2,1,0:T(8,128)(2,1)} %bitcast.9, bf16[8,17,80,128]{3,2,1,0:T(8,128)(2,1)} %bitcast.4.refs_1_, bf16[2,8,80,128]{3,2,1,0:T(8,128)(2,1)} %get-tuple-element.102.refs_2_, ...), custom_call_target="tpu_custom_call" | custom-call | tf_op jit(solution)/shard_map/attend/pallas_call | solution.py:407
  89.7 6.9 %all-to-all-start.2 = ((bf16[16,400,128]{2,1,0:T(8,128)(2,1)}), bf16[16,400,128]{2,1,0:T(8,128)(2,1)S(1)}, u32[]{:S(2)}, u32[]{:S(2)}) async-start(bf16[16,400,128]{2,1,0:T(8,128)(2,1)} %bitcast.10), calls=%async_computation.2 | async-start | bytes 3276800 | tf_op jit(solution)/shard_map/all_to_all | solution.py:424
  96.6 0.1 collective-permute-start.19
  96.7 14.2 %collective-permute-done.18.refs_3_ = bf16[160,2560]{1,0:T(8,128)(2,1)} collective-permute-done((bf16[160,2560]{1,0:T(8,128)(2,1)S(1)}, bf16[160,2560]{1,0:T(8,128)(2,1)}, u32[]{:S(2)}, u32[]{:S(2)}) %collective-permute-start.18) | collective-permute-done | bytes 819232 | tf_op jit(solution)/shard_map/ppermute | solution.py:47
  110.9 3.5 %collective-permute-done.17.refs_2_ = bf16[160,2560]{1,0:T(8,128)(2,1)} collective-permute-done((bf16[160,2560]{1,0:T(8,128)(2,1)S(1)}, bf16[160,2560]{1,0:T(8,128)(2,1)}, u32[]{:S(2)}, u32[]{:S(2)}) %collective-permute-start.17) | collective-permute-done | bytes 819232 | tf_op jit(solution)/shard_map/ppermute | solution.py:47
  114.3 0.5 collective-permute-start.20
  114.9 3.1 %collective-permute-done.21.refs_6_ = bf16[160,2560]{1,0:T(8,128)(2,1)S(1)} collective-permute-done((bf16[160,2560]{1,0:T(8,128)(2,1)}, bf16[160,2560]{1,0:T(8,128)(2,1)S(1)}, u32[]{:S(2)}, u32[]{:S(2)}) %collective-permute-start.21) | collective-permute-done | bytes 819232 | tf_op jit(solution)/shard_map/ppermute | solution.py:405
  118.0 0.9 copy-done.4
  118.9 2.6 %all-to-all-done.2.came = bf16[16,400,128]{2,1,0:T(8,128)(2,1)S(1)} async-done(((bf16[16,400,128]{2,1,0:T(8,128)(2,1)}), bf16[16,400,128]{2,1,0:T(8,128)(2,1)S(1)}, u32[]{:S(2)}, u32[]{:S(2)}) %all-to-all-start.2) | async-done | bytes 1638432 | tf_op jit(solution)/shard_map/all_to_all | solution.py:424
  121.5 1.2 copy-done.1
  122.7 8.2 %project.1 = bf16[320,2560]{1,0:T(8,128)(2,1)} custom-call(bf16[16,400,128]{2,1,0:T(8,128)(2,1)} %copy-done.1, bf16[1280,5120]{1,0:T(8,128)(2,1)} %own_weight.1, bf16[160,2560]{1,0:T(8,128)(2,1)S(1)} %pad_maximum_fusion.refs_0_, bf16[160,2560]{1,0:T(8,128)(2,1)S(1)} %collective-permute-done.16.refs_1_, bf16[160,2560]{1,0:T(8,128)(2,1)} %collective-permute-done.17.refs_2_, ...), custom_call_target="tpu_custom_call" | custom-call | tf_op jit(solution)/shard_map/project/pallas_call | solution.py:430
  (70 shorter events, 0.1 us)
Async XLA Ops:
  3.4 8.3 %copy-start.20 = (bf16[80,2560]{1,0:T(8,128)(2,1)S(1)}, bf16[80,2560]{1,0:T(8,128)(2,1)}, u32[]{:S(2)}) copy-start(bf16[80,2560]{1,0:T(8,128)(2,1)} %get-tuple-element.89) | copy-start | bytes 1228804
  3.4 9.0 %copy-start.19 = (bf16[80,2560]{1,0:T(8,128)(2,1)S(1)}, bf16[80,2560]{1,0:T(8,128)(2,1)}, u32[]{:S(2)}) copy-start(bf16[80,2560]{1,0:T(8,128)(2,1)} %get-tuple-element.90) | copy-start | bytes 1228804
  3.4 12.3 %copy-start.29 = (bf16[2,80,256]{2,1,0:T(8,128)(2,1)S(1)}, bf16[2,80,256]{2,1,0:T(8,128)(2,1)}, u32[]{:S(2)}) copy-start(bf16[2,80,256]{2,1,0:T(8,128)(2,1)} %get-tuple-element.71) | copy-start | bytes 245764
  3.4 15.4 %copy-start.28 = (bf16[2,80,256]{2,1,0:T(8,128)(2,1)S(1)}, bf16[2,80,256]{2,1,0:T(8,128)(2,1)}, u32[]{:S(2)}) copy-start(bf16[2,80,256]{2,1,0:T(8,128)(2,1)} %get-tuple-element.72) | copy-start | bytes 245764
  3.5 15.4 %copy-start.27 = (bf16[2,80,256]{2,1,0:T(8,128)(2,1)S(1)}, bf16[2,80,256]{2,1,0:T(8,128)(2,1)}, u32[]{:S(2)}) copy-start(bf16[2,80,256]{2,1,0:T(8,128)(2,1)} %get-tuple-element.73) | copy-start | bytes 245764
  3.5 18.3 %copy-start.26 = (bf16[2,80,256]{2,1,0:T(8,128)(2,1)S(1)}, bf16[2,80,256]{2,1,0:T(8,128)(2,1)}, u32[]{:S(2)}) copy-start(bf16[2,80,256]{2,1,0:T(8,128)(2,1)} %get-tuple-element.74) | copy-start | bytes 245764
  3.5 21.5 %copy-start.25 = (bf16[2,80,256]{2,1,0:T(8,128)(2,1)S(1)}, bf16[2,80,256]{2,1,0:T(8,128)(2,1)}, u32[]{:S(2)}) copy-start(bf16[2,80,256]{2,1,0:T(8,128)(2,1)} %get-tuple-element.75) | copy-start | bytes 245764
  3.5 22.4 %copy-start.24 = (bf16[2,80,256]{2,1,0:T(8,128)(2,1)S(1)}, bf16[2,80,256]{2,1,0:T(8,128)(2,1)}, u32[]{:S(2)}) copy-start(bf16[2,80,256]{2,1,0:T(8,128)(2,1)} %get-tuple-element.76) | copy-start | bytes 245764
  3.5 24.5 %copy-start.23 = (bf16[2,80,256]{2,1,0:T(8,128)(2,1)S(1)}, bf16[2,80,256]{2,1,0:T(8,128)(2,1)}, u32[]{:S(2)}) copy-start(bf16[2,80,256]{2,1,0:T(8,128)(2,1)} %get-tuple-element.77) | copy-start | bytes 245764
  3.5 27.3 %all-to-all-start = ((bf16[8,480,128]{2,1,0:T(8,128)(2,1)}), bf16[8,480,128]{2,1,0:T(8,128)(2,1)S(1)}, u32[]{:S(2)}, u32[]{:S(2)}) async-start(bf16[8,480,128]{2,1,0:T(8,128)(2,1)} %bitcast.11), calls=%async_computation | async-start | bytes 1966080 | tf_op jit(solution)/shard_map/all_to_all | solution.py:359
  11.7 23.8 %collective-permute-start.7 = (bf16[80,2560]{1,0:T(8,128)(2,1)S(1)}, bf16[80,2560]{1,0:T(8,128)(2,1)S(1)}, u32[]{:S(2)}, u32[]{:S(2)}) collective-permute-start(bf16[80,2560]{1,0:T(8,128)(2,1)S(1)} %copy-done.20), channel_id=1, source_target_pairs={{0,1},{1,0},{2,3},{3,2},{4,5},{5,4},{6,7},{7,6},{8,9},{9,8},{10,11... | collective-permute-start | bytes 1228808 | tf_op jit(solution)/shard_map/ppermute | solution.py:364
  12.4 23.0 %collective-permute-start.8 = (bf16[80,2560]{1,0:T(8,128)(2,1)S(1)}, bf16[80,2560]{1,0:T(8,128)(2,1)S(1)}, u32[]{:S(2)}, u32[]{:S(2)}) collective-permute-start(bf16[80,2560]{1,0:T(8,128)(2,1)S(1)} %copy-done.19), channel_id=1, source_target_pairs={{0,3},{1,2},{2,1},{3,0},{4,7},{5,6},{6,5},{7,4},{8,11},{9,10},{10,... | collective-permute-start | bytes 1228808 | tf_op jit(solution)/shard_map/ppermute | solution.py:365
  15.8 5.9 %collective-permute-start = (bf16[2,80,256]{2,1,0:T(8,128)(2,1)S(1)}, bf16[2,80,256]{2,1,0:T(8,128)(2,1)S(1)}, u32[]{:S(2)}, u32[]{:S(2)}) collective-permute-start(bf16[2,80,256]{2,1,0:T(8,128)(2,1)S(1)} %copy-done.29), channel_id=1, source_target_pairs={{0,64},{16,80},{32,96},{48,112},{64,0},{80,16},{96,32},{112,48},{1... | collective-permute-start | bytes 245768 | tf_op jit(solution)/shard_map/ppermute | solution.py:47
  18.8 6.2 %collective-permute-start.1 = (bf16[2,80,256]{2,1,0:T(8,128)(2,1)S(1)}, bf16[2,80,256]{2,1,0:T(8,128)(2,1)S(1)}, u32[]{:S(2)}, u32[]{:S(2)}) collective-permute-start(bf16[2,80,256]{2,1,0:T(8,128)(2,1)S(1)} %copy-done.28), channel_id=1, source_target_pairs={{0,80},{16,64},{32,112},{48,96},{64,16},{80,0},{96,48},{112,32},{1... | collective-permute-start | bytes 245768 | tf_op jit(solution)/shard_map/ppermute | solution.py:47
  18.8 7.1 %collective-permute-start.2 = (bf16[2,80,256]{2,1,0:T(8,128)(2,1)S(1)}, bf16[2,80,256]{2,1,0:T(8,128)(2,1)S(1)}, u32[]{:S(2)}, u32[]{:S(2)}) collective-permute-start(bf16[2,80,256]{2,1,0:T(8,128)(2,1)S(1)} %copy-done.27), channel_id=1, source_target_pairs={{0,32},{16,48},{32,64},{48,80},{64,96},{80,112},{96,0},{112,16},{1... | collective-permute-start | bytes 245768 | tf_op jit(solution)/shard_map/ppermute | solution.py:47
  21.7 9.0 %copy-start.12 = (bf16[2,80,256]{2,1,0:T(8,128)(2,1)}, bf16[2,80,256]{2,1,0:T(8,128)(2,1)S(1)}, u32[]{:S(2)}) copy-start(bf16[2,80,256]{2,1,0:T(8,128)(2,1)S(1)} %collective-permute-done.refs_1_) | copy-start | bytes 245764
  21.7 6.3 %collective-permute-start.3 = (bf16[2,80,256]{2,1,0:T(8,128)(2,1)S(1)}, bf16[2,80,256]{2,1,0:T(8,128)(2,1)S(1)}, u32[]{:S(2)}, u32[]{:S(2)}) collective-permute-start(bf16[2,80,256]{2,1,0:T(8,128)(2,1)S(1)} %copy-done.26), channel_id=1, source_target_pairs={{0,96},{16,112},{32,0},{48,16},{64,32},{80,48},{96,64},{112,80},{1... | collective-permute-start | bytes 245768 | tf_op jit(solution)/shard_map/ppermute | solution.py:47
  25.0 5.8 %copy-start.13 = (bf16[2,80,256]{2,1,0:T(8,128)(2,1)}, bf16[2,80,256]{2,1,0:T(8,128)(2,1)S(1)}, u32[]{:S(2)}) copy-start(bf16[2,80,256]{2,1,0:T(8,128)(2,1)S(1)} %collective-permute-done.1.refs_2_) | copy-start | bytes 245764
  25.0 5.8 %collective-permute-start.4 = (bf16[2,80,256]{2,1,0:T(8,128)(2,1)S(1)}, bf16[2,80,256]{2,1,0:T(8,128)(2,1)S(1)}, u32[]{:S(2)}, u32[]{:S(2)}) collective-permute-start(bf16[2,80,256]{2,1,0:T(8,128)(2,1)S(1)} %copy-done.25), channel_id=1, source_target_pairs={{0,48},{16,32},{32,80},{48,64},{64,112},{80,96},{96,16},{112,0},{1... | collective-permute-start | bytes 245768 | tf_op jit(solution)/shard_map/ppermute | solution.py:47
  25.9 4.9 %copy-start.14 = (bf16[2,80,256]{2,1,0:T(8,128)(2,1)}, bf16[2,80,256]{2,1,0:T(8,128)(2,1)S(1)}, u32[]{:S(2)}) copy-start(bf16[2,80,256]{2,1,0:T(8,128)(2,1)S(1)} %collective-permute-done.2.refs_3_) | copy-start | bytes 245764
  25.9 4.9 %collective-permute-start.5 = (bf16[2,80,256]{2,1,0:T(8,128)(2,1)S(1)}, bf16[2,80,256]{2,1,0:T(8,128)(2,1)S(1)}, u32[]{:S(2)}, u32[]{:S(2)}) collective-permute-start(bf16[2,80,256]{2,1,0:T(8,128)(2,1)S(1)} %copy-done.24), channel_id=1, source_target_pairs={{0,112},{16,96},{32,16},{48,0},{64,48},{80,32},{96,80},{112,64},{1... | collective-permute-start | bytes 245768 | tf_op jit(solution)/shard_map/ppermute | solution.py:47
  28.0 2.8 %copy-start.15 = (bf16[2,80,256]{2,1,0:T(8,128)(2,1)}, bf16[2,80,256]{2,1,0:T(8,128)(2,1)S(1)}, u32[]{:S(2)}) copy-start(bf16[2,80,256]{2,1,0:T(8,128)(2,1)S(1)} %collective-permute-done.3.refs_4_) | copy-start | bytes 245764
  28.0 2.8 %collective-permute-start.6 = (bf16[2,80,256]{2,1,0:T(8,128)(2,1)S(1)}, bf16[2,80,256]{2,1,0:T(8,128)(2,1)S(1)}, u32[]{:S(2)}, u32[]{:S(2)}) collective-permute-start(bf16[2,80,256]{2,1,0:T(8,128)(2,1)S(1)} %copy-done.23), channel_id=1, source_target_pairs={{0,16},{16,0},{32,48},{48,32},{64,80},{80,64},{96,112},{112,96},{1... | collective-permute-start | bytes 245768 | tf_op jit(solution)/shard_map/ppermute | solution.py:47
  35.5 4.6 %copy-start.22 = (bf16[2,8,80,128]{3,2,1,0:T(8,128)(2,1)S(1)}, bf16[2,8,80,128]{3,2,1,0:T(8,128)(2,1)}, u32[]{:S(2)}) copy-start(bf16[2,8,80,128]{3,2,1,0:T(8,128)(2,1)} %get-tuple-element.95) | copy-start | bytes 983044
  35.5 7.6 %copy-start.21 = (bf16[2,8,80,128]{3,2,1,0:T(8,128)(2,1)S(1)}, bf16[2,8,80,128]{3,2,1,0:T(8,128)(2,1)}, u32[]{:S(2)}) copy-start(bf16[2,8,80,128]{3,2,1,0:T(8,128)(2,1)} %get-tuple-element.96) | copy-start | bytes 983044
  35.5 41.9 %all-to-all-start.1 = ((bf16[8,1360,128]{2,1,0:T(8,128)(2,1)}), bf16[8,1360,128]{2,1,0:T(8,128)(2,1)}, u32[]{:S(2)}, u32[]{:S(2)}) async-start(bf16[8,1360,128]{2,1,0:T(8,128)(2,1)} %bitcast.7), calls=%async_computation.1 | async-start | bytes 5570560 | tf_op jit(solution)/shard_map/all_to_all | solution.py:398
  40.1 12.2 %collective-permute-start.9 = (bf16[2,8,80,128]{3,2,1,0:T(8,128)(2,1)S(1)}, bf16[2,8,80,128]{3,2,1,0:T(8,128)(2,1)S(1)}, u32[]{:S(2)}, u32[]{:S(2)}) collective-permute-start(bf16[2,8,80,128]{3,2,1,0:T(8,128)(2,1)S(1)} %copy-done.22), channel_id=1, source_target_pairs={{0,64},{16,80},{32,96},{48,112},{64,0},{80,16},{96,32},{112,48},{1... | collective-permute-start | bytes 983048 | tf_op jit(solution)/shard_map/ppermute | solution.py:47
  43.1 15.4 %collective-permute-start.10 = (bf16[2,8,80,128]{3,2,1,0:T(8,128)(2,1)S(1)}, bf16[2,8,80,128]{3,2,1,0:T(8,128)(2,1)S(1)}, u32[]{:S(2)}, u32[]{:S(2)}) collective-permute-start(bf16[2,8,80,128]{3,2,1,0:T(8,128)(2,1)S(1)} %copy-done.21), channel_id=1, source_target_pairs={{0,80},{16,64},{32,112},{48,96},{64,16},{80,0},{96,48},{112,32},{1... | collective-permute-start | bytes 983048 | tf_op jit(solution)/shard_map/ppermute | solution.py:47
  43.5 22.4 %collective-permute-start.11 = (bf16[2,8,80,128]{3,2,1,0:T(8,128)(2,1)}, bf16[2,8,80,128]{3,2,1,0:T(8,128)(2,1)S(1)}, u32[]{:S(2)}, u32[]{:S(2)}) collective-permute-start(bf16[2,8,80,128]{3,2,1,0:T(8,128)(2,1)} %get-tuple-element.97), channel_id=1, source_target_pairs={{0,32},{16,48},{32,64},{48,80},{64,96},{80,112},{96,0},{112,16},{1... | collective-permute-start | bytes 983048 | tf_op jit(solution)/shard_map/ppermute | solution.py:47
  43.9 22.4 %collective-permute-start.12 = (bf16[2,8,80,128]{3,2,1,0:T(8,128)(2,1)}, bf16[2,8,80,128]{3,2,1,0:T(8,128)(2,1)S(1)}, u32[]{:S(2)}, u32[]{:S(2)}) collective-permute-start(bf16[2,8,80,128]{3,2,1,0:T(8,128)(2,1)} %get-tuple-element.98), channel_id=1, source_target_pairs={{0,96},{16,112},{32,0},{48,16},{64,32},{80,48},{96,64},{112,80},{1... | collective-permute-start | bytes 983048 | tf_op jit(solution)/shard_map/ppermute | solution.py:47
  46.8 26.0 %collective-permute-start.13 = (bf16[2,8,80,128]{3,2,1,0:T(8,128)(2,1)}, bf16[2,8,80,128]{3,2,1,0:T(8,128)(2,1)S(1)}, u32[]{:S(2)}, u32[]{:S(2)}) collective-permute-start(bf16[2,8,80,128]{3,2,1,0:T(8,128)(2,1)} %get-tuple-element.99), channel_id=1, source_target_pairs={{0,48},{16,32},{32,80},{48,64},{64,112},{80,96},{96,16},{112,0},{1... | collective-permute-start | bytes 983048 | tf_op jit(solution)/shard_map/ppermute | solution.py:47
  52.3 25.1 %copy-start.5 = (bf16[2,8,80,128]{3,2,1,0:T(8,128)(2,1)}, bf16[2,8,80,128]{3,2,1,0:T(8,128)(2,1)S(1)}, u32[]{:S(2)}) copy-start(bf16[2,8,80,128]{3,2,1,0:T(8,128)(2,1)S(1)} %collective-permute-done.9.refs_3_) | copy-start | bytes 983044
  52.3 20.5 %collective-permute-start.14 = (bf16[2,8,80,128]{3,2,1,0:T(8,128)(2,1)}, bf16[2,8,80,128]{3,2,1,0:T(8,128)(2,1)S(1)}, u32[]{:S(2)}, u32[]{:S(2)}) collective-permute-start(bf16[2,8,80,128]{3,2,1,0:T(8,128)(2,1)} %get-tuple-element.100), channel_id=1, source_target_pairs={{0,112},{16,96},{32,16},{48,0},{64,48},{80,32},{96,80},{112,64},{1... | collective-permute-start | bytes 983048 | tf_op jit(solution)/shard_map/ppermute | solution.py:47
  58.5 19.0 %copy-start.6 = (bf16[2,8,80,128]{3,2,1,0:T(8,128)(2,1)}, bf16[2,8,80,128]{3,2,1,0:T(8,128)(2,1)S(1)}, u32[]{:S(2)}) copy-start(bf16[2,8,80,128]{3,2,1,0:T(8,128)(2,1)S(1)} %collective-permute-done.10.refs_4_) | copy-start | bytes 983044
  58.5 14.3 %collective-permute-start.15 = (bf16[2,8,80,128]{3,2,1,0:T(8,128)(2,1)}, bf16[2,8,80,128]{3,2,1,0:T(8,128)(2,1)S(1)}, u32[]{:S(2)}, u32[]{:S(2)}) collective-permute-start(bf16[2,8,80,128]{3,2,1,0:T(8,128)(2,1)} %get-tuple-element.101), channel_id=1, source_target_pairs={{0,16},{16,0},{32,48},{48,32},{64,80},{80,64},{96,112},{112,96},{1... | collective-permute-start | bytes 983048 | tf_op jit(solution)/shard_map/ppermute | solution.py:47
  65.9 11.5 %copy-start.7 = (bf16[2,8,80,128]{3,2,1,0:T(8,128)(2,1)}, bf16[2,8,80,128]{3,2,1,0:T(8,128)(2,1)S(1)}, u32[]{:S(2)}) copy-start(bf16[2,8,80,128]{3,2,1,0:T(8,128)(2,1)S(1)} %collective-permute-done.11.refs_5_) | copy-start | bytes 983044
  66.3 11.1 %copy-start.8 = (bf16[2,8,80,128]{3,2,1,0:T(8,128)(2,1)}, bf16[2,8,80,128]{3,2,1,0:T(8,128)(2,1)S(1)}, u32[]{:S(2)}) copy-start(bf16[2,8,80,128]{3,2,1,0:T(8,128)(2,1)S(1)} %collective-permute-done.12.refs_6_) | copy-start | bytes 983044
  72.8 4.7 %copy-start.9 = (bf16[2,8,80,128]{3,2,1,0:T(8,128)(2,1)}, bf16[2,8,80,128]{3,2,1,0:T(8,128)(2,1)S(1)}, u32[]{:S(2)}) copy-start(bf16[2,8,80,128]{3,2,1,0:T(8,128)(2,1)S(1)} %collective-permute-done.13.refs_7_) | copy-start | bytes 983044
  72.8 38.0 %collective-permute-start.18 = (bf16[160,2560]{1,0:T(8,128)(2,1)S(1)}, bf16[160,2560]{1,0:T(8,128)(2,1)}, u32[]{:S(2)}, u32[]{:S(2)}) collective-permute-start(bf16[160,2560]{1,0:T(8,128)(2,1)S(1)} %pad_maximum_fusion.refs_0_), channel_id=1, source_target_pairs={{0,96},{16,112},{32,0},{48,16},{64,32},{80,48},{96,64},{112,80},{1... | collective-permute-start | bytes 2457608 | tf_op jit(solution)/shard_map/ppermute | solution.py:47
  75.3 39.0 %collective-permute-start.17 = (bf16[160,2560]{1,0:T(8,128)(2,1)S(1)}, bf16[160,2560]{1,0:T(8,128)(2,1)}, u32[]{:S(2)}, u32[]{:S(2)}) collective-permute-start(bf16[160,2560]{1,0:T(8,128)(2,1)S(1)} %pad_maximum_fusion.refs_0_), channel_id=1, source_target_pairs={{0,32},{16,48},{32,64},{48,80},{64,96},{80,112},{96,0},{112,16},{1... | collective-permute-start | bytes 2457608 | tf_op jit(solution)/shard_map/ppermute | solution.py:47
  75.3 39.0 %collective-permute-start.16 = (bf16[160,2560]{1,0:T(8,128)(2,1)S(1)}, bf16[160,2560]{1,0:T(8,128)(2,1)S(1)}, u32[]{:S(2)}, u32[]{:S(2)}) collective-permute-start(bf16[160,2560]{1,0:T(8,128)(2,1)S(1)} %pad_maximum_fusion.refs_0_), channel_id=1, source_target_pairs={{0,64},{16,80},{32,96},{48,112},{64,0},{80,16},{96,32},{112,48},{1... | collective-permute-start | bytes 2457608 | tf_op jit(solution)/shard_map/ppermute | solution.py:47
  89.7 31.8 %all-to-all-start.2 = ((bf16[16,400,128]{2,1,0:T(8,128)(2,1)}), bf16[16,400,128]{2,1,0:T(8,128)(2,1)S(1)}, u32[]{:S(2)}, u32[]{:S(2)}) async-start(bf16[16,400,128]{2,1,0:T(8,128)(2,1)} %bitcast.10), calls=%async_computation.2 | async-start | bytes 3276800 | tf_op jit(solution)/shard_map/all_to_all | solution.py:424
  96.6 18.3 %collective-permute-start.19 = (bf16[160,2560]{1,0:T(8,128)(2,1)S(1)}, bf16[160,2560]{1,0:T(8,128)(2,1)S(1)}, u32[]{:S(2)}, u32[]{:S(2)}) collective-permute-start(bf16[160,2560]{1,0:T(8,128)(2,1)S(1)} %pad_maximum_fusion.refs_0_), channel_id=1, source_target_pairs={{0,16},{16,0},{32,48},{48,32},{64,80},{80,64},{96,112},{112,96},{1... | collective-permute-start | bytes 2457608 | tf_op jit(solution)/shard_map/ppermute | solution.py:405
  110.8 4.0 %collective-permute-start.22 = (bf16[160,2560]{1,0:T(8,128)(2,1)}, bf16[160,2560]{1,0:T(8,128)(2,1)S(1)}, u32[]{:S(2)}, u32[]{:S(2)}) collective-permute-start(bf16[160,2560]{1,0:T(8,128)(2,1)} %collective-permute-done.18.refs_3_), channel_id=1, source_target_pairs={{0,16},{16,0},{32,48},{48,32},{64,80},{80,64},{96,112},{112,96},{1... | collective-permute-start | bytes 2457608 | tf_op jit(solution)/shard_map/ppermute | solution.py:405
  114.3 3.6 %collective-permute-start.21 = (bf16[160,2560]{1,0:T(8,128)(2,1)}, bf16[160,2560]{1,0:T(8,128)(2,1)S(1)}, u32[]{:S(2)}, u32[]{:S(2)}) collective-permute-start(bf16[160,2560]{1,0:T(8,128)(2,1)} %collective-permute-done.17.refs_2_), channel_id=1, source_target_pairs={{0,16},{16,0},{32,48},{48,32},{64,80},{80,64},{96,112},{112,96},{1... | collective-permute-start | bytes 2457608 | tf_op jit(solution)/shard_map/ppermute | solution.py:405
  114.3 4.5 %collective-permute-start.20 = (bf16[160,2560]{1,0:T(8,128)(2,1)S(1)}, bf16[160,2560]{1,0:T(8,128)(2,1)}, u32[]{:S(2)}, u32[]{:S(2)}) collective-permute-start(bf16[160,2560]{1,0:T(8,128)(2,1)S(1)} %collective-permute-done.16.refs_1_), channel_id=1, source_target_pairs={{0,16},{16,0},{32,48},{48,32},{64,80},{80,64},{96,112},{112,96},{1... | collective-permute-start | bytes 2457608 | tf_op jit(solution)/shard_map/ppermute | solution.py:405
  114.9 3.1 %copy-start.2 = (bf16[160,2560]{1,0:T(8,128)(2,1)}, bf16[160,2560]{1,0:T(8,128)(2,1)S(1)}, u32[]{:S(2)}) copy-start(bf16[160,2560]{1,0:T(8,128)(2,1)S(1)} %collective-permute-done.19.refs_4_) | copy-start | bytes 2457604
  114.9 3.1 %copy-start.3 = (bf16[160,2560]{1,0:T(8,128)(2,1)}, bf16[160,2560]{1,0:T(8,128)(2,1)S(1)}, u32[]{:S(2)}) copy-start(bf16[160,2560]{1,0:T(8,128)(2,1)S(1)} %collective-permute-done.22.refs_7_) | copy-start | bytes 2457604
  (8 other events, 10.0 us)

commit v6 on v5

--- a/solution.py
+++ b/solution.py
@@ -60,6 +60,12 @@
     return place
 
 
+def owners_of(window, span_slot, group):
+    return [
+        span_slot[window[w, group * SPANS + span]] >> 1 for span in range(SPANS) for w in range(WIN)
+    ]
+
+
 def pack_slots(window, span_slot, cache_keys, cache_values, queries, out_weight, by_head, *refs):
     rest, lent = refs[:GROUPS], refs[GROUPS : GROUPS + 2]
     held, queries_held, lent_held, held_sems, sems = refs[GROUPS + 2 :]
@@ -78,15 +84,14 @@
         loads.append(pltpu.make_async_copy(source, lent_held.at[part], held_sems.at[3 + part]))
     for load in loads:
         load.start()
-    for load in loads[:2]:
-        load.wait()
-    for head in range(SPACE):
-        lanes = pl.ds(head * HD, HD)
-        for kv in range(2):
+    slots = [picked(window, span_slot, goes_to(me, step), me) for step in range(GROUPS)]
+    for kv in range(2):
+        loads[kv].wait()
+        for head in range(SPACE):
+            source = held.at[kv, :, :, pl.ds(head * HD, HD)]
             target = by_head.at[head, pl.ds(2 * kv, 2)]
-            pltpu.make_async_copy(held.at[kv, :, :, lanes], target, sems.at[0]).start()
-    for step in range(GROUPS):
-        slot = picked(window, span_slot, goes_to(me, step), me)
+            pltpu.make_async_copy(source, target, sems.at[0]).start()
+    for step, slot in enumerate(slots):
         source = held.at[:, slot, :, pl.ds(WIDE, 2 * HD)]
         pltpu.make_async_copy(source, rest[step], sems.at[1 + step]).start()
     loads[2].wait()
@@ -141,9 +146,10 @@
         loads.append(pltpu.make_async_copy(rest[step], target, held_sems.at[step]))
     for load in loads:
         load.start()
+    slots = [picked(window, span_slot, goes_to(group, step), group) for step in range(GROUPS)]
+    owners = owners_of(window, span_slot, group)
     loads[0].wait()
-    for step in range(GROUPS):
-        slot = picked(window, span_slot, goes_to(group, step), group)
+    for step, slot in enumerate(slots):
         for kv in range(2):
             source = heads.at[:, 2 * kv + slot]
             pltpu.make_async_copy(source, wide[step].at[kv], wide_sems.at[step]).start()
@@ -151,7 +157,7 @@
         load.wait()
     for to in range(SPACE):
         for w in range(WIN):
-            owner = span_slot[window[w, group * SPANS + to // 2]] >> 1
+            owner = owners[to // 2 * WIN + w]
             pltpu.make_async_copy(
                 held.at[owner, :, :, pl.ds(to % 2 * HD, HD)],
                 sent.at[to, pl.ds(unit_of(3, 2 * w), 2)],
@@ -192,13 +198,13 @@
             fetch(pair, 1 + kv, wide[step].at[kv], share(pair, 1 + kv, segment))
 
     fetch_pair(0)
+    owners = owners_of(window, span_slot, group)
     places = []
     for step in range(GROUPS):
-        owner = came_from(group, step)
+        source = came_from(group, step)
         place = jnp.int32(0)
-        for entry in range(SPANS * WIN):
-            slot = span_slot[window[entry % 2, group * SPANS + entry // 2]]
-            place = jnp.where((slot >> 1) == owner, entry, place)
+        for entry, owner in enumerate(owners):
+            place = jnp.where(owner == source, entry, place)
         places.append(place)
         pl.when(place < WIN)(lambda: fetch_wide(step, place))
     v_all[:, :, :, HD:] = jnp.ones((PAIRS, 3 * SPACE, ROWS, HD), jnp.bfloat16)

time: 132 us -> 131 us (level)
  no operation moved by 1% of the time
where the time goes in v6:
time: 131 us
  waiting for transfers between devices  50.7 us (39%)
  starting transfers between devices  46.5 us (35%)
  Pallas kernels  30 us (23%)
  local copies, waits for them, and re-layouts  3.21 us (2%)
    ppermute x17, waiting for transfers between devices, shift(): return lax.ppermute(x, axis, [(i, goes_to(i, step)) for i in range(8)])  45 us
    ppermute x17, starting transfers between devices, shift(): return lax.ppermute(x, axis, [(i, goes_to(i, step)) for i in range(8)])  22.1 us
    pallas_call x1, Pallas kernels, on_device(): pl.pallas_call(attend, out_shape=shape((2 * SPACE, PAIRS, ROWS, HD), bf16...  12.2 us
    pallas_call x1, Pallas kernels, on_device(): pl.pallas_call(project, out_shape=shape((SPANS * ROWS, columns), bf16), i...  8.24 us
    all_to_all x1, starting transfers between devices, on_device(): lax.all_to_all(by_head.reshape(SPACE, -1, HD), 'space', split_axis=0, con...  8.17 us
    all_to_all x1, starting transfers between devices, on_device(): lax.all_to_all(attended, ('space', 'head'), split_axis=0, concat_axis=0,...  6.89 us
    all_to_all x1, starting transfers between devices, on_device(): lax.all_to_all(pairs.reshape(SPACE, UNITS * ROWS, HD), 'space', split_axi...  4.61 us
    pallas_call x1, Pallas kernels, on_device(): pl.pallas_call(pack_cached, out_shape=[shape(pairs.shape, bf16)] + [shape...  3.6 us
  transfers between devices with their start and end apart: 26, of which 12 were waited for; matrix products, arithmetic and copies ran while one was open for 0% of the time, Pallas kernels for 14%

profile of v6, /device:TPU:0, one launch (start us, length us, event | category | flops | bytes accessed | tf_op | source)
XLA Modules:
  0.0 131.0 jit_solution(10615221124279396676)
XLA Ops:
  0.0 3.3 %pack_slots.1 = (bf16[8,6,80,128]{3,2,1,0:T(8,128)(2,1)}, bf16[2,80,256]{2,1,0:T(8,128)(2,1)}, bf16[2,80,256]{2,1,0:T(8,128)(2,1)}, bf16[2,80,256]{2,1,0:T(8,128...) custom-call(s32[2,32]{1,0:T(2,128)} %bitcast.12, ...), custom_call_target="tpu_custom_call" | custom-call | tf_op jit(solution)/shard_map/pack_slots/pallas_call | solution.py:346
  3.4 8.2 %all-to-all-start = ((bf16[8,480,128]{2,1,0:T(8,128)(2,1)}), bf16[8,480,128]{2,1,0:T(8,128)(2,1)S(1)}, u32[]{:S(2)}, u32[]{:S(2)}) async-start(bf16[8,480,128]{2,1,0:T(8,128)(2,1)} %bitcast.11), calls=%async_computation | async-start | bytes 1966080 | tf_op jit(solution)/shard_map/all_to_all | solution.py:365
  11.6 0.8 collective-permute-start.7
  12.3 3.3 %collective-permute-start.8 = (bf16[80,2560]{1,0:T(8,128)(2,1)S(1)}, bf16[80,2560]{1,0:T(8,128)(2,1)S(1)}, u32[]{:S(2)}, u32[]{:S(2)}) collective-permute-start(bf16[80,2560]{1,0:T(8,128)(2,1)S(1)} %copy-done.19), channel_id=1, source_target_pairs={{0,3},{1,2},{2,1},{3,0},{4,7},{5,6},{6,5},{7,4},{8,11},{9,10},{10,... | collective-permute-start | bytes 1228808 | tf_op jit(solution)/shard_map/ppermute | solution.py:371
  15.7 3.0 %collective-permute-start = (bf16[2,80,256]{2,1,0:T(8,128)(2,1)S(1)}, bf16[2,80,256]{2,1,0:T(8,128)(2,1)S(1)}, u32[]{:S(2)}, u32[]{:S(2)}) collective-permute-start(bf16[2,80,256]{2,1,0:T(8,128)(2,1)S(1)} %copy-done.29), channel_id=1, source_target_pairs={{0,64},{16,80},{32,96},{48,112},{64,0},{80,16},{96,32},{112,48},{1... | collective-permute-start | bytes 245768 | tf_op jit(solution)/shard_map/ppermute | solution.py:47
  18.7 0.0 collective-permute-start.1
  18.7 0.7 collective-permute-start.2
  19.4 2.2 %collective-permute-done.refs_1_ = bf16[2,80,256]{2,1,0:T(8,128)(2,1)S(1)} collective-permute-done((bf16[2,80,256]{2,1,0:T(8,128)(2,1)S(1)}, bf16[2,80,256]{2,1,0:T(8,128)(2,1)S(1)}, u32[]{:S(2)}, u32[]{:S(2)}) %collective-permute-start) | collective-permute-done | bytes 81952 | tf_op jit(solution)/shard_map/ppermute | solution.py:47
  21.6 2.8 %collective-permute-start.3 = (bf16[2,80,256]{2,1,0:T(8,128)(2,1)S(1)}, bf16[2,80,256]{2,1,0:T(8,128)(2,1)S(1)}, u32[]{:S(2)}, u32[]{:S(2)}) collective-permute-start(bf16[2,80,256]{2,1,0:T(8,128)(2,1)S(1)} %copy-done.26), channel_id=1, source_target_pairs={{0,96},{16,112},{32,0},{48,16},{64,32},{80,48},{96,64},{112,80},{1... | collective-permute-start | bytes 245768 | tf_op jit(solution)/shard_map/ppermute | solution.py:47
  24.5 0.4 collective-permute-done.1.refs_2_
  24.9 0.0 collective-permute-start.4
  24.9 0.9 collective-permute-done.2.refs_3_
  25.8 2.1 %collective-permute-start.5 = (bf16[2,80,256]{2,1,0:T(8,128)(2,1)S(1)}, bf16[2,80,256]{2,1,0:T(8,128)(2,1)S(1)}, u32[]{:S(2)}, u32[]{:S(2)}) collective-permute-start(bf16[2,80,256]{2,1,0:T(8,128)(2,1)S(1)} %copy-done.24), channel_id=1, source_target_pairs={{0,112},{16,96},{32,16},{48,0},{64,48},{80,32},{96,80},{112,64},{1... | collective-permute-start | bytes 245768 | tf_op jit(solution)/shard_map/ppermute | solution.py:47
  27.9 0.0 collective-permute-done.3.refs_4_
  27.9 0.1 collective-permute-start.6
  28.0 2.6 %pack_pairs.1.refs_8_ = bf16[8,17,80,128]{3,2,1,0:T(8,128)(2,1)} custom-call(bf16[4,80,1280]{2,1,0:T(8,128)(2,1)} %queries.2, bf16[4,80,1280]{2,1,0:T(8,128)(2,1)} %keys.1, bf16[4,80,1280]{2,1,0:T(8,128)(2,1)} %values.1), custom_call_target="tpu_custom_call" | custom-call | tf_op jit(solution)/shard_map/pack_pairs/pallas_call | solution.py:373
  30.8 0.6 copy-done.16
  31.3 0.1 copy-done.17
  31.4 0.0 copy-done.18
  31.4 0.3 copy-done
  31.8 3.6 %pack_cached.1 = (bf16[8,17,80,128]{3,2,1,0:T(8,128)(2,1)}, bf16[2,8,80,128]{3,2,1,0:T(8,128)(2,1)}, bf16[2,8,80,128]{3,2,1,0:T(8,128)(2,1)}, bf16[2,8,80,128]{3...) custom-call(s32[2,32]{1,0:T(2,128)} %bitcast.13, ...), custom_call_target="tpu_custom_call", output_to_operand_aliasing={{0}: (11, {})} | custom-call | tf_op jit(solution)/shard_map/pack_cached/pallas_call | solution.py:387
  35.4 0.0 copy-start.22
  35.4 4.6 %all-to-all-start.1 = ((bf16[8,1360,128]{2,1,0:T(8,128)(2,1)}), bf16[8,1360,128]{2,1,0:T(8,128)(2,1)}, u32[]{:S(2)}, u32[]{:S(2)}) async-start(bf16[8,1360,128]{2,1,0:T(8,128)(2,1)} %bitcast.7), calls=%async_computation.1 | async-start | bytes 5570560 | tf_op jit(solution)/shard_map/all_to_all | solution.py:404
  40.0 3.0 %collective-permute-start.9 = (bf16[2,8,80,128]{3,2,1,0:T(8,128)(2,1)S(1)}, bf16[2,8,80,128]{3,2,1,0:T(8,128)(2,1)S(1)}, u32[]{:S(2)}, u32[]{:S(2)}) collective-permute-start(bf16[2,8,80,128]{3,2,1,0:T(8,128)(2,1)S(1)} %copy-done.22), channel_id=1, source_target_pairs={{0,64},{16,80},{32,96},{48,112},{64,0},{80,16},{96,32},{112,48},{1... | collective-permute-start | bytes 983048 | tf_op jit(solution)/shard_map/ppermute | solution.py:47
  43.0 0.4 collective-permute-start.10
  43.4 0.3 collective-permute-start.11
  43.8 2.9 %collective-permute-start.12 = (bf16[2,8,80,128]{3,2,1,0:T(8,128)(2,1)}, bf16[2,8,80,128]{3,2,1,0:T(8,128)(2,1)S(1)}, u32[]{:S(2)}, u32[]{:S(2)}) collective-permute-start(bf16[2,8,80,128]{3,2,1,0:T(8,128)(2,1)} %get-tuple-element.98), channel_id=1, source_target_pairs={{0,96},{16,112},{32,0},{48,16},{64,32},{80,48},{96,64},{112,80},{1... | collective-permute-start | bytes 983048 | tf_op jit(solution)/shard_map/ppermute | solution.py:47
  46.7 5.6 %collective-permute-done.9.refs_3_ = bf16[2,8,80,128]{3,2,1,0:T(8,128)(2,1)S(1)} collective-permute-done((bf16[2,8,80,128]{3,2,1,0:T(8,128)(2,1)S(1)}, bf16[2,8,80,128]{3,2,1,0:T(8,128)(2,1)S(1)}, u32[]{:S(2)}, u32[]{:S(2)}) %collective-permute-start.9) | collective-permute-done | bytes 327712 | tf_op jit(solution)/shard_map/ppermute | solution.py:47
  52.2 1.1 collective-permute-start.14
  53.3 5.0 %collective-permute-done.10.refs_4_ = bf16[2,8,80,128]{3,2,1,0:T(8,128)(2,1)S(1)} collective-permute-done((bf16[2,8,80,128]{3,2,1,0:T(8,128)(2,1)S(1)}, bf16[2,8,80,128]{3,2,1,0:T(8,128)(2,1)S(1)}, u32[]{:S(2)}, u32[]{:S(2)}) %collective-permute-start.10) | collective-permute-done | bytes 327712 | tf_op jit(solution)/shard_map/ppermute | solution.py:47
  58.4 1.0 collective-permute-start.15
  59.4 0.1 pad_maximum_fusion.refs_0_
  59.5 6.3 %collective-permute-done.11.refs_5_ = bf16[2,8,80,128]{3,2,1,0:T(8,128)(2,1)S(1)} collective-permute-done((bf16[2,8,80,128]{3,2,1,0:T(8,128)(2,1)}, bf16[2,8,80,128]{3,2,1,0:T(8,128)(2,1)S(1)}, u32[]{:S(2)}, u32[]{:S(2)}) %collective-permute-start.11) | collective-permute-done | bytes 327712 | tf_op jit(solution)/shard_map/ppermute | solution.py:47
  65.8 0.4 collective-permute-done.12.refs_6_
  66.2 6.5 %collective-permute-done.13.refs_7_ = bf16[2,8,80,128]{3,2,1,0:T(8,128)(2,1)S(1)} collective-permute-done((bf16[2,8,80,128]{3,2,1,0:T(8,128)(2,1)}, bf16[2,8,80,128]{3,2,1,0:T(8,128)(2,1)S(1)}, u32[]{:S(2)}, u32[]{:S(2)}) %collective-permute-start.13) | collective-permute-done | bytes 327712 | tf_op jit(solution)/shard_map/ppermute | solution.py:47
  72.7 2.5 %collective-permute-start.18 = (bf16[160,2560]{1,0:T(8,128)(2,1)S(1)}, bf16[160,2560]{1,0:T(8,128)(2,1)}, u32[]{:S(2)}, u32[]{:S(2)}) collective-permute-start(bf16[160,2560]{1,0:T(8,128)(2,1)S(1)} %pad_maximum_fusion.refs_0_), channel_id=1, source_target_pairs={{0,96},{16,112},{32,0},{48,16},{64,32},{80,48},{96,64},{112,80},{1... | collective-permute-start | bytes 2457608 | tf_op jit(solution)/shard_map/ppermute | solution.py:47
  75.2 2.1 %collective-permute-start.16 = (bf16[160,2560]{1,0:T(8,128)(2,1)S(1)}, bf16[160,2560]{1,0:T(8,128)(2,1)S(1)}, u32[]{:S(2)}, u32[]{:S(2)}) collective-permute-start(bf16[160,2560]{1,0:T(8,128)(2,1)S(1)} %pad_maximum_fusion.refs_0_), channel_id=1, source_target_pairs={{0,64},{16,80},{32,96},{48,112},{64,0},{80,16},{96,32},{112,48},{1... | collective-permute-start | bytes 2457608 | tf_op jit(solution)/shard_map/ppermute | solution.py:47
  77.4 12.2 %attend.1 = bf16[16,5,80,128]{3,2,1,0:T(8,128)(2,1)} custom-call(s32[2,32]{1,0:T(2,128)} %bitcast.14, s32[16]{0:T(128)} %span_slot.5, s32[16]{0:T(128)} %counts.1, bf16[8,6,80,128]{3,2,1,0:T(8,128)(2,1)} %bitcast.9, bf16[8,17,80,128]{3,2,1,0:T(8,128)(2,1)} %bitcast.4.refs_1_, bf16[2,8,80,128]{3,2,1,0:T(8,128)(2,1)} %get-tuple-element.102.refs_2_, ...), custom_call_target="tpu_custom_call" | custom-call | tf_op jit(solution)/shard_map/attend/pallas_call | solution.py:413
  89.6 6.9 %all-to-all-start.2 = ((bf16[16,400,128]{2,1,0:T(8,128)(2,1)}), bf16[16,400,128]{2,1,0:T(8,128)(2,1)S(1)}, u32[]{:S(2)}, u32[]{:S(2)}) async-start(bf16[16,400,128]{2,1,0:T(8,128)(2,1)} %bitcast.10), calls=%async_computation.2 | async-start | bytes 3276800 | tf_op jit(solution)/shard_map/all_to_all | solution.py:430
  96.5 0.1 collective-permute-start.19
  96.6 14.2 %collective-permute-done.18.refs_3_ = bf16[160,2560]{1,0:T(8,128)(2,1)} collective-permute-done((bf16[160,2560]{1,0:T(8,128)(2,1)S(1)}, bf16[160,2560]{1,0:T(8,128)(2,1)}, u32[]{:S(2)}, u32[]{:S(2)}) %collective-permute-start.18) | collective-permute-done | bytes 819232 | tf_op jit(solution)/shard_map/ppermute | solution.py:47
  110.7 3.5 %collective-permute-done.17.refs_2_ = bf16[160,2560]{1,0:T(8,128)(2,1)} collective-permute-done((bf16[160,2560]{1,0:T(8,128)(2,1)S(1)}, bf16[160,2560]{1,0:T(8,128)(2,1)}, u32[]{:S(2)}, u32[]{:S(2)}) %collective-permute-start.17) | collective-permute-done | bytes 819232 | tf_op jit(solution)/shard_map/ppermute | solution.py:47
  114.2 0.5 collective-permute-start.20
  114.8 3.1 %collective-permute-done.21.refs_6_ = bf16[160,2560]{1,0:T(8,128)(2,1)S(1)} collective-permute-done((bf16[160,2560]{1,0:T(8,128)(2,1)}, bf16[160,2560]{1,0:T(8,128)(2,1)S(1)}, u32[]{:S(2)}, u32[]{:S(2)}) %collective-permute-start.21) | collective-permute-done | bytes 819232 | tf_op jit(solution)/shard_map/ppermute | solution.py:411
  117.9 0.9 copy-done.4
  118.8 2.6 %all-to-all-done.2.came = bf16[16,400,128]{2,1,0:T(8,128)(2,1)S(1)} async-done(((bf16[16,400,128]{2,1,0:T(8,128)(2,1)}), bf16[16,400,128]{2,1,0:T(8,128)(2,1)S(1)}, u32[]{:S(2)}, u32[]{:S(2)}) %all-to-all-start.2) | async-done | bytes 1638432 | tf_op jit(solution)/shard_map/all_to_all | solution.py:430
  121.3 1.2 copy-done.1
  122.6 8.2 %project.1 = bf16[320,2560]{1,0:T(8,128)(2,1)} custom-call(bf16[16,400,128]{2,1,0:T(8,128)(2,1)} %copy-done.1, bf16[1280,5120]{1,0:T(8,128)(2,1)} %own_weight.1, bf16[160,2560]{1,0:T(8,128)(2,1)S(1)} %pad_maximum_fusion.refs_0_, bf16[160,2560]{1,0:T(8,128)(2,1)S(1)} %collective-permute-done.16.refs_1_, bf16[160,2560]{1,0:T(8,128)(2,1)} %collective-permute-done.17.refs_2_, ...), custom_call_target="tpu_custom_call" | custom-call | tf_op jit(solution)/shard_map/project/pallas_call | solution.py:436
  (70 shorter events, 0.1 us)
Async XLA Ops:
  3.3 8.3 %copy-start.20 = (bf16[80,2560]{1,0:T(8,128)(2,1)S(1)}, bf16[80,2560]{1,0:T(8,128)(2,1)}, u32[]{:S(2)}) copy-start(bf16[80,2560]{1,0:T(8,128)(2,1)} %get-tuple-element.89) | copy-start | bytes 1228804
  3.3 9.0 %copy-start.19 = (bf16[80,2560]{1,0:T(8,128)(2,1)S(1)}, bf16[80,2560]{1,0:T(8,128)(2,1)}, u32[]{:S(2)}) copy-start(bf16[80,2560]{1,0:T(8,128)(2,1)} %get-tuple-element.90) | copy-start | bytes 1228804
  3.3 12.3 %copy-start.29 = (bf16[2,80,256]{2,1,0:T(8,128)(2,1)S(1)}, bf16[2,80,256]{2,1,0:T(8,128)(2,1)}, u32[]{:S(2)}) copy-start(bf16[2,80,256]{2,1,0:T(8,128)(2,1)} %get-tuple-element.71) | copy-start | bytes 245764
  3.3 15.4 %copy-start.28 = (bf16[2,80,256]{2,1,0:T(8,128)(2,1)S(1)}, bf16[2,80,256]{2,1,0:T(8,128)(2,1)}, u32[]{:S(2)}) copy-start(bf16[2,80,256]{2,1,0:T(8,128)(2,1)} %get-tuple-element.72) | copy-start | bytes 245764
  3.4 15.4 %copy-start.27 = (bf16[2,80,256]{2,1,0:T(8,128)(2,1)S(1)}, bf16[2,80,256]{2,1,0:T(8,128)(2,1)}, u32[]{:S(2)}) copy-start(bf16[2,80,256]{2,1,0:T(8,128)(2,1)} %get-tuple-element.73) | copy-start | bytes 245764
  3.4 18.3 %copy-start.26 = (bf16[2,80,256]{2,1,0:T(8,128)(2,1)S(1)}, bf16[2,80,256]{2,1,0:T(8,128)(2,1)}, u32[]{:S(2)}) copy-start(bf16[2,80,256]{2,1,0:T(8,128)(2,1)} %get-tuple-element.74) | copy-start | bytes 245764
  3.4 21.5 %copy-start.25 = (bf16[2,80,256]{2,1,0:T(8,128)(2,1)S(1)}, bf16[2,80,256]{2,1,0:T(8,128)(2,1)}, u32[]{:S(2)}) copy-start(bf16[2,80,256]{2,1,0:T(8,128)(2,1)} %get-tuple-element.75) | copy-start | bytes 245764
  3.4 22.4 %copy-start.24 = (bf16[2,80,256]{2,1,0:T(8,128)(2,1)S(1)}, bf16[2,80,256]{2,1,0:T(8,128)(2,1)}, u32[]{:S(2)}) copy-start(bf16[2,80,256]{2,1,0:T(8,128)(2,1)} %get-tuple-element.76) | copy-start | bytes 245764
  3.4 24.5 %copy-start.23 = (bf16[2,80,256]{2,1,0:T(8,128)(2,1)S(1)}, bf16[2,80,256]{2,1,0:T(8,128)(2,1)}, u32[]{:S(2)}) copy-start(bf16[2,80,256]{2,1,0:T(8,128)(2,1)} %get-tuple-element.77) | copy-start | bytes 245764
  3.4 27.3 %all-to-all-start = ((bf16[8,480,128]{2,1,0:T(8,128)(2,1)}), bf16[8,480,128]{2,1,0:T(8,128)(2,1)S(1)}, u32[]{:S(2)}, u32[]{:S(2)}) async-start(bf16[8,480,128]{2,1,0:T(8,128)(2,1)} %bitcast.11), calls=%async_computation | async-start | bytes 1966080 | tf_op jit(solution)/shard_map/all_to_all | solution.py:365
  11.6 23.8 %collective-permute-start.7 = (bf16[80,2560]{1,0:T(8,128)(2,1)S(1)}, bf16[80,2560]{1,0:T(8,128)(2,1)S(1)}, u32[]{:S(2)}, u32[]{:S(2)}) collective-permute-start(bf16[80,2560]{1,0:T(8,128)(2,1)S(1)} %copy-done.20), channel_id=1, source_target_pairs={{0,1},{1,0},{2,3},{3,2},{4,5},{5,4},{6,7},{7,6},{8,9},{9,8},{10,11... | collective-permute-start | bytes 1228808 | tf_op jit(solution)/shard_map/ppermute | solution.py:370
  12.3 23.0 %collective-permute-start.8 = (bf16[80,2560]{1,0:T(8,128)(2,1)S(1)}, bf16[80,2560]{1,0:T(8,128)(2,1)S(1)}, u32[]{:S(2)}, u32[]{:S(2)}) collective-permute-start(bf16[80,2560]{1,0:T(8,128)(2,1)S(1)} %copy-done.19), channel_id=1, source_target_pairs={{0,3},{1,2},{2,1},{3,0},{4,7},{5,6},{6,5},{7,4},{8,11},{9,10},{10,... | collective-permute-start | bytes 1228808 | tf_op jit(solution)/shard_map/ppermute | solution.py:371
  15.7 5.9 %collective-permute-start = (bf16[2,80,256]{2,1,0:T(8,128)(2,1)S(1)}, bf16[2,80,256]{2,1,0:T(8,128)(2,1)S(1)}, u32[]{:S(2)}, u32[]{:S(2)}) collective-permute-start(bf16[2,80,256]{2,1,0:T(8,128)(2,1)S(1)} %copy-done.29), channel_id=1, source_target_pairs={{0,64},{16,80},{32,96},{48,112},{64,0},{80,16},{96,32},{112,48},{1... | collective-permute-start | bytes 245768 | tf_op jit(solution)/shard_map/ppermute | solution.py:47
  18.7 6.2 %collective-permute-start.1 = (bf16[2,80,256]{2,1,0:T(8,128)(2,1)S(1)}, bf16[2,80,256]{2,1,0:T(8,128)(2,1)S(1)}, u32[]{:S(2)}, u32[]{:S(2)}) collective-permute-start(bf16[2,80,256]{2,1,0:T(8,128)(2,1)S(1)} %copy-done.28), channel_id=1, source_target_pairs={{0,80},{16,64},{32,112},{48,96},{64,16},{80,0},{96,48},{112,32},{1... | collective-permute-start | bytes 245768 | tf_op jit(solution)/shard_map/ppermute | solution.py:47
  18.7 7.1 %collective-permute-start.2 = (bf16[2,80,256]{2,1,0:T(8,128)(2,1)S(1)}, bf16[2,80,256]{2,1,0:T(8,128)(2,1)S(1)}, u32[]{:S(2)}, u32[]{:S(2)}) collective-permute-start(bf16[2,80,256]{2,1,0:T(8,128)(2,1)S(1)} %copy-done.27), channel_id=1, source_target_pairs={{0,32},{16,48},{32,64},{48,80},{64,96},{80,112},{96,0},{112,16},{1... | collective-permute-start | bytes 245768 | tf_op jit(solution)/shard_map/ppermute | solution.py:47
  21.6 9.0 %copy-start.12 = (bf16[2,80,256]{2,1,0:T(8,128)(2,1)}, bf16[2,80,256]{2,1,0:T(8,128)(2,1)S(1)}, u32[]{:S(2)}) copy-start(bf16[2,80,256]{2,1,0:T(8,128)(2,1)S(1)} %collective-permute-done.refs_1_) | copy-start | bytes 245764
  21.6 6.3 %collective-permute-start.3 = (bf16[2,80,256]{2,1,0:T(8,128)(2,1)S(1)}, bf16[2,80,256]{2,1,0:T(8,128)(2,1)S(1)}, u32[]{:S(2)}, u32[]{:S(2)}) collective-permute-start(bf16[2,80,256]{2,1,0:T(8,128)(2,1)S(1)} %copy-done.26), channel_id=1, source_target_pairs={{0,96},{16,112},{32,0},{48,16},{64,32},{80,48},{96,64},{112,80},{1... | collective-permute-start | bytes 245768 | tf_op jit(solution)/shard_map/ppermute | solution.py:47
  24.9 5.8 %copy-start.13 = (bf16[2,80,256]{2,1,0:T(8,128)(2,1)}, bf16[2,80,256]{2,1,0:T(8,128)(2,1)S(1)}, u32[]{:S(2)}) copy-start(bf16[2,80,256]{2,1,0:T(8,128)(2,1)S(1)} %collective-permute-done.1.refs_2_) | copy-start | bytes 245764
  24.9 5.8 %collective-permute-start.4 = (bf16[2,80,256]{2,1,0:T(8,128)(2,1)S(1)}, bf16[2,80,256]{2,1,0:T(8,128)(2,1)S(1)}, u32[]{:S(2)}, u32[]{:S(2)}) collective-permute-start(bf16[2,80,256]{2,1,0:T(8,128)(2,1)S(1)} %copy-done.25), channel_id=1, source_target_pairs={{0,48},{16,32},{32,80},{48,64},{64,112},{80,96},{96,16},{112,0},{1... | collective-permute-start | bytes 245768 | tf_op jit(solution)/shard_map/ppermute | solution.py:47
  25.8 4.9 %copy-start.14 = (bf16[2,80,256]{2,1,0:T(8,128)(2,1)}, bf16[2,80,256]{2,1,0:T(8,128)(2,1)S(1)}, u32[]{:S(2)}) copy-start(bf16[2,80,256]{2,1,0:T(8,128)(2,1)S(1)} %collective-permute-done.2.refs_3_) | copy-start | bytes 245764
  25.8 4.9 %collective-permute-start.5 = (bf16[2,80,256]{2,1,0:T(8,128)(2,1)S(1)}, bf16[2,80,256]{2,1,0:T(8,128)(2,1)S(1)}, u32[]{:S(2)}, u32[]{:S(2)}) collective-permute-start(bf16[2,80,256]{2,1,0:T(8,128)(2,1)S(1)} %copy-done.24), channel_id=1, source_target_pairs={{0,112},{16,96},{32,16},{48,0},{64,48},{80,32},{96,80},{112,64},{1... | collective-permute-start | bytes 245768 | tf_op jit(solution)/shard_map/ppermute | solution.py:47
  27.9 2.8 %copy-start.15 = (bf16[2,80,256]{2,1,0:T(8,128)(2,1)}, bf16[2,80,256]{2,1,0:T(8,128)(2,1)S(1)}, u32[]{:S(2)}) copy-start(bf16[2,80,256]{2,1,0:T(8,128)(2,1)S(1)} %collective-permute-done.3.refs_4_) | copy-start | bytes 245764
  27.9 2.8 %collective-permute-start.6 = (bf16[2,80,256]{2,1,0:T(8,128)(2,1)S(1)}, bf16[2,80,256]{2,1,0:T(8,128)(2,1)S(1)}, u32[]{:S(2)}, u32[]{:S(2)}) collective-permute-start(bf16[2,80,256]{2,1,0:T(8,128)(2,1)S(1)} %copy-done.23), channel_id=1, source_target_pairs={{0,16},{16,0},{32,48},{48,32},{64,80},{80,64},{96,112},{112,96},{1... | collective-permute-start | bytes 245768 | tf_op jit(solution)/shard_map/ppermute | solution.py:47
  35.4 4.6 %copy-start.22 = (bf16[2,8,80,128]{3,2,1,0:T(8,128)(2,1)S(1)}, bf16[2,8,80,128]{3,2,1,0:T(8,128)(2,1)}, u32[]{:S(2)}) copy-start(bf16[2,8,80,128]{3,2,1,0:T(8,128)(2,1)} %get-tuple-element.95) | copy-start | bytes 983044
  35.4 7.6 %copy-start.21 = (bf16[2,8,80,128]{3,2,1,0:T(8,128)(2,1)S(1)}, bf16[2,8,80,128]{3,2,1,0:T(8,128)(2,1)}, u32[]{:S(2)}) copy-start(bf16[2,8,80,128]{3,2,1,0:T(8,128)(2,1)} %get-tuple-element.96) | copy-start | bytes 983044
  35.4 41.9 %all-to-all-start.1 = ((bf16[8,1360,128]{2,1,0:T(8,128)(2,1)}), bf16[8,1360,128]{2,1,0:T(8,128)(2,1)}, u32[]{:S(2)}, u32[]{:S(2)}) async-start(bf16[8,1360,128]{2,1,0:T(8,128)(2,1)} %bitcast.7), calls=%async_computation.1 | async-start | bytes 5570560 | tf_op jit(solution)/shard_map/all_to_all | solution.py:404
  40.0 12.2 %collective-permute-start.9 = (bf16[2,8,80,128]{3,2,1,0:T(8,128)(2,1)S(1)}, bf16[2,8,80,128]{3,2,1,0:T(8,128)(2,1)S(1)}, u32[]{:S(2)}, u32[]{:S(2)}) collective-permute-start(bf16[2,8,80,128]{3,2,1,0:T(8,128)(2,1)S(1)} %copy-done.22), channel_id=1, source_target_pairs={{0,64},{16,80},{32,96},{48,112},{64,0},{80,16},{96,32},{112,48},{1... | collective-permute-start | bytes 983048 | tf_op jit(solution)/shard_map/ppermute | solution.py:47
  43.0 15.4 %collective-permute-start.10 = (bf16[2,8,80,128]{3,2,1,0:T(8,128)(2,1)S(1)}, bf16[2,8,80,128]{3,2,1,0:T(8,128)(2,1)S(1)}, u32[]{:S(2)}, u32[]{:S(2)}) collective-permute-start(bf16[2,8,80,128]{3,2,1,0:T(8,128)(2,1)S(1)} %copy-done.21), channel_id=1, source_target_pairs={{0,80},{16,64},{32,112},{48,96},{64,16},{80,0},{96,48},{112,32},{1... | collective-permute-start | bytes 983048 | tf_op jit(solution)/shard_map/ppermute | solution.py:47
  43.4 22.4 %collective-permute-start.11 = (bf16[2,8,80,128]{3,2,1,0:T(8,128)(2,1)}, bf16[2,8,80,128]{3,2,1,0:T(8,128)(2,1)S(1)}, u32[]{:S(2)}, u32[]{:S(2)}) collective-permute-start(bf16[2,8,80,128]{3,2,1,0:T(8,128)(2,1)} %get-tuple-element.97), channel_id=1, source_target_pairs={{0,32},{16,48},{32,64},{48,80},{64,96},{80,112},{96,0},{112,16},{1... | collective-permute-start | bytes 983048 | tf_op jit(solution)/shard_map/ppermute | solution.py:47
  43.8 22.4 %collective-permute-start.12 = (bf16[2,8,80,128]{3,2,1,0:T(8,128)(2,1)}, bf16[2,8,80,128]{3,2,1,0:T(8,128)(2,1)S(1)}, u32[]{:S(2)}, u32[]{:S(2)}) collective-permute-start(bf16[2,8,80,128]{3,2,1,0:T(8,128)(2,1)} %get-tuple-element.98), channel_id=1, source_target_pairs={{0,96},{16,112},{32,0},{48,16},{64,32},{80,48},{96,64},{112,80},{1... | collective-permute-start | bytes 983048 | tf_op jit(solution)/shard_map/ppermute | solution.py:47
  46.7 26.0 %collective-permute-start.13 = (bf16[2,8,80,128]{3,2,1,0:T(8,128)(2,1)}, bf16[2,8,80,128]{3,2,1,0:T(8,128)(2,1)S(1)}, u32[]{:S(2)}, u32[]{:S(2)}) collective-permute-start(bf16[2,8,80,128]{3,2,1,0:T(8,128)(2,1)} %get-tuple-element.99), channel_id=1, source_target_pairs={{0,48},{16,32},{32,80},{48,64},{64,112},{80,96},{96,16},{112,0},{1... | collective-permute-start | bytes 983048 | tf_op jit(solution)/shard_map/ppermute | solution.py:47
  52.2 25.1 %copy-start.5 = (bf16[2,8,80,128]{3,2,1,0:T(8,128)(2,1)}, bf16[2,8,80,128]{3,2,1,0:T(8,128)(2,1)S(1)}, u32[]{:S(2)}) copy-start(bf16[2,8,80,128]{3,2,1,0:T(8,128)(2,1)S(1)} %collective-permute-done.9.refs_3_) | copy-start | bytes 983044
  52.2 20.5 %collective-permute-start.14 = (bf16[2,8,80,128]{3,2,1,0:T(8,128)(2,1)}, bf16[2,8,80,128]{3,2,1,0:T(8,128)(2,1)S(1)}, u32[]{:S(2)}, u32[]{:S(2)}) collective-permute-start(bf16[2,8,80,128]{3,2,1,0:T(8,128)(2,1)} %get-tuple-element.100), channel_id=1, source_target_pairs={{0,112},{16,96},{32,16},{48,0},{64,48},{80,32},{96,80},{112,64},{1... | collective-permute-start | bytes 983048 | tf_op jit(solution)/shard_map/ppermute | solution.py:47
  58.4 19.0 %copy-start.6 = (bf16[2,8,80,128]{3,2,1,0:T(8,128)(2,1)}, bf16[2,8,80,128]{3,2,1,0:T(8,128)(2,1)S(1)}, u32[]{:S(2)}) copy-start(bf16[2,8,80,128]{3,2,1,0:T(8,128)(2,1)S(1)} %collective-permute-done.10.refs_4_) | copy-start | bytes 983044
  58.4 14.3 %collective-permute-start.15 = (bf16[2,8,80,128]{3,2,1,0:T(8,128)(2,1)}, bf16[2,8,80,128]{3,2,1,0:T(8,128)(2,1)S(1)}, u32[]{:S(2)}, u32[]{:S(2)}) collective-permute-start(bf16[2,8,80,128]{3,2,1,0:T(8,128)(2,1)} %get-tuple-element.101), channel_id=1, source_target_pairs={{0,16},{16,0},{32,48},{48,32},{64,80},{80,64},{96,112},{112,96},{1... | collective-permute-start | bytes 983048 | tf_op jit(solution)/shard_map/ppermute | solution.py:47
  65.8 11.5 %copy-start.7 = (bf16[2,8,80,128]{3,2,1,0:T(8,128)(2,1)}, bf16[2,8,80,128]{3,2,1,0:T(8,128)(2,1)S(1)}, u32[]{:S(2)}) copy-start(bf16[2,8,80,128]{3,2,1,0:T(8,128)(2,1)S(1)} %collective-permute-done.11.refs_5_) | copy-start | bytes 983044
  66.2 11.1 %copy-start.8 = (bf16[2,8,80,128]{3,2,1,0:T(8,128)(2,1)}, bf16[2,8,80,128]{3,2,1,0:T(8,128)(2,1)S(1)}, u32[]{:S(2)}) copy-start(bf16[2,8,80,128]{3,2,1,0:T(8,128)(2,1)S(1)} %collective-permute-done.12.refs_6_) | copy-start | bytes 983044
  72.7 4.7 %copy-start.9 = (bf16[2,8,80,128]{3,2,1,0:T(8,128)(2,1)}, bf16[2,8,80,128]{3,2,1,0:T(8,128)(2,1)S(1)}, u32[]{:S(2)}) copy-start(bf16[2,8,80,128]{3,2,1,0:T(8,128)(2,1)S(1)} %collective-permute-done.13.refs_7_) | copy-start | bytes 983044
  72.7 38.0 %collective-permute-start.18 = (bf16[160,2560]{1,0:T(8,128)(2,1)S(1)}, bf16[160,2560]{1,0:T(8,128)(2,1)}, u32[]{:S(2)}, u32[]{:S(2)}) collective-permute-start(bf16[160,2560]{1,0:T(8,128)(2,1)S(1)} %pad_maximum_fusion.refs_0_), channel_id=1, source_target_pairs={{0,96},{16,112},{32,0},{48,16},{64,32},{80,48},{96,64},{112,80},{1... | collective-permute-start | bytes 2457608 | tf_op jit(solution)/shard_map/ppermute | solution.py:47
  75.2 39.0 %collective-permute-start.17 = (bf16[160,2560]{1,0:T(8,128)(2,1)S(1)}, bf16[160,2560]{1,0:T(8,128)(2,1)}, u32[]{:S(2)}, u32[]{:S(2)}) collective-permute-start(bf16[160,2560]{1,0:T(8,128)(2,1)S(1)} %pad_maximum_fusion.refs_0_), channel_id=1, source_target_pairs={{0,32},{16,48},{32,64},{48,80},{64,96},{80,112},{96,0},{112,16},{1... | collective-permute-start | bytes 2457608 | tf_op jit(solution)/shard_map/ppermute | solution.py:47
  75.2 39.0 %collective-permute-start.16 = (bf16[160,2560]{1,0:T(8,128)(2,1)S(1)}, bf16[160,2560]{1,0:T(8,128)(2,1)S(1)}, u32[]{:S(2)}, u32[]{:S(2)}) collective-permute-start(bf16[160,2560]{1,0:T(8,128)(2,1)S(1)} %pad_maximum_fusion.refs_0_), channel_id=1, source_target_pairs={{0,64},{16,80},{32,96},{48,112},{64,0},{80,16},{96,32},{112,48},{1... | collective-permute-start | bytes 2457608 | tf_op jit(solution)/shard_map/ppermute | solution.py:47
  89.6 31.8 %all-to-all-start.2 = ((bf16[16,400,128]{2,1,0:T(8,128)(2,1)}), bf16[16,400,128]{2,1,0:T(8,128)(2,1)S(1)}, u32[]{:S(2)}, u32[]{:S(2)}) async-start(bf16[16,400,128]{2,1,0:T(8,128)(2,1)} %bitcast.10), calls=%async_computation.2 | async-start | bytes 3276800 | tf_op jit(solution)/shard_map/all_to_all | solution.py:430
  96.5 18.3 %collective-permute-start.19 = (bf16[160,2560]{1,0:T(8,128)(2,1)S(1)}, bf16[160,2560]{1,0:T(8,128)(2,1)S(1)}, u32[]{:S(2)}, u32[]{:S(2)}) collective-permute-start(bf16[160,2560]{1,0:T(8,128)(2,1)S(1)} %pad_maximum_fusion.refs_0_), channel_id=1, source_target_pairs={{0,16},{16,0},{32,48},{48,32},{64,80},{80,64},{96,112},{112,96},{1... | collective-permute-start | bytes 2457608 | tf_op jit(solution)/shard_map/ppermute | solution.py:411
  110.7 4.0 %collective-permute-start.22 = (bf16[160,2560]{1,0:T(8,128)(2,1)}, bf16[160,2560]{1,0:T(8,128)(2,1)S(1)}, u32[]{:S(2)}, u32[]{:S(2)}) collective-permute-start(bf16[160,2560]{1,0:T(8,128)(2,1)} %collective-permute-done.18.refs_3_), channel_id=1, source_target_pairs={{0,16},{16,0},{32,48},{48,32},{64,80},{80,64},{96,112},{112,96},{1... | collective-permute-start | bytes 2457608 | tf_op jit(solution)/shard_map/ppermute | solution.py:411
  114.2 3.6 %collective-permute-start.21 = (bf16[160,2560]{1,0:T(8,128)(2,1)}, bf16[160,2560]{1,0:T(8,128)(2,1)S(1)}, u32[]{:S(2)}, u32[]{:S(2)}) collective-permute-start(bf16[160,2560]{1,0:T(8,128)(2,1)} %collective-permute-done.17.refs_2_), channel_id=1, source_target_pairs={{0,16},{16,0},{32,48},{48,32},{64,80},{80,64},{96,112},{112,96},{1... | collective-permute-start | bytes 2457608 | tf_op jit(solution)/shard_map/ppermute | solution.py:411
  114.2 4.5 %collective-permute-start.20 = (bf16[160,2560]{1,0:T(8,128)(2,1)S(1)}, bf16[160,2560]{1,0:T(8,128)(2,1)}, u32[]{:S(2)}, u32[]{:S(2)}) collective-permute-start(bf16[160,2560]{1,0:T(8,128)(2,1)S(1)} %collective-permute-done.16.refs_1_), channel_id=1, source_target_pairs={{0,16},{16,0},{32,48},{48,32},{64,80},{80,64},{96,112},{112,96},{1... | collective-permute-start | bytes 2457608 | tf_op jit(solution)/shard_map/ppermute | solution.py:411
  114.7 3.1 %copy-start.2 = (bf16[160,2560]{1,0:T(8,128)(2,1)}, bf16[160,2560]{1,0:T(8,128)(2,1)S(1)}, u32[]{:S(2)}) copy-start(bf16[160,2560]{1,0:T(8,128)(2,1)S(1)} %collective-permute-done.19.refs_4_) | copy-start | bytes 2457604
  114.8 3.1 %copy-start.3 = (bf16[160,2560]{1,0:T(8,128)(2,1)}, bf16[160,2560]{1,0:T(8,128)(2,1)S(1)}, u32[]{:S(2)}) copy-start(bf16[160,2560]{1,0:T(8,128)(2,1)S(1)} %collective-permute-done.22.refs_7_) | copy-start | bytes 2457604
  (8 other events, 10.0 us)

commit v7 on v6

--- a/solution.py
+++ b/solution.py
@@ -220,7 +220,7 @@
             extent = (SPACE // 2, ROWS, HD)
             spots = SPAN // 2 + lax.broadcasted_iota(jnp.int32, extent, 1)
             valid = spots + ROWS * lax.broadcasted_iota(jnp.int32, extent, 0) < limit
-            key = k_all[pair, first, 0:1].astype(jnp.float32)
+            key = k_all[pair, first, 0:16].astype(jnp.float32)[0:1]
             key = jnp.broadcast_to(key[None], extent)
             held = k_all[pair, half].astype(jnp.float32)
             k_all[pair, half] = jnp.where(valid, held, key).astype(jnp.bfloat16)

time: 131 us -> 131 us (level)
  no operation moved by 1% of the time
where the time goes in v7:
time: 131 us
  waiting for transfers between devices  50.7 us (39%)
  starting transfers between devices  46.5 us (35%)
  Pallas kernels  30 us (23%)
  local copies, waits for them, and re-layouts  3.21 us (2%)
    ppermute x17, waiting for transfers between devices, shift(): return lax.ppermute(x, axis, [(i, goes_to(i, step)) for i in range(8)])  45 us
    ppermute x17, starting transfers between devices, shift(): return lax.ppermute(x, axis, [(i, goes_to(i, step)) for i in range(8)])  22.1 us
    pallas_call x1, Pallas kernels, on_device(): pl.pallas_call(attend, out_shape=shape((2 * SPACE, PAIRS, ROWS, HD), bf16...  12.2 us
    pallas_call x1, Pallas kernels, on_device(): pl.pallas_call(project, out_shape=shape((SPANS * ROWS, columns), bf16), i...  8.24 us
    all_to_all x1, starting transfers between devices, on_device(): lax.all_to_all(by_head.reshape(SPACE, -1, HD), 'space', split_axis=0, con...  8.17 us
    all_to_all x1, starting transfers between devices, on_device(): lax.all_to_all(attended, ('space', 'head'), split_axis=0, concat_axis=0,...  6.9 us
    all_to_all x1, starting transfers between devices, on_device(): lax.all_to_all(pairs.reshape(SPACE, UNITS * ROWS, HD), 'space', split_axi...  4.61 us
    pallas_call x1, Pallas kernels, on_device(): pl.pallas_call(pack_cached, out_shape=[shape(pairs.shape, bf16)] + [shape...  3.6 us
  transfers between devices with their start and end apart: 26, of which 12 were waited for; matrix products, arithmetic and copies ran while one was open for 0% of the time, Pallas kernels for 14%

profile of v7, /device:TPU:0, one launch (start us, length us, event | category | flops | bytes accessed | tf_op | source)
XLA Modules:
  0.0 131.0 jit_solution(1697690689847926850)
XLA Ops:
  0.0 3.3 %pack_slots.1 = (bf16[8,6,80,128]{3,2,1,0:T(8,128)(2,1)}, bf16[2,80,256]{2,1,0:T(8,128)(2,1)}, bf16[2,80,256]{2,1,0:T(8,128)(2,1)}, bf16[2,80,256]{2,1,0:T(8,128...) custom-call(s32[2,32]{1,0:T(2,128)} %bitcast.12, ...), custom_call_target="tpu_custom_call" | custom-call | tf_op jit(solution)/shard_map/pack_slots/pallas_call | solution.py:346
  3.4 8.2 %all-to-all-start = ((bf16[8,480,128]{2,1,0:T(8,128)(2,1)}), bf16[8,480,128]{2,1,0:T(8,128)(2,1)S(1)}, u32[]{:S(2)}, u32[]{:S(2)}) async-start(bf16[8,480,128]{2,1,0:T(8,128)(2,1)} %bitcast.11), calls=%async_computation | async-start | bytes 1966080 | tf_op jit(solution)/shard_map/all_to_all | solution.py:365
  11.6 0.8 collective-permute-start.7
  12.3 3.3 %collective-permute-start.8 = (bf16[80,2560]{1,0:T(8,128)(2,1)S(1)}, bf16[80,2560]{1,0:T(8,128)(2,1)S(1)}, u32[]{:S(2)}, u32[]{:S(2)}) collective-permute-start(bf16[80,2560]{1,0:T(8,128)(2,1)S(1)} %copy-done.19), channel_id=1, source_target_pairs={{0,3},{1,2},{2,1},{3,0},{4,7},{5,6},{6,5},{7,4},{8,11},{9,10},{10,... | collective-permute-start | bytes 1228808 | tf_op jit(solution)/shard_map/ppermute | solution.py:371
  15.7 3.0 %collective-permute-start = (bf16[2,80,256]{2,1,0:T(8,128)(2,1)S(1)}, bf16[2,80,256]{2,1,0:T(8,128)(2,1)S(1)}, u32[]{:S(2)}, u32[]{:S(2)}) collective-permute-start(bf16[2,80,256]{2,1,0:T(8,128)(2,1)S(1)} %copy-done.29), channel_id=1, source_target_pairs={{0,64},{16,80},{32,96},{48,112},{64,0},{80,16},{96,32},{112,48},{1... | collective-permute-start | bytes 245768 | tf_op jit(solution)/shard_map/ppermute | solution.py:47
  18.7 0.7 collective-permute-start.2
  19.4 2.2 %collective-permute-done.refs_1_ = bf16[2,80,256]{2,1,0:T(8,128)(2,1)S(1)} collective-permute-done((bf16[2,80,256]{2,1,0:T(8,128)(2,1)S(1)}, bf16[2,80,256]{2,1,0:T(8,128)(2,1)S(1)}, u32[]{:S(2)}, u32[]{:S(2)}) %collective-permute-start) | collective-permute-done | bytes 81952 | tf_op jit(solution)/shard_map/ppermute | solution.py:47
  21.6 2.8 %collective-permute-start.3 = (bf16[2,80,256]{2,1,0:T(8,128)(2,1)S(1)}, bf16[2,80,256]{2,1,0:T(8,128)(2,1)S(1)}, u32[]{:S(2)}, u32[]{:S(2)}) collective-permute-start(bf16[2,80,256]{2,1,0:T(8,128)(2,1)S(1)} %copy-done.26), channel_id=1, source_target_pairs={{0,96},{16,112},{32,0},{48,16},{64,32},{80,48},{96,64},{112,80},{1... | collective-permute-start | bytes 245768 | tf_op jit(solution)/shard_map/ppermute | solution.py:47
  24.5 0.4 collective-permute-done.1.refs_2_
  24.9 0.9 collective-permute-done.2.refs_3_
  25.8 2.1 %collective-permute-start.5 = (bf16[2,80,256]{2,1,0:T(8,128)(2,1)S(1)}, bf16[2,80,256]{2,1,0:T(8,128)(2,1)S(1)}, u32[]{:S(2)}, u32[]{:S(2)}) collective-permute-start(bf16[2,80,256]{2,1,0:T(8,128)(2,1)S(1)} %copy-done.24), channel_id=1, source_target_pairs={{0,112},{16,96},{32,16},{48,0},{64,48},{80,32},{96,80},{112,64},{1... | collective-permute-start | bytes 245768 | tf_op jit(solution)/shard_map/ppermute | solution.py:47
  27.9 0.1 collective-permute-start.6
  28.0 2.6 %pack_pairs.1.refs_8_ = bf16[8,17,80,128]{3,2,1,0:T(8,128)(2,1)} custom-call(bf16[4,80,1280]{2,1,0:T(8,128)(2,1)} %queries.2, bf16[4,80,1280]{2,1,0:T(8,128)(2,1)} %keys.1, bf16[4,80,1280]{2,1,0:T(8,128)(2,1)} %values.1), custom_call_target="tpu_custom_call" | custom-call | tf_op jit(solution)/shard_map/pack_pairs/pallas_call | solution.py:373
  30.7 0.0 collective-permute-done.4.refs_5_
  30.7 0.0 collective-permute-done.5.refs_6_
  30.7 0.0 all-to-all-done
  30.8 0.6 copy-done.16
  31.3 0.1 copy-done.17
  31.4 0.0 copy-done.18
  31.4 0.3 copy-done
  31.8 3.6 %pack_cached.1 = (bf16[8,17,80,128]{3,2,1,0:T(8,128)(2,1)}, bf16[2,8,80,128]{3,2,1,0:T(8,128)(2,1)}, bf16[2,8,80,128]{3,2,1,0:T(8,128)(2,1)}, bf16[2,8,80,128]{3...) custom-call(s32[2,32]{1,0:T(2,128)} %bitcast.13, ...), custom_call_target="tpu_custom_call", output_to_operand_aliasing={{0}: (11, {})} | custom-call | tf_op jit(solution)/shard_map/pack_cached/pallas_call | solution.py:387
  35.4 0.0 copy-start.22
  35.4 4.6 %all-to-all-start.1 = ((bf16[8,1360,128]{2,1,0:T(8,128)(2,1)}), bf16[8,1360,128]{2,1,0:T(8,128)(2,1)}, u32[]{:S(2)}, u32[]{:S(2)}) async-start(bf16[8,1360,128]{2,1,0:T(8,128)(2,1)} %bitcast.7), calls=%async_computation.1 | async-start | bytes 5570560 | tf_op jit(solution)/shard_map/all_to_all | solution.py:404
  40.0 3.0 %collective-permute-start.9 = (bf16[2,8,80,128]{3,2,1,0:T(8,128)(2,1)S(1)}, bf16[2,8,80,128]{3,2,1,0:T(8,128)(2,1)S(1)}, u32[]{:S(2)}, u32[]{:S(2)}) collective-permute-start(bf16[2,8,80,128]{3,2,1,0:T(8,128)(2,1)S(1)} %copy-done.22), channel_id=1, source_target_pairs={{0,64},{16,80},{32,96},{48,112},{64,0},{80,16},{96,32},{112,48},{1... | collective-permute-start | bytes 983048 | tf_op jit(solution)/shard_map/ppermute | solution.py:47
  43.0 0.4 collective-permute-start.10
  43.4 0.3 collective-permute-start.11
  43.8 2.9 %collective-permute-start.12 = (bf16[2,8,80,128]{3,2,1,0:T(8,128)(2,1)}, bf16[2,8,80,128]{3,2,1,0:T(8,128)(2,1)S(1)}, u32[]{:S(2)}, u32[]{:S(2)}) collective-permute-start(bf16[2,8,80,128]{3,2,1,0:T(8,128)(2,1)} %get-tuple-element.98), channel_id=1, source_target_pairs={{0,96},{16,112},{32,0},{48,16},{64,32},{80,48},{96,64},{112,80},{1... | collective-permute-start | bytes 983048 | tf_op jit(solution)/shard_map/ppermute | solution.py:47
  46.7 5.6 %collective-permute-done.9.refs_3_ = bf16[2,8,80,128]{3,2,1,0:T(8,128)(2,1)S(1)} collective-permute-done((bf16[2,8,80,128]{3,2,1,0:T(8,128)(2,1)S(1)}, bf16[2,8,80,128]{3,2,1,0:T(8,128)(2,1)S(1)}, u32[]{:S(2)}, u32[]{:S(2)}) %collective-permute-start.9) | collective-permute-done | bytes 327712 | tf_op jit(solution)/shard_map/ppermute | solution.py:47
  52.2 1.1 collective-permute-start.14
  53.3 5.0 %collective-permute-done.10.refs_4_ = bf16[2,8,80,128]{3,2,1,0:T(8,128)(2,1)S(1)} collective-permute-done((bf16[2,8,80,128]{3,2,1,0:T(8,128)(2,1)S(1)}, bf16[2,8,80,128]{3,2,1,0:T(8,128)(2,1)S(1)}, u32[]{:S(2)}, u32[]{:S(2)}) %collective-permute-start.10) | collective-permute-done | bytes 327712 | tf_op jit(solution)/shard_map/ppermute | solution.py:47
  58.4 1.0 collective-permute-start.15
  59.4 0.1 pad_maximum_fusion.refs_0_
  59.5 6.3 %collective-permute-done.11.refs_5_ = bf16[2,8,80,128]{3,2,1,0:T(8,128)(2,1)S(1)} collective-permute-done((bf16[2,8,80,128]{3,2,1,0:T(8,128)(2,1)}, bf16[2,8,80,128]{3,2,1,0:T(8,128)(2,1)S(1)}, u32[]{:S(2)}, u32[]{:S(2)}) %collective-permute-start.11) | collective-permute-done | bytes 327712 | tf_op jit(solution)/shard_map/ppermute | solution.py:47
  65.8 0.4 collective-permute-done.12.refs_6_
  66.2 6.5 %collective-permute-done.13.refs_7_ = bf16[2,8,80,128]{3,2,1,0:T(8,128)(2,1)S(1)} collective-permute-done((bf16[2,8,80,128]{3,2,1,0:T(8,128)(2,1)}, bf16[2,8,80,128]{3,2,1,0:T(8,128)(2,1)S(1)}, u32[]{:S(2)}, u32[]{:S(2)}) %collective-permute-start.13) | collective-permute-done | bytes 327712 | tf_op jit(solution)/shard_map/ppermute | solution.py:47
  72.7 2.5 %collective-permute-start.18 = (bf16[160,2560]{1,0:T(8,128)(2,1)S(1)}, bf16[160,2560]{1,0:T(8,128)(2,1)}, u32[]{:S(2)}, u32[]{:S(2)}) collective-permute-start(bf16[160,2560]{1,0:T(8,128)(2,1)S(1)} %pad_maximum_fusion.refs_0_), channel_id=1, source_target_pairs={{0,96},{16,112},{32,0},{48,16},{64,32},{80,48},{96,64},{112,80},{1... | collective-permute-start | bytes 2457608 | tf_op jit(solution)/shard_map/ppermute | solution.py:47
  75.2 2.1 %collective-permute-start.16 = (bf16[160,2560]{1,0:T(8,128)(2,1)S(1)}, bf16[160,2560]{1,0:T(8,128)(2,1)S(1)}, u32[]{:S(2)}, u32[]{:S(2)}) collective-permute-start(bf16[160,2560]{1,0:T(8,128)(2,1)S(1)} %pad_maximum_fusion.refs_0_), channel_id=1, source_target_pairs={{0,64},{16,80},{32,96},{48,112},{64,0},{80,16},{96,32},{112,48},{1... | collective-permute-start | bytes 2457608 | tf_op jit(solution)/shard_map/ppermute | solution.py:47
  77.4 12.2 %attend.1 = bf16[16,5,80,128]{3,2,1,0:T(8,128)(2,1)} custom-call(s32[2,32]{1,0:T(2,128)} %bitcast.14, s32[16]{0:T(128)} %span_slot.5, s32[16]{0:T(128)} %counts.1, bf16[8,6,80,128]{3,2,1,0:T(8,128)(2,1)} %bitcast.9, bf16[8,17,80,128]{3,2,1,0:T(8,128)(2,1)} %bitcast.4.refs_1_, bf16[2,8,80,128]{3,2,1,0:T(8,128)(2,1)} %get-tuple-element.102.refs_2_, ...), custom_call_target="tpu_custom_call" | custom-call | tf_op jit(solution)/shard_map/attend/pallas_call | solution.py:413
  89.6 6.9 %all-to-all-start.2 = ((bf16[16,400,128]{2,1,0:T(8,128)(2,1)}), bf16[16,400,128]{2,1,0:T(8,128)(2,1)S(1)}, u32[]{:S(2)}, u32[]{:S(2)}) async-start(bf16[16,400,128]{2,1,0:T(8,128)(2,1)} %bitcast.10), calls=%async_computation.2 | async-start | bytes 3276800 | tf_op jit(solution)/shard_map/all_to_all | solution.py:430
  96.5 0.1 collective-permute-start.19
  96.6 14.2 %collective-permute-done.18.refs_3_ = bf16[160,2560]{1,0:T(8,128)(2,1)} collective-permute-done((bf16[160,2560]{1,0:T(8,128)(2,1)S(1)}, bf16[160,2560]{1,0:T(8,128)(2,1)}, u32[]{:S(2)}, u32[]{:S(2)}) %collective-permute-start.18) | collective-permute-done | bytes 819232 | tf_op jit(solution)/shard_map/ppermute | solution.py:47
  110.7 3.5 %collective-permute-done.17.refs_2_ = bf16[160,2560]{1,0:T(8,128)(2,1)} collective-permute-done((bf16[160,2560]{1,0:T(8,128)(2,1)S(1)}, bf16[160,2560]{1,0:T(8,128)(2,1)}, u32[]{:S(2)}, u32[]{:S(2)}) %collective-permute-start.17) | collective-permute-done | bytes 819232 | tf_op jit(solution)/shard_map/ppermute | solution.py:47
  114.2 0.5 collective-permute-start.20
  114.8 3.1 %collective-permute-done.21.refs_6_ = bf16[160,2560]{1,0:T(8,128)(2,1)S(1)} collective-permute-done((bf16[160,2560]{1,0:T(8,128)(2,1)}, bf16[160,2560]{1,0:T(8,128)(2,1)S(1)}, u32[]{:S(2)}, u32[]{:S(2)}) %collective-permute-start.21) | collective-permute-done | bytes 819232 | tf_op jit(solution)/shard_map/ppermute | solution.py:411
  117.9 0.9 copy-done.4
  118.8 2.6 %all-to-all-done.2.came = bf16[16,400,128]{2,1,0:T(8,128)(2,1)S(1)} async-done(((bf16[16,400,128]{2,1,0:T(8,128)(2,1)}), bf16[16,400,128]{2,1,0:T(8,128)(2,1)S(1)}, u32[]{:S(2)}, u32[]{:S(2)}) %all-to-all-start.2) | async-done | bytes 1638432 | tf_op jit(solution)/shard_map/all_to_all | solution.py:430
  121.3 1.2 copy-done.1
  122.5 8.2 %project.1 = bf16[320,2560]{1,0:T(8,128)(2,1)} custom-call(bf16[16,400,128]{2,1,0:T(8,128)(2,1)} %copy-done.1, bf16[1280,5120]{1,0:T(8,128)(2,1)} %own_weight.1, bf16[160,2560]{1,0:T(8,128)(2,1)S(1)} %pad_maximum_fusion.refs_0_, bf16[160,2560]{1,0:T(8,128)(2,1)S(1)} %collective-permute-done.16.refs_1_, bf16[160,2560]{1,0:T(8,128)(2,1)} %collective-permute-done.17.refs_2_, ...), custom_call_target="tpu_custom_call" | custom-call | tf_op jit(solution)/shard_map/project/pallas_call | solution.py:436
  (70 shorter events, 0.1 us)
Async XLA Ops:
  3.3 8.3 %copy-start.20 = (bf16[80,2560]{1,0:T(8,128)(2,1)S(1)}, bf16[80,2560]{1,0:T(8,128)(2,1)}, u32[]{:S(2)}) copy-start(bf16[80,2560]{1,0:T(8,128)(2,1)} %get-tuple-element.89) | copy-start | bytes 1228804
  3.3 9.0 %copy-start.19 = (bf16[80,2560]{1,0:T(8,128)(2,1)S(1)}, bf16[80,2560]{1,0:T(8,128)(2,1)}, u32[]{:S(2)}) copy-start(bf16[80,2560]{1,0:T(8,128)(2,1)} %get-tuple-element.90) | copy-start | bytes 1228804
  3.3 12.3 %copy-start.29 = (bf16[2,80,256]{2,1,0:T(8,128)(2,1)S(1)}, bf16[2,80,256]{2,1,0:T(8,128)(2,1)}, u32[]{:S(2)}) copy-start(bf16[2,80,256]{2,1,0:T(8,128)(2,1)} %get-tuple-element.71) | copy-start | bytes 245764
  3.3 15.4 %copy-start.28 = (bf16[2,80,256]{2,1,0:T(8,128)(2,1)S(1)}, bf16[2,80,256]{2,1,0:T(8,128)(2,1)}, u32[]{:S(2)}) copy-start(bf16[2,80,256]{2,1,0:T(8,128)(2,1)} %get-tuple-element.72) | copy-start | bytes 245764
  3.4 15.4 %copy-start.27 = (bf16[2,80,256]{2,1,0:T(8,128)(2,1)S(1)}, bf16[2,80,256]{2,1,0:T(8,128)(2,1)}, u32[]{:S(2)}) copy-start(bf16[2,80,256]{2,1,0:T(8,128)(2,1)} %get-tuple-element.73) | copy-start | bytes 245764
  3.4 18.3 %copy-start.26 = (bf16[2,80,256]{2,1,0:T(8,128)(2,1)S(1)}, bf16[2,80,256]{2,1,0:T(8,128)(2,1)}, u32[]{:S(2)}) copy-start(bf16[2,80,256]{2,1,0:T(8,128)(2,1)} %get-tuple-element.74) | copy-start | bytes 245764
  3.4 21.5 %copy-start.25 = (bf16[2,80,256]{2,1,0:T(8,128)(2,1)S(1)}, bf16[2,80,256]{2,1,0:T(8,128)(2,1)}, u32[]{:S(2)}) copy-start(bf16[2,80,256]{2,1,0:T(8,128)(2,1)} %get-tuple-element.75) | copy-start | bytes 245764
  3.4 22.4 %copy-start.24 = (bf16[2,80,256]{2,1,0:T(8,128)(2,1)S(1)}, bf16[2,80,256]{2,1,0:T(8,128)(2,1)}, u32[]{:S(2)}) copy-start(bf16[2,80,256]{2,1,0:T(8,128)(2,1)} %get-tuple-element.76) | copy-start | bytes 245764
  3.4 24.5 %copy-start.23 = (bf16[2,80,256]{2,1,0:T(8,128)(2,1)S(1)}, bf16[2,80,256]{2,1,0:T(8,128)(2,1)}, u32[]{:S(2)}) copy-start(bf16[2,80,256]{2,1,0:T(8,128)(2,1)} %get-tuple-element.77) | copy-start | bytes 245764
  3.4 27.3 %all-to-all-start = ((bf16[8,480,128]{2,1,0:T(8,128)(2,1)}), bf16[8,480,128]{2,1,0:T(8,128)(2,1)S(1)}, u32[]{:S(2)}, u32[]{:S(2)}) async-start(bf16[8,480,128]{2,1,0:T(8,128)(2,1)} %bitcast.11), calls=%async_computation | async-start | bytes 1966080 | tf_op jit(solution)/shard_map/all_to_all | solution.py:365
  11.6 23.8 %collective-permute-start.7 = (bf16[80,2560]{1,0:T(8,128)(2,1)S(1)}, bf16[80,2560]{1,0:T(8,128)(2,1)S(1)}, u32[]{:S(2)}, u32[]{:S(2)}) collective-permute-start(bf16[80,2560]{1,0:T(8,128)(2,1)S(1)} %copy-done.20), channel_id=1, source_target_pairs={{0,1},{1,0},{2,3},{3,2},{4,5},{5,4},{6,7},{7,6},{8,9},{9,8},{10,11... | collective-permute-start | bytes 1228808 | tf_op jit(solution)/shard_map/ppermute | solution.py:370
  12.3 23.0 %collective-permute-start.8 = (bf16[80,2560]{1,0:T(8,128)(2,1)S(1)}, bf16[80,2560]{1,0:T(8,128)(2,1)S(1)}, u32[]{:S(2)}, u32[]{:S(2)}) collective-permute-start(bf16[80,2560]{1,0:T(8,128)(2,1)S(1)} %copy-done.19), channel_id=1, source_target_pairs={{0,3},{1,2},{2,1},{3,0},{4,7},{5,6},{6,5},{7,4},{8,11},{9,10},{10,... | collective-permute-start | bytes 1228808 | tf_op jit(solution)/shard_map/ppermute | solution.py:371
  15.7 5.9 %collective-permute-start = (bf16[2,80,256]{2,1,0:T(8,128)(2,1)S(1)}, bf16[2,80,256]{2,1,0:T(8,128)(2,1)S(1)}, u32[]{:S(2)}, u32[]{:S(2)}) collective-permute-start(bf16[2,80,256]{2,1,0:T(8,128)(2,1)S(1)} %copy-done.29), channel_id=1, source_target_pairs={{0,64},{16,80},{32,96},{48,112},{64,0},{80,16},{96,32},{112,48},{1... | collective-permute-start | bytes 245768 | tf_op jit(solution)/shard_map/ppermute | solution.py:47
  18.7 6.2 %collective-permute-start.1 = (bf16[2,80,256]{2,1,0:T(8,128)(2,1)S(1)}, bf16[2,80,256]{2,1,0:T(8,128)(2,1)S(1)}, u32[]{:S(2)}, u32[]{:S(2)}) collective-permute-start(bf16[2,80,256]{2,1,0:T(8,128)(2,1)S(1)} %copy-done.28), channel_id=1, source_target_pairs={{0,80},{16,64},{32,112},{48,96},{64,16},{80,0},{96,48},{112,32},{1... | collective-permute-start | bytes 245768 | tf_op jit(solution)/shard_map/ppermute | solution.py:47
  18.7 7.1 %collective-permute-start.2 = (bf16[2,80,256]{2,1,0:T(8,128)(2,1)S(1)}, bf16[2,80,256]{2,1,0:T(8,128)(2,1)S(1)}, u32[]{:S(2)}, u32[]{:S(2)}) collective-permute-start(bf16[2,80,256]{2,1,0:T(8,128)(2,1)S(1)} %copy-done.27), channel_id=1, source_target_pairs={{0,32},{16,48},{32,64},{48,80},{64,96},{80,112},{96,0},{112,16},{1... | collective-permute-start | bytes 245768 | tf_op jit(solution)/shard_map/ppermute | solution.py:47
  21.6 9.0 %copy-start.12 = (bf16[2,80,256]{2,1,0:T(8,128)(2,1)}, bf16[2,80,256]{2,1,0:T(8,128)(2,1)S(1)}, u32[]{:S(2)}) copy-start(bf16[2,80,256]{2,1,0:T(8,128)(2,1)S(1)} %collective-permute-done.refs_1_) | copy-start | bytes 245764
  21.6 6.3 %collective-permute-start.3 = (bf16[2,80,256]{2,1,0:T(8,128)(2,1)S(1)}, bf16[2,80,256]{2,1,0:T(8,128)(2,1)S(1)}, u32[]{:S(2)}, u32[]{:S(2)}) collective-permute-start(bf16[2,80,256]{2,1,0:T(8,128)(2,1)S(1)} %copy-done.26), channel_id=1, source_target_pairs={{0,96},{16,112},{32,0},{48,16},{64,32},{80,48},{96,64},{112,80},{1... | collective-permute-start | bytes 245768 | tf_op jit(solution)/shard_map/ppermute | solution.py:47
  24.9 5.8 %copy-start.13 = (bf16[2,80,256]{2,1,0:T(8,128)(2,1)}, bf16[2,80,256]{2,1,0:T(8,128)(2,1)S(1)}, u32[]{:S(2)}) copy-start(bf16[2,80,256]{2,1,0:T(8,128)(2,1)S(1)} %collective-permute-done.1.refs_2_) | copy-start | bytes 245764
  24.9 5.8 %collective-permute-start.4 = (bf16[2,80,256]{2,1,0:T(8,128)(2,1)S(1)}, bf16[2,80,256]{2,1,0:T(8,128)(2,1)S(1)}, u32[]{:S(2)}, u32[]{:S(2)}) collective-permute-start(bf16[2,80,256]{2,1,0:T(8,128)(2,1)S(1)} %copy-done.25), channel_id=1, source_target_pairs={{0,48},{16,32},{32,80},{48,64},{64,112},{80,96},{96,16},{112,0},{1... | collective-permute-start | bytes 245768 | tf_op jit(solution)/shard_map/ppermute | solution.py:47
  25.8 4.9 %copy-start.14 = (bf16[2,80,256]{2,1,0:T(8,128)(2,1)}, bf16[2,80,256]{2,1,0:T(8,128)(2,1)S(1)}, u32[]{:S(2)}) copy-start(bf16[2,80,256]{2,1,0:T(8,128)(2,1)S(1)} %collective-permute-done.2.refs_3_) | copy-start | bytes 245764
  25.8 4.9 %collective-permute-start.5 = (bf16[2,80,256]{2,1,0:T(8,128)(2,1)S(1)}, bf16[2,80,256]{2,1,0:T(8,128)(2,1)S(1)}, u32[]{:S(2)}, u32[]{:S(2)}) collective-permute-start(bf16[2,80,256]{2,1,0:T(8,128)(2,1)S(1)} %copy-done.24), channel_id=1, source_target_pairs={{0,112},{16,96},{32,16},{48,0},{64,48},{80,32},{96,80},{112,64},{1... | collective-permute-start | bytes 245768 | tf_op jit(solution)/shard_map/ppermute | solution.py:47
  27.9 2.8 %copy-start.15 = (bf16[2,80,256]{2,1,0:T(8,128)(2,1)}, bf16[2,80,256]{2,1,0:T(8,128)(2,1)S(1)}, u32[]{:S(2)}) copy-start(bf16[2,80,256]{2,1,0:T(8,128)(2,1)S(1)} %collective-permute-done.3.refs_4_) | copy-start | bytes 245764
  27.9 2.8 %collective-permute-start.6 = (bf16[2,80,256]{2,1,0:T(8,128)(2,1)S(1)}, bf16[2,80,256]{2,1,0:T(8,128)(2,1)S(1)}, u32[]{:S(2)}, u32[]{:S(2)}) collective-permute-start(bf16[2,80,256]{2,1,0:T(8,128)(2,1)S(1)} %copy-done.23), channel_id=1, source_target_pairs={{0,16},{16,0},{32,48},{48,32},{64,80},{80,64},{96,112},{112,96},{1... | collective-permute-start | bytes 245768 | tf_op jit(solution)/shard_map/ppermute | solution.py:47
  35.4 4.6 %copy-start.22 = (bf16[2,8,80,128]{3,2,1,0:T(8,128)(2,1)S(1)}, bf16[2,8,80,128]{3,2,1,0:T(8,128)(2,1)}, u32[]{:S(2)}) copy-start(bf16[2,8,80,128]{3,2,1,0:T(8,128)(2,1)} %get-tuple-element.95) | copy-start | bytes 983044
  35.4 7.6 %copy-start.21 = (bf16[2,8,80,128]{3,2,1,0:T(8,128)(2,1)S(1)}, bf16[2,8,80,128]{3,2,1,0:T(8,128)(2,1)}, u32[]{:S(2)}) copy-start(bf16[2,8,80,128]{3,2,1,0:T(8,128)(2,1)} %get-tuple-element.96) | copy-start | bytes 983044
  35.4 41.9 %all-to-all-start.1 = ((bf16[8,1360,128]{2,1,0:T(8,128)(2,1)}), bf16[8,1360,128]{2,1,0:T(8,128)(2,1)}, u32[]{:S(2)}, u32[]{:S(2)}) async-start(bf16[8,1360,128]{2,1,0:T(8,128)(2,1)} %bitcast.7), calls=%async_computation.1 | async-start | bytes 5570560 | tf_op jit(solution)/shard_map/all_to_all | solution.py:404
  40.0 12.2 %collective-permute-start.9 = (bf16[2,8,80,128]{3,2,1,0:T(8,128)(2,1)S(1)}, bf16[2,8,80,128]{3,2,1,0:T(8,128)(2,1)S(1)}, u32[]{:S(2)}, u32[]{:S(2)}) collective-permute-start(bf16[2,8,80,128]{3,2,1,0:T(8,128)(2,1)S(1)} %copy-done.22), channel_id=1, source_target_pairs={{0,64},{16,80},{32,96},{48,112},{64,0},{80,16},{96,32},{112,48},{1... | collective-permute-start | bytes 983048 | tf_op jit(solution)/shard_map/ppermute | solution.py:47
  43.0 15.4 %collective-permute-start.10 = (bf16[2,8,80,128]{3,2,1,0:T(8,128)(2,1)S(1)}, bf16[2,8,80,128]{3,2,1,0:T(8,128)(2,1)S(1)}, u32[]{:S(2)}, u32[]{:S(2)}) collective-permute-start(bf16[2,8,80,128]{3,2,1,0:T(8,128)(2,1)S(1)} %copy-done.21), channel_id=1, source_target_pairs={{0,80},{16,64},{32,112},{48,96},{64,16},{80,0},{96,48},{112,32},{1... | collective-permute-start | bytes 983048 | tf_op jit(solution)/shard_map/ppermute | solution.py:47
  43.4 22.4 %collective-permute-start.11 = (bf16[2,8,80,128]{3,2,1,0:T(8,128)(2,1)}, bf16[2,8,80,128]{3,2,1,0:T(8,128)(2,1)S(1)}, u32[]{:S(2)}, u32[]{:S(2)}) collective-permute-start(bf16[2,8,80,128]{3,2,1,0:T(8,128)(2,1)} %get-tuple-element.97), channel_id=1, source_target_pairs={{0,32},{16,48},{32,64},{48,80},{64,96},{80,112},{96,0},{112,16},{1... | collective-permute-start | bytes 983048 | tf_op jit(solution)/shard_map/ppermute | solution.py:47
  43.8 22.4 %collective-permute-start.12 = (bf16[2,8,80,128]{3,2,1,0:T(8,128)(2,1)}, bf16[2,8,80,128]{3,2,1,0:T(8,128)(2,1)S(1)}, u32[]{:S(2)}, u32[]{:S(2)}) collective-permute-start(bf16[2,8,80,128]{3,2,1,0:T(8,128)(2,1)} %get-tuple-element.98), channel_id=1, source_target_pairs={{0,96},{16,112},{32,0},{48,16},{64,32},{80,48},{96,64},{112,80},{1... | collective-permute-start | bytes 983048 | tf_op jit(solution)/shard_map/ppermute | solution.py:47
  46.7 26.0 %collective-permute-start.13 = (bf16[2,8,80,128]{3,2,1,0:T(8,128)(2,1)}, bf16[2,8,80,128]{3,2,1,0:T(8,128)(2,1)S(1)}, u32[]{:S(2)}, u32[]{:S(2)}) collective-permute-start(bf16[2,8,80,128]{3,2,1,0:T(8,128)(2,1)} %get-tuple-element.99), channel_id=1, source_target_pairs={{0,48},{16,32},{32,80},{48,64},{64,112},{80,96},{96,16},{112,0},{1... | collective-permute-start | bytes 983048 | tf_op jit(solution)/shard_map/ppermute | solution.py:47
  52.2 25.1 %copy-start.5 = (bf16[2,8,80,128]{3,2,1,0:T(8,128)(2,1)}, bf16[2,8,80,128]{3,2,1,0:T(8,128)(2,1)S(1)}, u32[]{:S(2)}) copy-start(bf16[2,8,80,128]{3,2,1,0:T(8,128)(2,1)S(1)} %collective-permute-done.9.refs_3_) | copy-start | bytes 983044
  52.2 20.5 %collective-permute-start.14 = (bf16[2,8,80,128]{3,2,1,0:T(8,128)(2,1)}, bf16[2,8,80,128]{3,2,1,0:T(8,128)(2,1)S(1)}, u32[]{:S(2)}, u32[]{:S(2)}) collective-permute-start(bf16[2,8,80,128]{3,2,1,0:T(8,128)(2,1)} %get-tuple-element.100), channel_id=1, source_target_pairs={{0,112},{16,96},{32,16},{48,0},{64,48},{80,32},{96,80},{112,64},{1... | collective-permute-start | bytes 983048 | tf_op jit(solution)/shard_map/ppermute | solution.py:47
  58.4 19.0 %copy-start.6 = (bf16[2,8,80,128]{3,2,1,0:T(8,128)(2,1)}, bf16[2,8,80,128]{3,2,1,0:T(8,128)(2,1)S(1)}, u32[]{:S(2)}) copy-start(bf16[2,8,80,128]{3,2,1,0:T(8,128)(2,1)S(1)} %collective-permute-done.10.refs_4_) | copy-start | bytes 983044
  58.4 14.3 %collective-permute-start.15 = (bf16[2,8,80,128]{3,2,1,0:T(8,128)(2,1)}, bf16[2,8,80,128]{3,2,1,0:T(8,128)(2,1)S(1)}, u32[]{:S(2)}, u32[]{:S(2)}) collective-permute-start(bf16[2,8,80,128]{3,2,1,0:T(8,128)(2,1)} %get-tuple-element.101), channel_id=1, source_target_pairs={{0,16},{16,0},{32,48},{48,32},{64,80},{80,64},{96,112},{112,96},{1... | collective-permute-start | bytes 983048 | tf_op jit(solution)/shard_map/ppermute | solution.py:47
  65.8 11.5 %copy-start.7 = (bf16[2,8,80,128]{3,2,1,0:T(8,128)(2,1)}, bf16[2,8,80,128]{3,2,1,0:T(8,128)(2,1)S(1)}, u32[]{:S(2)}) copy-start(bf16[2,8,80,128]{3,2,1,0:T(8,128)(2,1)S(1)} %collective-permute-done.11.refs_5_) | copy-start | bytes 983044
  66.2 11.1 %copy-start.8 = (bf16[2,8,80,128]{3,2,1,0:T(8,128)(2,1)}, bf16[2,8,80,128]{3,2,1,0:T(8,128)(2,1)S(1)}, u32[]{:S(2)}) copy-start(bf16[2,8,80,128]{3,2,1,0:T(8,128)(2,1)S(1)} %collective-permute-done.12.refs_6_) | copy-start | bytes 983044
  72.7 4.7 %copy-start.9 = (bf16[2,8,80,128]{3,2,1,0:T(8,128)(2,1)}, bf16[2,8,80,128]{3,2,1,0:T(8,128)(2,1)S(1)}, u32[]{:S(2)}) copy-start(bf16[2,8,80,128]{3,2,1,0:T(8,128)(2,1)S(1)} %collective-permute-done.13.refs_7_) | copy-start | bytes 983044
  72.7 38.0 %collective-permute-start.18 = (bf16[160,2560]{1,0:T(8,128)(2,1)S(1)}, bf16[160,2560]{1,0:T(8,128)(2,1)}, u32[]{:S(2)}, u32[]{:S(2)}) collective-permute-start(bf16[160,2560]{1,0:T(8,128)(2,1)S(1)} %pad_maximum_fusion.refs_0_), channel_id=1, source_target_pairs={{0,96},{16,112},{32,0},{48,16},{64,32},{80,48},{96,64},{112,80},{1... | collective-permute-start | bytes 2457608 | tf_op jit(solution)/shard_map/ppermute | solution.py:47
  75.2 39.0 %collective-permute-start.17 = (bf16[160,2560]{1,0:T(8,128)(2,1)S(1)}, bf16[160,2560]{1,0:T(8,128)(2,1)}, u32[]{:S(2)}, u32[]{:S(2)}) collective-permute-start(bf16[160,2560]{1,0:T(8,128)(2,1)S(1)} %pad_maximum_fusion.refs_0_), channel_id=1, source_target_pairs={{0,32},{16,48},{32,64},{48,80},{64,96},{80,112},{96,0},{112,16},{1... | collective-permute-start | bytes 2457608 | tf_op jit(solution)/shard_map/ppermute | solution.py:47
  75.2 39.0 %collective-permute-start.16 = (bf16[160,2560]{1,0:T(8,128)(2,1)S(1)}, bf16[160,2560]{1,0:T(8,128)(2,1)S(1)}, u32[]{:S(2)}, u32[]{:S(2)}) collective-permute-start(bf16[160,2560]{1,0:T(8,128)(2,1)S(1)} %pad_maximum_fusion.refs_0_), channel_id=1, source_target_pairs={{0,64},{16,80},{32,96},{48,112},{64,0},{80,16},{96,32},{112,48},{1... | collective-permute-start | bytes 2457608 | tf_op jit(solution)/shard_map/ppermute | solution.py:47
  89.6 31.8 %all-to-all-start.2 = ((bf16[16,400,128]{2,1,0:T(8,128)(2,1)}), bf16[16,400,128]{2,1,0:T(8,128)(2,1)S(1)}, u32[]{:S(2)}, u32[]{:S(2)}) async-start(bf16[16,400,128]{2,1,0:T(8,128)(2,1)} %bitcast.10), calls=%async_computation.2 | async-start | bytes 3276800 | tf_op jit(solution)/shard_map/all_to_all | solution.py:430
  96.5 18.3 %collective-permute-start.19 = (bf16[160,2560]{1,0:T(8,128)(2,1)S(1)}, bf16[160,2560]{1,0:T(8,128)(2,1)S(1)}, u32[]{:S(2)}, u32[]{:S(2)}) collective-permute-start(bf16[160,2560]{1,0:T(8,128)(2,1)S(1)} %pad_maximum_fusion.refs_0_), channel_id=1, source_target_pairs={{0,16},{16,0},{32,48},{48,32},{64,80},{80,64},{96,112},{112,96},{1... | collective-permute-start | bytes 2457608 | tf_op jit(solution)/shard_map/ppermute | solution.py:411
  110.7 4.0 %collective-permute-start.22 = (bf16[160,2560]{1,0:T(8,128)(2,1)}, bf16[160,2560]{1,0:T(8,128)(2,1)S(1)}, u32[]{:S(2)}, u32[]{:S(2)}) collective-permute-start(bf16[160,2560]{1,0:T(8,128)(2,1)} %collective-permute-done.18.refs_3_), channel_id=1, source_target_pairs={{0,16},{16,0},{32,48},{48,32},{64,80},{80,64},{96,112},{112,96},{1... | collective-permute-start | bytes 2457608 | tf_op jit(solution)/shard_map/ppermute | solution.py:411
  114.2 3.6 %collective-permute-start.21 = (bf16[160,2560]{1,0:T(8,128)(2,1)}, bf16[160,2560]{1,0:T(8,128)(2,1)S(1)}, u32[]{:S(2)}, u32[]{:S(2)}) collective-permute-start(bf16[160,2560]{1,0:T(8,128)(2,1)} %collective-permute-done.17.refs_2_), channel_id=1, source_target_pairs={{0,16},{16,0},{32,48},{48,32},{64,80},{80,64},{96,112},{112,96},{1... | collective-permute-start | bytes 2457608 | tf_op jit(solution)/shard_map/ppermute | solution.py:411
  114.2 4.5 %collective-permute-start.20 = (bf16[160,2560]{1,0:T(8,128)(2,1)S(1)}, bf16[160,2560]{1,0:T(8,128)(2,1)}, u32[]{:S(2)}, u32[]{:S(2)}) collective-permute-start(bf16[160,2560]{1,0:T(8,128)(2,1)S(1)} %collective-permute-done.16.refs_1_), channel_id=1, source_target_pairs={{0,16},{16,0},{32,48},{48,32},{64,80},{80,64},{96,112},{112,96},{1... | collective-permute-start | bytes 2457608 | tf_op jit(solution)/shard_map/ppermute | solution.py:411
  114.7 3.1 %copy-start.2 = (bf16[160,2560]{1,0:T(8,128)(2,1)}, bf16[160,2560]{1,0:T(8,128)(2,1)S(1)}, u32[]{:S(2)}) copy-start(bf16[160,2560]{1,0:T(8,128)(2,1)S(1)} %collective-permute-done.19.refs_4_) | copy-start | bytes 2457604
  114.8 3.1 %copy-start.3 = (bf16[160,2560]{1,0:T(8,128)(2,1)}, bf16[160,2560]{1,0:T(8,128)(2,1)S(1)}, u32[]{:S(2)}) copy-start(bf16[160,2560]{1,0:T(8,128)(2,1)S(1)} %collective-permute-done.22.refs_7_) | copy-start | bytes 2457604
  (8 other events, 10.0 us)
